TPU v7x, 32 devices: a whole 2x2x4 slice. The times are simulated.
32 devices in a mesh: groups: 2 (over y), seq: 4 (over z), weight: 4 (over x, core).
Axes of the slice: x: 2, y: 2, z: 4, core: 2. Of those that a mesh axis runs over, the one named last changes fastest.
Arguments:
- tokens: bfloat16 [8, 512, 1536], P(('groups', 'weight'), 'seq'), parts along dimension 0, may hold values from -20 to 20
- upstream_grad: bfloat16 [8, 512, 1536], P(('groups', 'weight'), 'seq'), parts along dimension 0, may hold values from -6 to 6
- norm_gain: float32 [1536], replicated, may hold values from 0.5 to 1.5
- norm_bias: float32 [1536], replicated, may hold values from -3 to 3
- input_codes: bfloat16 [1536, 2304], P('weight'), may hold values from -10 to 10
- input_scales: float32 [12, 18], P('weight'), may hold values from 0.02 to 0.06
- input_bias: float32 [2304], replicated, may hold values from -3 to 3
- output_codes: bfloat16 [768, 1536], replicated, may hold values from -4 to 4
- output_scales: float32 [6, 12], replicated, may hold values from 0.02 to 0.06
- layer_scale: float32 [1536], replicated, may hold values from 0.3 to 3
Outputs:
- input_grad: float32 [8, 512, 1536], P(('groups', 'weight'), 'seq'), parts along dimension 0
There are 2 independent parts, one for each index of `groups`. A program takes and returns all parts, laid end to end along the dimension named above; an argument that names none is the same for every part. Nothing has to cross between parts.
All inputs are finite; a program needn't handle non-finite values.
Results may differ from a plain program's by a relative error of at most 0.024.
Values may be sent and summed in bfloat16 or wider, within the bound.
No kernel may reach another device: no remote copies, remote signals or barrier semaphores. Data moves between devices by JAX's collectives and lax.ppermute only.
A program may use at most 128 MiB of HBM per device.

v0:
```python
import math

import jax
import jax.numpy as jnp
from jax import lax
from jax.sharding import PartitionSpec as P

HEADS = 12
HEAD_DIM = 64
QBLOCK = 128
HD = 768


def dequantize(codes, scales):
    expanded = jnp.repeat(jnp.repeat(scales, QBLOCK, axis=0), QBLOCK, axis=1)
    return (codes.astype(jnp.float32) * expanded).astype(jnp.bfloat16)


def normalize(rows, gain, shift):
    mean_value = jnp.mean(rows, axis=-1, keepdims=True)
    centered = rows - mean_value
    variance = jnp.mean(centered * centered, axis=-1, keepdims=True)
    inverse = lax.rsqrt(variance + 1e-06)
    normed = centered * inverse
    return (normed, inverse, (normed * gain + shift).astype(jnp.bfloat16))


def norm_backward(grad_norm, normed, inverse, gain):
    grad_hat = grad_norm * gain
    first_mean = jnp.mean(grad_hat, axis=-1, keepdims=True)
    second_mean = jnp.mean(grad_hat * normed, axis=-1, keepdims=True)
    return inverse * (grad_hat - first_mean - normed * second_mean)


def score_block(queries, head_grads, pair_block):
    row_count = pair_block.shape[0]
    keys_blk = pair_block[:, :HD].reshape(row_count, HEADS, HEAD_DIM)
    values_blk = pair_block[:, HD:].reshape(row_count, HEADS, HEAD_DIM)
    scores = jnp.einsum(
        "qhd,khd->hqk", queries, keys_blk, preferred_element_type=jnp.float32
    ) * HEAD_DIM ** (-0.5)
    dprob = jnp.einsum("qhd,khd->hqk", head_grads, values_blk, preferred_element_type=jnp.float32)
    return (keys_blk, scores, dprob)


def update_stats(statistics, queries, head_grads, pair_rows):
    sub_size = math.gcd(pair_rows.shape[0], 512)

    def visit_block(block_index, running):
        run_max, run_total, run_mix = running
        pair_block = lax.dynamic_slice_in_dim(pair_rows, block_index * sub_size, sub_size, 0)
        keys_blk, scores, dprob = score_block(queries, head_grads, pair_block)
        new_max = jnp.maximum(run_max, jnp.max(scores, axis=-1))
        factor = jnp.exp(run_max - new_max)
        expo = jnp.exp(scores - new_max[..., None])
        return (
            new_max,
            run_total * factor + jnp.sum(expo, axis=-1),
            run_mix * factor + jnp.sum(expo * dprob, axis=-1),
        )

    return lax.fori_loop(0, pair_rows.shape[0] // sub_size, visit_block, statistics)


def block_backward(queries, head_grads, pair_block, log_total, row_delta):
    keys_blk, scores, dprob = score_block(queries, head_grads, pair_block)
    weights = jnp.exp(scores - log_total[..., None])
    prob_weights = weights.astype(jnp.bfloat16)
    dscore = (weights * (dprob - row_delta[..., None])).astype(jnp.bfloat16)
    return (keys_blk, prob_weights, dscore)


def key_terms_from(queries, head_grads, prob_weights, dscore):
    key_part = jnp.einsum(
        "hqk,qhd->khd", dscore, queries, preferred_element_type=jnp.float32
    ) * HEAD_DIM ** (-0.5)
    value_part = jnp.einsum(
        "hqk,qhd->khd", prob_weights, head_grads, preferred_element_type=jnp.float32
    )
    row_count = key_part.shape[0]
    return jnp.concatenate(
        [key_part.reshape(row_count, HD), value_part.reshape(row_count, HD)], axis=1
    )


def query_side(queries, head_grads, keys_values, local_rows):
    seq_rows = local_rows * lax.axis_size("seq")
    start_stats = (
        jnp.full((HEADS, local_rows), -1e30, jnp.float32),
        jnp.zeros((HEADS, local_rows), jnp.float32),
        jnp.zeros((HEADS, local_rows), jnp.float32),
    )
    all_pairs = lax.all_gather(keys_values, "seq", axis=0, tiled=True)
    statistics = update_stats(start_stats, queries, head_grads, all_pairs)
    row_max, row_total, row_mix = statistics
    log_total = row_max + jnp.log(row_total)
    row_delta = row_mix / row_total
    sub_size = math.gcd(seq_rows, 512)
    block_count = seq_rows // sub_size
    empty_query = jnp.zeros((local_rows, HEADS, HEAD_DIM), jnp.float32)

    def backward_step(block_index, running):
        query_grad, buffer = running
        pair_block = lax.dynamic_slice_in_dim(all_pairs, block_index * sub_size, sub_size, 0)
        keys_blk, prob_weights, dscore = block_backward(
            queries, head_grads, pair_block, log_total, row_delta
        )
        query_grad = query_grad + jnp.einsum(
            "hqk,khd->qhd", dscore, keys_blk, preferred_element_type=jnp.float32
        )
        block_terms = key_terms_from(queries, head_grads, prob_weights, dscore)
        buffer = lax.dynamic_update_slice_in_dim(buffer, block_terms, block_index * sub_size, 0)
        return (query_grad, buffer)

    empty_terms = jnp.zeros((seq_rows, 2 * HD), jnp.float32)
    query_grad, buffer = lax.fori_loop(0, block_count, backward_step, (empty_query, empty_terms))
    pair_grads = lax.psum_scatter(
        buffer.astype(jnp.bfloat16), "seq", scatter_dimension=0, tiled=True
    ).astype(jnp.float32)
    return (query_grad, pair_grads)


def local(
    tokens,
    upstream_grad,
    norm_gain,
    norm_bias,
    input_codes,
    input_scales,
    input_bias,
    output_codes,
    output_scales,
    layer_scale,
):
    all_codes, all_scales = (
        lax.all_gather(input_codes.astype(jnp.float32), "weight", axis=0, tiled=True).astype(
            input_codes.dtype
        ),
        lax.all_gather(input_scales, "weight", axis=0, tiled=True),
    )
    input_weight = dequantize(all_codes, all_scales)
    output_weight = dequantize(output_codes, output_scales)
    normed, inverse, norm_out = normalize(tokens[0].astype(jnp.float32), norm_gain, norm_bias)
    projected = (
        jnp.dot(norm_out, input_weight, preferred_element_type=jnp.float32) + input_bias
    ).astype(jnp.bfloat16)
    local_rows = projected.shape[0]
    queries = projected[:, :HD].reshape(local_rows, HEADS, HEAD_DIM)
    keys_values = projected[:, HD:]
    scaled_grad = (upstream_grad[0].astype(jnp.float32) * layer_scale).astype(jnp.bfloat16)
    head_grads = jnp.dot(scaled_grad, output_weight.T, preferred_element_type=jnp.float32).astype(
        jnp.bfloat16
    )
    head_grads = head_grads.reshape(local_rows, HEADS, HEAD_DIM)
    query_grad, pair_grads = query_side(queries, head_grads, keys_values, local_rows)
    query_grad = (query_grad * HEAD_DIM ** (-0.5)).reshape(local_rows, HD)
    grad_proj = jnp.concatenate([query_grad, pair_grads], axis=1).astype(jnp.bfloat16)
    grad_norm = jnp.dot(grad_proj, input_weight.T, preferred_element_type=jnp.float32)
    result = norm_backward(grad_norm, normed, inverse, norm_gain)
    return result[None]


def solution(mesh):
    in_specs = (
        P(("groups", "weight"), "seq", None),
        P(("groups", "weight"), "seq", None),
        P(),
        P(),
        P("weight", None),
        P("weight", None),
        P(),
        P(),
        P(),
        P(),
    )
    out_specs = P(("groups", "weight"), "seq", None)
    return jax.shard_map(local, mesh=mesh, in_specs=in_specs, out_specs=out_specs, check_vma=False)
```

profile of v0, /device:TPU:0, one launch (start us, length us, event | category | flops | bytes accessed | tf_op | source)
XLA Modules:
  0.0 167.3 jit_solution(9870443607912164000)
XLA Ops:
  6.5 4.0 %copy.26 = bf16[384,2304]{0,1:T(8,128)(2,1)} copy(bf16[384,2304]{1,0:T(8,128)(2,1)} %param.14) | data formatting | bytes 3538944 | tf_op args[4]
  10.6 6.1 %all-gather = f32[4,3,18]{2,1,0:T(4,128)S(1)} all-gather(f32[1,3,18]{2,1,0:T(4,128)S(1)} %bitcast.98), channel_id=1, replica_groups=mesh['groups'=2,'seq'=4,'weight'=4] {'weight'}, dimensions={0}, use_global_device_ids=true | all-gather | bytes 1080 | tf_op jit(solution)/shard_map/all_gather | solution.py:139
  16.7 0.1 copy.27
  17.0 0.1 convert_reduce_fusion
  17.2 0.3 fusion.25
  17.4 46.7 %all-gather.4.cloned.1.call-done = bf16[1536,2304]{0,1:T(8,128)(2,1)} async-done(((bf16[384,2304]{0,1:T(8,128)(2,1)}), bf16[1536,2304]{0,1:T(8,128)(2,1)}) %all-gather.4.cloned.1.call-update) | async-done | bytes 7077904 | tf_op jit(solution)/shard_map/all_gather | solution.py:136
  64.2 4.4 %fusion = bf16[1536,2304]{0,1:T(8,128)(2,1)S(1)} fusion(f32[1536,18]{0,1:T(8,128)S(1)} %bitcast.95, bf16[1536,2304]{0,1:T(8,128)(2,1)} %all-gather.4.cloned.1.call-done), kind=kLoop, calls=%fused_computation.1 | loop fusion | flops 10616832 | bytes 14266368 | tf_op jit(solution)/shard_map/convert_element_type | solution.py:16
  68.7 2.5 %fusion.2 = bf16[128,2304]{1,0:T(8,128)(2,1)S(1)} fusion(bf16[1536,2304]{0,1:T(8,128)(2,1)S(1)} %fusion, f32[2304]{0:T(1024)S(1)} %copy-done.4, bf16[1,128,1536]{2,1,0:T(8,128)(2,1)S(1)} %copy-done.1, f32[1536]{0:T(1024)S(1)} %copy-done.5, f32[1536]{0:T(1024)S(1)} %copy-done.3, f32[128]{0:T(128)S(1)} %add_rsqrt_fusion, f32[128]{0:T(128)S(1)} %broadcast_multiply_fusion.2), kind=kOutput, calls=%fused_computation.5 | convolution fusion | flops 907739136 | bytes 8083456 | tf_op jit(solution)/shard_map/dot_general | solution.py:145
  71.1 0.4 copy-done
  71.5 0.8 slice.22
  72.6 2.8 %copy.30 = bf16[768,1536]{0,1:T(8,128)(2,1)S(1)} copy(bf16[768,1536]{1,0:T(8,128)(2,1)} %param.17) | data formatting | bytes 4718592 | tf_op args[7]
  75.5 0.5 fusion.1
  75.9 0.5 copy-done.2
  76.5 0.5 convolution_convert_fusion
  77.0 0.2 copy.32
  77.1 0.2 copy.29
  77.3 32.3 %all-gather.6.cloned.1.call-done = bf16[512,1536]{1,0:T(8,128)(2,1)} async-done(((bf16[128,1536]{1,0:T(8,128)(2,1)}), bf16[512,1536]{1,0:T(8,128)(2,1)}) %all-gather.6.cloned.1.call-update) | async-done | bytes 1572880 | tf_op jit(solution)/shard_map/all_gather | solution.py:93
  109.6 1.5 fusion.42
  111.1 0.3 copy.33
  111.4 0.3 copy.28
  111.6 0.7 multiply_reduce_fusion.1
  112.3 1.3 multiply_reduce_fusion
  113.7 0.8 fusion.9
  114.5 0.9 multiply_convert_fusion
  115.4 0.4 multiply_convert_fusion.1
  115.8 1.3 pad_maximum_fusion
  117.1 2.7 %copy.34 = bf16[512,1536]{1,0:T(8,128)(2,1)} copy(bf16[512,1536]{0,1:T(8,128)(2,1)} %pad_maximum_fusion) | data formatting | bytes 3145728
  119.8 0.7 fusion.12
  120.4 33.6 %reduce-scatter.4.cloned.1.call-done = bf16[128,1536]{1,0:T(8,128)(2,1)} async-done(((bf16[512,1536]{1,0:T(8,128)(2,1)}), bf16[128,1536]{1,0:T(8,128)(2,1)}) %reduce-scatter.4.cloned.1.call-update) | async-done | bytes 393232
  154.1 1.2 copy.35
  155.3 4.3 %fusion.41 = (f32[128]{0:T(128)S(1)}, f32[128]{0:T(128)S(1)}, f32[128,1536]{1,0:T(8,128)S(1)}) fusion(f32[128]{0:T(128)S(1)} %add_rsqrt_fusion, f32[128]{0:T(128)S(1)} %broadcast_multiply_fusion.2, bf16[1,128,1536]{2,1,0:T(8,128)(2,1)S(1)} %copy-done.1, f32[1536]{0:T(1024)S(1)} %copy-done.3, bf16[1536,2304]{0,1:T(8,128)(2,1)} %copy-done, ...), kind=kOutput, calls=%fused_computation.62 | convolution fusion | flops 908525312 | bytes 8855552 | tf_op jit(solution)/shard_map/dot_general | solution.py:158
  159.6 1.2 fusion.24
  (36 shorter events, 0.6 us)
Async XLA Ops:
  6.5 4.1 %copy-start.8 = (f32[3,18]{1,0:T(4,128)S(1)}, f32[3,18]{1,0:T(4,128)}, u32[]{:S(2)}) copy-start(f32[3,18]{1,0:T(4,128)} %param.15) | copy-start | bytes 652
  6.5 10.5 %copy-start.1 = (bf16[1,128,1536]{2,1,0:T(8,128)(2,1)S(1)}, bf16[1,128,1536]{2,1,0:T(8,128)(2,1)}, u32[]{:S(2)}) copy-start(bf16[1,128,1536]{2,1,0:T(8,128)(2,1)} %param.10) | copy-start | bytes 1179652
  6.5 57.6 %all-gather.4.cloned.1.call-start = ((), (), s32[]{:S(2)}) async-start(), calls=%async_computation.1 | async-start | bytes 8847360 | tf_op jit(solution)/shard_map/all_gather | solution.py:136
  10.5 99.0 %all-gather.6.cloned.1.call-start = ((), (), s32[]{:S(2)}) async-start(), calls=%async_computation.2 | async-start | bytes 1966080 | tf_op jit(solution)/shard_map/all_gather | solution.py:93
  64.1 4.5 %copy-start.3 = (f32[1536]{0:T(1024)S(1)}, f32[1536]{0:T(1024)}, u32[]{:S(2)}) copy-start(f32[1536]{0:T(1024)} %param.12) | copy-start | bytes 18436
  64.2 4.5 %copy-start.4 = (f32[2304]{0:T(1024)S(1)}, f32[2304]{0:T(1024)}, u32[]{:S(2)}) copy-start(f32[2304]{0:T(1024)} %param.16) | copy-start | bytes 27652
  64.2 4.5 %copy-start.5 = (f32[1536]{0:T(1024)S(1)}, f32[1536]{0:T(1024)}, u32[]{:S(2)}) copy-start(f32[1536]{0:T(1024)} %param.13) | copy-start | bytes 18436
  68.6 2.9 %copy-start = (bf16[1536,2304]{0,1:T(8,128)(2,1)}, bf16[1536,2304]{0,1:T(8,128)(2,1)S(1)}, u32[]{:S(2)}) copy-start(bf16[1536,2304]{0,1:T(8,128)(2,1)S(1)} %fusion) | copy-start | bytes 21233668
  68.6 3.7 %copy-start.7 = (f32[6,12]{1,0:T(8,128)S(1)}, f32[6,12]{1,0:T(8,128)}, u32[]{:S(2)}) copy-start(f32[6,12]{1,0:T(8,128)} %param.18) | copy-start | bytes 868
  72.3 81.7 %reduce-scatter.4.cloned.1.call-start = ((), (), s32[]{:S(2)}) async-start(), calls=%async_computation.3 | async-start | bytes 1966080
  75.5 1.0 copy-start.2
  75.5 1.0 copy-start.6
Sparse Core Ops, SparseCore 0:
  10.7 53.4 all-gather.3
  72.5 37.0 all-gather.5
  119.9 34.1 reduce-scatter.3
where the time goes:
time: 168 us; the launch traced here: 167 us
  waiting for transfers between devices  113 us (67%)
  local copies, waits for them, and re-layouts  15.2 us (9%)
  between operations  13.4 us (8%)
  matrix products  11.1 us (7%)
  other arithmetic  8.71 us (5%)
  blocking collectives  6.11 us (4%)
    all_gather x1, waiting for transfers between devices, local(): lax.all_gather(input_codes.astype(jnp.float32), 'weight', axis=0, tiled=T...  46.7 us
    unnamed x4, waiting for transfers between devices  33.7 us
    all_gather x1, waiting for transfers between devices, query_side(): all_pairs = lax.all_gather(keys_values, 'seq', axis=0, tiled=True)  32.3 us
    unnamed x31, local copies, waits for them, and re-layouts  12.1 us
    all_gather x1, blocking collectives, local(): lax.all_gather(input_scales, 'weight', axis=0, tiled=True)  6.11 us
    convert_element_type x2, other arithmetic, dequantize(): return (codes.astype(jnp.float32) * expanded).astype(jnp.bfloat16)  4.89 us
    dot_general x1, matrix products, local(): jnp.dot(grad_proj, input_weight.T, preferred_element_type=jnp.float32)  4.29 us
  transfers between devices with their start and end apart: 3, of which 3 were waited for; matrix products, arithmetic and copies ran while one was open for 3% of the time, Pallas kernels for 0%

commit v1 on v0

--- a/solution.py
+++ b/solution.py
@@ -3,12 +3,318 @@
 import jax
 import jax.numpy as jnp
 from jax import lax
+from jax.experimental import pallas as pl
+from jax.experimental.pallas import tpu as pltpu
 from jax.sharding import PartitionSpec as P
 
 HEADS = 12
 HEAD_DIM = 64
 QBLOCK = 128
 HD = 768
+HALF = HD // 2
+EPSILON = 1e-06
+VMEM = pltpu.VMEM
+SMEM = pltpu.SMEM
+
+
+def half_index():
+    return lax.axis_index("seq") * 2 // lax.axis_size("seq")
+
+
+def spec(memory_space=VMEM):
+    return pl.BlockSpec(memory_space=memory_space)
+
+
+def norm_rows(rows):
+    mean_value = jnp.mean(rows, axis=-1, keepdims=True)
+    centered = rows - mean_value
+    variance = jnp.mean(centered * centered, axis=-1, keepdims=True)
+    inverse = lax.rsqrt(variance + EPSILON)
+    return centered * inverse, inverse
+
+
+def copy_columns(codes_ref, held, sems, half):
+    copies = []
+    for part in range(3):
+        start = pl.multiple_of(part * HD + half * HALF, QBLOCK)
+        copies.append(
+            pltpu.make_async_copy(
+                codes_ref.at[:, pl.ds(start, HALF)],
+                held.at[:, pl.ds(part * HALF, HALF)],
+                sems.at[part],
+            )
+        )
+        copies[-1].start()
+    return copies
+
+
+def scale_columns(copies, held, scales_ref, out_ref, half):
+    row_blocks = held.shape[0] // QBLOCK
+    for part in range(3):
+        copies[part].wait()
+        for r in range(row_blocks):
+            for c in range(HALF // QBLOCK):
+                scale = scales_ref[r, (part * HD + c * QBLOCK) // QBLOCK + half * (HALF // QBLOCK)]
+                at = (
+                    slice(r * QBLOCK, (r + 1) * QBLOCK),
+                    slice(part * HALF + c * QBLOCK, part * HALF + (c + 1) * QBLOCK),
+                )
+                out_ref[at] = (held[at].astype(jnp.float32) * scale).astype(jnp.bfloat16)
+
+
+def first_kernel(tokens_ref, gain_ref, shift_ref, scales_ref, codes_ref, norm_ref, weight_ref, held, sems):
+    half = half_index()
+    copies = copy_columns(codes_ref, held, sems, half)
+    gain = gain_ref[...]
+    shift = shift_ref[...]
+    for r in range(0, tokens_ref.shape[1], 16):
+        normed, _ = norm_rows(tokens_ref[0, r : r + 16, :].astype(jnp.float32))
+        norm_ref[r : r + 16, :] = (normed * gain + shift).astype(jnp.bfloat16)
+    scale_columns(copies, held, scales_ref, weight_ref, half)
+
+
+def first_step(tokens, gain, shift, scales, codes):
+    rows = codes.shape[0]
+    return pl.pallas_call(
+        first_kernel,
+        out_shape=(
+            jax.ShapeDtypeStruct(tokens.shape[1:], jnp.bfloat16),
+            jax.ShapeDtypeStruct((rows, 3 * HALF), jnp.bfloat16),
+        ),
+        in_specs=[spec(), spec(), spec(), spec(SMEM), spec(pl.ANY)],
+        out_specs=(spec(), spec()),
+        scratch_shapes=[VMEM((rows, 3 * HALF), codes.dtype), pltpu.SemaphoreType.DMA((3,))],
+        name="norm_and_near_weight",
+    )(tokens, gain, shift, scales, codes)
+
+
+def second_kernel(
+    grad_ref, layer_ref, out_scales_ref, out_codes_ref, scales_ref, codes_ref,
+    near_ref, far_ref, weight_ref, held, sems, scaled, out_weight
+):
+    half = half_index()
+    other = 1 - half
+    copies = copy_columns(codes_ref, held, sems, other)
+    scaled[...] = (grad_ref[0].astype(jnp.float32) * layer_ref[...]).astype(jnp.bfloat16)
+    width = grad_ref.shape[2]
+    for out_ref, which in ((far_ref, other), (near_ref, half)):
+        for r in range(HALF // QBLOCK):
+            first = pl.multiple_of(which * HALF + r * QBLOCK, QBLOCK)
+            for c in range(width // QBLOCK):
+                scale = out_scales_ref[which * (HALF // QBLOCK) + r, c]
+                cols = slice(c * QBLOCK, (c + 1) * QBLOCK)
+                out_weight[r * QBLOCK : (r + 1) * QBLOCK, cols] = (
+                    out_codes_ref[pl.ds(first, QBLOCK), cols].astype(jnp.float32) * scale
+                ).astype(jnp.bfloat16)
+        out_ref[...] = lax.dot_general(
+            scaled[...], out_weight[...], (((1,), (1,)), ((), ())), preferred_element_type=jnp.float32
+        ).astype(jnp.bfloat16)
+    scale_columns(copies, held, scales_ref, weight_ref, other)
+
+
+def second_step(grad, layer_scale, out_scales, out_codes, scales, codes):
+    rows = codes.shape[0]
+    tokens, width = grad.shape[1:]
+    return pl.pallas_call(
+        second_kernel,
+        out_shape=(
+            jax.ShapeDtypeStruct((tokens, HALF), jnp.bfloat16),
+            jax.ShapeDtypeStruct((tokens, HALF), jnp.bfloat16),
+            jax.ShapeDtypeStruct((rows, 3 * HALF), jnp.bfloat16),
+        ),
+        in_specs=[spec(), spec(), spec(SMEM), spec(), spec(SMEM), spec(pl.ANY)],
+        out_specs=(spec(), spec(), spec()),
+        scratch_shapes=[
+            VMEM((rows, 3 * HALF), codes.dtype),
+            pltpu.SemaphoreType.DMA((3,)),
+            VMEM((tokens, width), jnp.bfloat16),
+            VMEM((HALF, width), jnp.bfloat16),
+        ],
+        name="head_grads_and_far_weight",
+    )(grad, layer_scale, out_scales, out_codes, scales, codes)
+
+
+def dot_last(a, b):
+    return lax.dot_general(a, b, (((1,), (1,)), ((), ())), preferred_element_type=jnp.float32)
+
+
+def dot_plain(a, b):
+    return jnp.dot(a, b, preferred_element_type=jnp.float32)
+
+
+def attention_kernel(*refs):
+    norms, weights, grads = refs[0:4], refs[4:8], refs[8:12]
+    bias_ref = refs[12]
+    outs = refs[13:17]
+    proj = refs[17]
+    mine = lax.axis_index("weight")
+    half = half_index()
+    depth = weights[0].shape[0]
+    tokens = norms[0].shape[0]
+    total = tokens * len(norms)
+
+    rows = []
+    for norm_ref in norms:
+        rows.append(
+            jnp.concatenate(
+                [
+                    norm_ref[:, pl.ds(pl.multiple_of((mine ^ j) * depth, QBLOCK), depth)]
+                    for j in range(len(weights))
+                ],
+                axis=1,
+            )
+        )
+    rows = jnp.concatenate(rows, axis=0)
+    for part in range(3):
+        columns = jnp.concatenate([w[:, part * HALF : (part + 1) * HALF] for w in weights], axis=0)
+        bias = bias_ref[:, pl.ds(pl.multiple_of(part * HD + half * HALF, QBLOCK), HALF)]
+        value = (dot_plain(rows, columns) + bias).astype(jnp.bfloat16)
+        if part == 0:
+            value = value * jnp.bfloat16(HEAD_DIM**-0.5)
+        proj[:, part * HALF : (part + 1) * HALF] = value
+
+    pair = 2 * HEAD_DIM
+    low = lax.broadcasted_iota(jnp.int32, (total, pair), 1) < HEAD_DIM
+    zero = jnp.zeros((total, pair), jnp.bfloat16)
+    step = 256
+    for t in range(HALF // pair):
+        query = proj[:, t * pair : (t + 1) * pair]
+        key = proj[:, HALF + t * pair : HALF + (t + 1) * pair]
+        value = proj[:, 2 * HALF + t * pair : 2 * HALF + (t + 1) * pair]
+        grad = jnp.concatenate([g[:, t * pair : (t + 1) * pair] for g in grads], axis=0)
+        key_t = key.T
+        key_grad = jnp.zeros((total, pair), jnp.float32)
+        value_grad = jnp.zeros((total, pair), jnp.float32)
+        query_grad_t = []
+        for side in range(2):
+            mask = low if side == 0 else ~low
+            key_m = jnp.where(mask, key, zero)
+            value_m = jnp.where(mask, value, zero)
+            query_m = jnp.where(mask, query, zero)
+            grad_m = jnp.where(mask, grad, zero)
+            blocks = []
+            for first in range(0, total, step):
+                at = slice(first, first + step)
+                scores = dot_last(key_m, query[at])
+                dprob = dot_last(value_m, grad[at])
+                expo = jnp.exp(scores - jnp.max(scores, axis=0, keepdims=True))
+                scale = 1.0 / jnp.sum(expo, axis=0, keepdims=True)
+                delta = jnp.sum(expo * dprob, axis=0, keepdims=True) * scale
+                prob = expo * scale
+                dscore = (prob * (dprob - delta)).astype(jnp.bfloat16)
+                key_grad += dot_plain(dscore, query_m[at])
+                value_grad += dot_plain(prob.astype(jnp.bfloat16), grad_m[at])
+                blocks.append(dot_plain(key_t[side * HEAD_DIM : (side + 1) * HEAD_DIM], dscore))
+            query_grad_t.append(jnp.concatenate(blocks, axis=1))
+        query_grad = jnp.concatenate(query_grad_t, axis=0).T * HEAD_DIM**-0.5
+        for part, piece in enumerate((query_grad, key_grad, value_grad)):
+            piece = piece.astype(jnp.bfloat16)
+            for i, out in enumerate(outs):
+                out[:, part * HALF + t * pair : part * HALF + (t + 1) * pair] = piece[
+                    i * tokens : (i + 1) * tokens
+                ]
+
+
+def attention_step(norms, weights, grads, bias):
+    tokens = norms[0].shape[0]
+    return pl.pallas_call(
+        attention_kernel,
+        out_shape=tuple(jax.ShapeDtypeStruct((tokens, 3 * HALF), jnp.bfloat16) for _ in norms),
+        in_specs=[spec()] * 13,
+        out_specs=(spec(),) * 4,
+        scratch_shapes=[VMEM((tokens * len(norms), 3 * HALF), jnp.bfloat16)],
+        compiler_params=pltpu.CompilerParams(vmem_limit_bytes=40 * 2**20),
+        name="attention",
+    )(*norms, *weights, *grads, bias)
+
+
+def last_kernel(*refs):
+    near_w, far_w = refs[0:4], refs[4:8]
+    own_ref, back_ref, cross_ref, skip_ref, tokens_ref, gain_ref, out_ref, grad_norm = refs[8:]
+    mine = lax.axis_index("weight")
+    place = lax.axis_index("seq")
+    middle = (place == 1) | (place == 2)
+    near = jnp.where(middle, own_ref[...], back_ref[...])
+    far = jnp.where(middle, cross_ref[...], skip_ref[...])
+    depth = near_w[0].shape[0]
+    for j in range(4):
+        value = dot_last(near, near_w[j][...]) + dot_last(far, far_w[j][...])
+        grad_norm[:, pl.ds(pl.multiple_of((mine ^ j) * depth, QBLOCK), depth)] = value
+    gain = gain_ref[...]
+    for r in range(0, tokens_ref.shape[1], 16):
+        normed, inverse = norm_rows(tokens_ref[0, r : r + 16, :].astype(jnp.float32))
+        grad_hat = grad_norm[r : r + 16, :] * gain
+        first_mean = jnp.mean(grad_hat, axis=-1, keepdims=True)
+        second_mean = jnp.mean(grad_hat * normed, axis=-1, keepdims=True)
+        out_ref[0, r : r + 16, :] = inverse * (grad_hat - first_mean - normed * second_mean)
+
+
+def last_step(near_w, far_w, own, back, cross, skip, tokens, gain):
+    return pl.pallas_call(
+        last_kernel,
+        out_shape=jax.ShapeDtypeStruct(tokens.shape, jnp.float32),
+        in_specs=[spec()] * 14,
+        out_specs=spec(),
+        scratch_shapes=[VMEM(tokens.shape[1:], jnp.float32)],
+        compiler_params=pltpu.CompilerParams(vmem_limit_bytes=40 * 2**20),
+        name="input_grad",
+    )(*near_w, *far_w, own, back, cross, skip, tokens, gain)
+
+
+END_TO_MIDDLE = [(0, 1), (3, 2)]
+MIDDLE = [(1, 2), (2, 1)]
+END_TO_FAR = [(0, 2), (3, 1)]
+MIDDLE_TO_END = [(1, 0), (2, 3)]
+FAR_TO_END = [(1, 3), (2, 0)]
+
+
+def flip(bit):
+    return [(i, i ^ bit) for i in range(4)]
+
+
+def spread_weight(mine):
+    across = lax.ppermute(mine, "weight", flip(2))
+    beside = lax.ppermute(mine, "weight", flip(1))
+    diagonal = lax.ppermute(across, "weight", flip(1))
+    return (mine, beside, across, diagonal)
+
+
+def local_middle(
+    tokens,
+    upstream_grad,
+    norm_gain,
+    norm_bias,
+    input_codes,
+    input_scales,
+    input_bias,
+    output_codes,
+    output_scales,
+    layer_scale,
+):
+    gain = norm_gain[None]
+    norm_out, near_mine = first_step(tokens, gain, norm_bias[None], input_scales, input_codes)
+    near_w = spread_weight(near_mine)
+    norm_far = lax.ppermute(norm_out, "seq", END_TO_FAR)
+    norm_mid = lax.ppermute(norm_out, "seq", MIDDLE)
+    norm_end = lax.ppermute(norm_out, "seq", END_TO_MIDDLE)
+    grad_near, grad_far, far_mine = second_step(
+        upstream_grad, layer_scale[None], output_scales, output_codes, input_scales, input_codes
+    )
+    head_far = lax.ppermute(grad_far, "seq", END_TO_FAR)
+    head_mid = lax.ppermute(grad_far, "seq", MIDDLE)
+    head_end = lax.ppermute(grad_near, "seq", END_TO_MIDDLE)
+    own, end, mid, far = attention_step(
+        (norm_out, norm_end, norm_mid, norm_far),
+        near_w,
+        (grad_near, head_end, head_mid, head_far),
+        input_bias[None],
+    )
+    far_mine, _ = lax.optimization_barrier((far_mine, near_w[2]))
+    far_w = spread_weight(far_mine)
+    skip = lax.ppermute(far, "seq", FAR_TO_END)
+    cross = lax.ppermute(mid, "seq", MIDDLE)
+    back = lax.ppermute(end, "seq", MIDDLE_TO_END)
+    return last_step(near_w, far_w, own, back, cross, skip, tokens, gain)
 
 
 def dequantize(codes, scales):
@@ -174,4 +480,6 @@
         P(),
     )
     out_specs = P(("groups", "weight"), "seq", None)
-    return jax.shard_map(local, mesh=mesh, in_specs=in_specs, out_specs=out_specs, check_vma=False)
+    fits = mesh.shape["seq"] == 4 and mesh.shape["weight"] == 4
+    plan = local_middle if fits else local
+    return jax.shard_map(plan, mesh=mesh, in_specs=in_specs, out_specs=out_specs, check_vma=False)

time: 168 us -> 100 us (0.60)
  waiting for transfers between devices: 113 us -> 40.6 us
  starting transfers between devices: 0.09 us -> 33.2 us
  Pallas kernels: 0 us -> 21.1 us
  between operations: 13.4 us -> 0.24 us
  matrix products: 11.1 us -> 0 us
  local copies, waits for them, and re-layouts: 15.2 us -> 4.81 us
  other arithmetic: 8.71 us -> 0 us
  blocking collectives: 6.11 us -> 0 us
    all_gather x2 -> x0, waiting for transfers between devices: 79 us -> none  [the longest x1 46.7 us: local(): lax.all_gather(input_codes.astype(jnp.float32), 'weight', axis=0, tiled=T...]
    ppermute x0 -> x15, waiting for transfers between devices: none -> 40.6 us  [the longest x2 13.8 us: spread_weight(): across = lax.ppermute(mine, 'weight', flip(2))]
    unnamed x4 -> x0, waiting for transfers between devices: 33.7 us -> none
    ppermute x0 -> x15, starting transfers between devices: none -> 33.2 us  [the longest x1 14.4 us: local_middle(): norm_far = lax.ppermute(norm_out, 'seq', END_TO_FAR)]
    pallas_call x0 -> x4, Pallas kernels: none -> 21.1 us  [the longest x1 9.58 us: attention_step(): pl.pallas_call(attention_kernel, out_shape=tuple((jax.ShapeDtypeStruct((t...]
    unnamed x31 -> x14, local copies, waits for them, and re-layouts: 12.1 us -> 0.93 us
    dot_general x8 -> x0, matrix products: 11.1 us -> none  [the longest x1 4.29 us: local(): jnp.dot(grad_proj, input_weight.T, preferred_element_type=jnp.float32)]
    all_gather x1 -> x0, blocking collectives: 6.11 us -> none  [local(): lax.all_gather(input_scales, 'weight', axis=0, tiled=True)]
  transfers between devices with their start and end apart: 3 -> 15, of which waited for: 3 -> 7; matrix products, arithmetic and copies ran while one was open for 3% -> 1% of each run, Pallas kernels for 0% -> 14%
where the time goes in v1:
time: 100 us; the launch traced here: 99.9 us
  waiting for transfers between devices  40.6 us (41%)
  starting transfers between devices  33.2 us (33%)
  Pallas kernels  21.1 us (21%)
  local copies, waits for them, and re-layouts  4.81 us (5%)
    ppermute x1, starting transfers between devices, local_middle(): norm_far = lax.ppermute(norm_out, 'seq', END_TO_FAR)  14.4 us
    ppermute x2, waiting for transfers between devices, spread_weight(): across = lax.ppermute(mine, 'weight', flip(2))  13.8 us
    pallas_call x1, Pallas kernels, attention_step(): pl.pallas_call(attention_kernel, out_shape=tuple((jax.ShapeDtypeStruct((t...  9.58 us
    ppermute x1, waiting for transfers between devices, local_middle(): back = lax.ppermute(end, 'seq', MIDDLE_TO_END)  8.48 us
    ppermute x1, waiting for transfers between devices, local_middle(): head_end = lax.ppermute(grad_near, 'seq', END_TO_MIDDLE)  8.08 us
    ppermute x1, starting transfers between devices, local_middle(): head_far = lax.ppermute(grad_far, 'seq', END_TO_FAR)  6.19 us
    ppermute x1, waiting for transfers between devices, local_middle(): norm_far = lax.ppermute(norm_out, 'seq', END_TO_FAR)  5.19 us
    pallas_call x1, Pallas kernels, second_step(): pl.pallas_call(second_kernel, out_shape=(jax.ShapeDtypeStruct((tokens, HA...  4.83 us
  transfers between devices with their start and end apart: 15, of which 7 were waited for; matrix products, arithmetic and copies ran while one was open for 1% of the time, Pallas kernels for 14%

profile of v1, /device:TPU:0, one launch (start us, length us, event | category | flops | bytes accessed | tf_op | source)
XLA Modules:
  0.0 99.9 jit_solution(816004109952489083)
XLA Ops:
  0.0 1.3 %broadcast_in_dim.12.gain_ref.refs_13_ = f32[1,1536]{1,0:T(1,128)} reshape(f32[1536]{0:T(1024)} %param.12) | data formatting | bytes 12288 | tf_op jit(solution)/shard_map/broadcast_in_dim | solution.py:294
  1.3 1.3 %broadcast_in_dim.13.shift_ref = f32[1,1536]{1,0:T(1,128)} reshape(f32[1536]{0:T(1024)} %param.13) | data formatting | bytes 12288 | tf_op jit(solution)/shard_map/broadcast_in_dim | solution.py:295
  2.6 3.3 %norm_and_near_weight.1 = (bf16[128,1536]{1,0:T(8,128)(2,1)}, bf16[384,1152]{1,0:T(8,128)(2,1)}) custom-call(bf16[1,128,1536]{2,1,0:T(8,128)(2,1)} %refs_12_.1, f32[1,1536]{1,0:T(1,128)} %broadcast_in_dim.12.gain_ref.refs_13_, f32[1,1536]{1,0:T(1,128)} %broadcast_in_dim.13.shift_ref, f32[3,18]{1,0:T(4,128)} %scales_ref.3, bf16[384,2304]{1,0:T(8,128)(2,1)} %codes_ref.3), custom_call_target="tpu_custom_call" | custom-call | tf_op jit(solution)/shard_map/norm_and_near_weight/pallas_call | solution.py:78
  5.9 0.0 copy-start.3
  5.9 0.0 copy-start.6
  5.9 3.0 %collective-permute-start.1 = (bf16[384,1152]{1,0:T(8,128)(2,1)}, bf16[384,1152]{1,0:T(8,128)(2,1)S(1)}, u32[]{:S(2)}, u32[]{:S(2)}) collective-permute-start(bf16[384,1152]{1,0:T(8,128)(2,1)} %get-tuple-element.15.refs_4_.refs_0_), channel_id=1, source_target_pairs={{0,2},{1,3},{2,0},{3,1},{4,6},{5,7},{6,4},{7,5},{8,10},{9,11},{10,... | collective-permute-start | bytes 2654216 | tf_op jit(solution)/shard_map/ppermute | solution.py:276
  8.9 1.3 %broadcast_in_dim.14.layer_ref = f32[1,1536]{1,0:T(1,128)} reshape(f32[1536]{0:T(1024)} %param.19) | data formatting | bytes 12288 | tf_op jit(solution)/shard_map/broadcast_in_dim | solution.py:301
  10.2 4.8 %head_grads_and_far_weight.1 = (bf16[128,384]{1,0:T(8,128)(2,1)}, bf16[128,384]{1,0:T(8,128)(2,1)}, bf16[384,1152]{1,0:T(8,128)(2,1)}) custom-call(bf16[1,128,1536]{2,1,0:T(8,128)(2,1)} %grad_ref.1, f32[1,1536]{1,0:T(1,128)} %broadcast_in_dim.14.layer_ref, f32[6,12]{1,0:T(8,128)} %out_scales_ref.1, bf16[768,1536]{1,0:T(8,128)(2,1)} %out_codes_ref.1, ...), custom_call_target="tpu_custom_call" | custom-call | tf_op jit(solution)/shard_map/head_grads_and_far_weight/pallas_call | solution.py:118
  15.0 13.7 %collective-permute-done.1.refs_6_.refs_2_ = bf16[384,1152]{1,0:T(8,128)(2,1)S(1)} collective-permute-done((bf16[384,1152]{1,0:T(8,128)(2,1)}, bf16[384,1152]{1,0:T(8,128)(2,1)S(1)}, u32[]{:S(2)}, u32[]{:S(2)}) %collective-permute-start.1) | collective-permute-done | bytes 884768 | tf_op jit(solution)/shard_map/ppermute | solution.py:276
  28.8 1.7 %collective-permute-start.4 = (bf16[384,1152]{1,0:T(8,128)(2,1)}, bf16[384,1152]{1,0:T(8,128)(2,1)S(1)}, u32[]{:S(2)}, u32[]{:S(2)}) collective-permute-start(bf16[384,1152]{1,0:T(8,128)(2,1)} %get-tuple-element.17.refs_4_), channel_id=1, source_target_pairs={{0,2},{1,3},{2,0},{3,1},{4,6},{5,7},{6,4},{7,5},{8,10},{9,11},{10,... | collective-permute-start | bytes 2654216 | tf_op jit(solution)/shard_map/ppermute | solution.py:276
  30.5 0.7 collective-permute-start.10
  31.2 6.2 %collective-permute-start.11 = (bf16[128,384]{1,0:T(8,128)(2,1)}, bf16[128,384]{1,0:T(8,128)(2,1)S(1)}, u32[]{:S(2)}, u32[]{:S(2)}) collective-permute-start(bf16[128,384]{1,0:T(8,128)(2,1)} %get-tuple-element.20), channel_id=1, source_target_pairs={{0,8},{12,4},{1,9},{13,5},{2,10},{14,6},{3,11},{15,7},{16,24},{28,... | collective-permute-start | bytes 294920 | tf_op jit(solution)/shard_map/ppermute | solution.py:303
  37.4 1.4 %collective-permute-start.6 = (bf16[128,1536]{1,0:T(8,128)(2,1)S(1)}, bf16[128,1536]{1,0:T(8,128)(2,1)S(1)}, u32[]{:S(2)}, u32[]{:S(2)}) collective-permute-start(bf16[128,1536]{1,0:T(8,128)(2,1)S(1)} %copy-done.3), channel_id=1, source_target_pairs={{0,4},{12,8},{1,5},{13,9},{2,6},{14,10},{3,7},{15,11},{16,20},{28,... | collective-permute-start | bytes 1179656 | tf_op jit(solution)/shard_map/ppermute | solution.py:299
  38.8 1.3 %collective-permute-start.9 = (bf16[128,384]{1,0:T(8,128)(2,1)}, bf16[128,384]{1,0:T(8,128)(2,1)S(1)}, u32[]{:S(2)}, u32[]{:S(2)}) collective-permute-start(bf16[128,384]{1,0:T(8,128)(2,1)} %get-tuple-element.19.refs_8_), channel_id=1, source_target_pairs={{0,4},{12,8},{1,5},{13,9},{2,6},{14,10},{3,7},{15,11},{16,20},{28,... | collective-permute-start | bytes 294920 | tf_op jit(solution)/shard_map/ppermute | solution.py:305
  40.1 0.1 collective-permute-start
  40.2 0.7 collective-permute-done.11.refs_11_
  40.9 8.1 %collective-permute-done.9.refs_9_ = bf16[128,384]{1,0:T(8,128)(2,1)S(1)} collective-permute-done((bf16[128,384]{1,0:T(8,128)(2,1)}, bf16[128,384]{1,0:T(8,128)(2,1)S(1)}, u32[]{:S(2)}, u32[]{:S(2)}) %collective-permute-start.9) | collective-permute-done | bytes 98336 | tf_op jit(solution)/shard_map/ppermute | solution.py:305
  49.0 0.7 collective-permute-start.7
  49.7 0.1 collective-permute-start.3
  49.7 0.1 collective-permute-done.4.refs_6_
  49.8 0.4 collective-permute-start.5
  50.2 14.4 %collective-permute-start.8 = (bf16[128,1536]{1,0:T(8,128)(2,1)S(1)}, bf16[128,1536]{1,0:T(8,128)(2,1)S(1)}, u32[]{:S(2)}, u32[]{:S(2)}) collective-permute-start(bf16[128,1536]{1,0:T(8,128)(2,1)S(1)} %copy-done.3), channel_id=1, source_target_pairs={{0,8},{12,4},{1,9},{13,5},{2,10},{14,6},{3,11},{15,7},{16,24},{28,... | collective-permute-start | bytes 1179656 | tf_op jit(solution)/shard_map/ppermute | solution.py:297
  64.6 0.0 copy-start.1
  64.7 5.2 %collective-permute-done.8.refs_3_ = bf16[128,1536]{1,0:T(8,128)(2,1)S(1)} collective-permute-done((bf16[128,1536]{1,0:T(8,128)(2,1)S(1)}, bf16[128,1536]{1,0:T(8,128)(2,1)S(1)}, u32[]{:S(2)}, u32[]{:S(2)}) %collective-permute-start.8) | collective-permute-done | bytes 393248 | tf_op jit(solution)/shard_map/ppermute | solution.py:297
  69.9 0.9 copy-done.4
  70.8 9.6 %attention.1 = (bf16[128,1152]{1,0:T(8,128)(2,1)S(1)}, bf16[128,1152]{1,0:T(8,128)(2,1)S(1)}, bf16[128,1152]{1,0:T(8,128)(2,1)S(1)}, bf16[128,1152]{1,0:T(8,128)(2,1)S(1)}) custom-call(bf16[128,1536]{1,0:T(8,128)(2,1)S(1)} %copy-done.3, bf16[128,1536]{1,0:T(8,128)(2,1)S(1)} %collective-permute-done.6.refs_1_, ...), custom_call_target="tpu_custom_call" | custom-call | tf_op jit(solution)/shard_map/attention/pallas_call | solution.py:220
  80.4 1.3 %collective-permute-start.12 = (bf16[128,1152]{1,0:T(8,128)(2,1)S(1)}, bf16[128,1152]{1,0:T(8,128)(2,1)S(1)}, u32[]{:S(2)}, u32[]{:S(2)}) collective-permute-start(bf16[128,1152]{1,0:T(8,128)(2,1)S(1)} %get-tuple-element.22), channel_id=1, source_target_pairs={{4,0},{8,12},{5,1},{9,13},{6,2},{10,14},{7,3},{11,15},{20,16},{24,... | collective-permute-start | bytes 884744 | tf_op jit(solution)/shard_map/ppermute | solution.py:316
  81.7 0.7 collective-permute-start.13
  82.3 1.3 %collective-permute-start.14 = (bf16[128,1152]{1,0:T(8,128)(2,1)S(1)}, bf16[128,1152]{1,0:T(8,128)(2,1)S(1)}, u32[]{:S(2)}, u32[]{:S(2)}) collective-permute-start(bf16[128,1152]{1,0:T(8,128)(2,1)S(1)} %get-tuple-element.24), channel_id=1, source_target_pairs={{4,12},{8,0},{5,13},{9,1},{6,14},{10,2},{7,15},{11,3},{20,28},{24,... | collective-permute-start | bytes 884744 | tf_op jit(solution)/shard_map/ppermute | solution.py:314
  83.7 8.5 %collective-permute-done.12.refs_9_ = bf16[128,1152]{1,0:T(8,128)(2,1)S(1)} collective-permute-done((bf16[128,1152]{1,0:T(8,128)(2,1)S(1)}, bf16[128,1152]{1,0:T(8,128)(2,1)S(1)}, u32[]{:S(2)}, u32[]{:S(2)}) %collective-permute-start.12) | collective-permute-done | bytes 294944 | tf_op jit(solution)/shard_map/ppermute | solution.py:316
  92.1 4.3 %collective-permute-done.14.refs_11_ = bf16[128,1152]{1,0:T(8,128)(2,1)S(1)} collective-permute-done((bf16[128,1152]{1,0:T(8,128)(2,1)S(1)}, bf16[128,1152]{1,0:T(8,128)(2,1)S(1)}, u32[]{:S(2)}, u32[]{:S(2)}) %collective-permute-start.14) | collective-permute-done | bytes 294944 | tf_op jit(solution)/shard_map/ppermute | solution.py:314
  96.5 3.4 %input_grad.1 = f32[1,128,1536]{2,1,0:T(8,128)} custom-call(bf16[384,1152]{1,0:T(8,128)(2,1)S(1)} %copy-done, bf16[384,1152]{1,0:T(8,128)(2,1)S(1)} %collective-permute-done.refs_5_.refs_1_, bf16[384,1152]{1,0:T(8,128)(2,1)S(1)} %collective-permute-done.1.refs_6_.refs_2_, bf16[384,1152]{1,0:T(8,128)(2,1)S(1)} %collective-permute-done.2.refs_7_.refs_3_, ...), custom_call_target="tpu_custom_call" | custom-call | tf_op jit(solution)/shard_map/input_grad/pallas_call | solution.py:253
  (20 shorter events, 0.1 us)
Async XLA Ops:
  5.9 31.5 %copy-start.3 = (bf16[128,1536]{1,0:T(8,128)(2,1)S(1)}, bf16[128,1536]{1,0:T(8,128)(2,1)}, u32[]{:S(2)}) copy-start(bf16[128,1536]{1,0:T(8,128)(2,1)} %get-tuple-element.18.refs_0_) | copy-start | bytes 1179652
  5.9 34.2 %copy-start = (bf16[384,1152]{1,0:T(8,128)(2,1)S(1)}, bf16[384,1152]{1,0:T(8,128)(2,1)}, u32[]{:S(2)}) copy-start(bf16[384,1152]{1,0:T(8,128)(2,1)} %get-tuple-element.15.refs_4_.refs_0_) | copy-start | bytes 2654212
  5.9 58.7 %copy-start.6 = (f32[2304]{0:T(1024)S(1)}, f32[2304]{0:T(1024)}, u32[]{:S(2)}) copy-start(f32[2304]{0:T(1024)} %param.16) | copy-start | bytes 27652
  5.9 22.9 %collective-permute-start.1 = (bf16[384,1152]{1,0:T(8,128)(2,1)}, bf16[384,1152]{1,0:T(8,128)(2,1)S(1)}, u32[]{:S(2)}, u32[]{:S(2)}) collective-permute-start(bf16[384,1152]{1,0:T(8,128)(2,1)} %get-tuple-element.15.refs_4_.refs_0_), channel_id=1, source_target_pairs={{0,2},{1,3},{2,0},{3,1},{4,6},{5,7},{6,4},{7,5},{8,10},{9,11},{10,... | collective-permute-start | bytes 2654216 | tf_op jit(solution)/shard_map/ppermute | solution.py:276
  28.8 21.0 %collective-permute-start.4 = (bf16[384,1152]{1,0:T(8,128)(2,1)}, bf16[384,1152]{1,0:T(8,128)(2,1)S(1)}, u32[]{:S(2)}, u32[]{:S(2)}) collective-permute-start(bf16[384,1152]{1,0:T(8,128)(2,1)} %get-tuple-element.17.refs_4_), channel_id=1, source_target_pairs={{0,2},{1,3},{2,0},{3,1},{4,6},{5,7},{6,4},{7,5},{8,10},{9,11},{10,... | collective-permute-start | bytes 2654216 | tf_op jit(solution)/shard_map/ppermute | solution.py:276
  30.5 9.6 %collective-permute-start.10 = (bf16[128,384]{1,0:T(8,128)(2,1)}, bf16[128,384]{1,0:T(8,128)(2,1)S(1)}, u32[]{:S(2)}, u32[]{:S(2)}) collective-permute-start(bf16[128,384]{1,0:T(8,128)(2,1)} %get-tuple-element.20), channel_id=1, source_target_pairs={{4,8},{8,4},{5,9},{9,5},{6,10},{10,6},{7,11},{11,7},{20,24},{24,20... | collective-permute-start | bytes 294920 | tf_op jit(solution)/shard_map/ppermute | solution.py:304
  31.2 9.7 %collective-permute-start.11 = (bf16[128,384]{1,0:T(8,128)(2,1)}, bf16[128,384]{1,0:T(8,128)(2,1)S(1)}, u32[]{:S(2)}, u32[]{:S(2)}) collective-permute-start(bf16[128,384]{1,0:T(8,128)(2,1)} %get-tuple-element.20), channel_id=1, source_target_pairs={{0,8},{12,4},{1,9},{13,5},{2,10},{14,6},{3,11},{15,7},{16,24},{28,... | collective-permute-start | bytes 294920 | tf_op jit(solution)/shard_map/ppermute | solution.py:303
  37.4 12.3 %collective-permute-start.6 = (bf16[128,1536]{1,0:T(8,128)(2,1)S(1)}, bf16[128,1536]{1,0:T(8,128)(2,1)S(1)}, u32[]{:S(2)}, u32[]{:S(2)}) collective-permute-start(bf16[128,1536]{1,0:T(8,128)(2,1)S(1)} %copy-done.3), channel_id=1, source_target_pairs={{0,4},{12,8},{1,5},{13,9},{2,6},{14,10},{3,7},{15,11},{16,20},{28,... | collective-permute-start | bytes 1179656 | tf_op jit(solution)/shard_map/ppermute | solution.py:299
  38.8 10.2 %collective-permute-start.9 = (bf16[128,384]{1,0:T(8,128)(2,1)}, bf16[128,384]{1,0:T(8,128)(2,1)S(1)}, u32[]{:S(2)}, u32[]{:S(2)}) collective-permute-start(bf16[128,384]{1,0:T(8,128)(2,1)} %get-tuple-element.19.refs_8_), channel_id=1, source_target_pairs={{0,4},{12,8},{1,5},{13,9},{2,6},{14,10},{3,7},{15,11},{16,20},{28,... | collective-permute-start | bytes 294920 | tf_op jit(solution)/shard_map/ppermute | solution.py:305
  40.1 29.7 %collective-permute-start = (bf16[384,1152]{1,0:T(8,128)(2,1)S(1)}, bf16[384,1152]{1,0:T(8,128)(2,1)S(1)}, u32[]{:S(2)}, u32[]{:S(2)}) collective-permute-start(bf16[384,1152]{1,0:T(8,128)(2,1)S(1)} %copy-done), channel_id=1, source_target_pairs={{0,1},{1,0},{2,3},{3,2},{4,5},{5,4},{6,7},{7,6},{8,9},{9,8},{10,11... | collective-permute-start | bytes 2654216 | tf_op jit(solution)/shard_map/ppermute | solution.py:277
  40.9 29.0 %collective-permute-start.2 = (bf16[384,1152]{1,0:T(8,128)(2,1)S(1)}, bf16[384,1152]{1,0:T(8,128)(2,1)S(1)}, u32[]{:S(2)}, u32[]{:S(2)}) collective-permute-start(bf16[384,1152]{1,0:T(8,128)(2,1)S(1)} %collective-permute-done.1.refs_6_.refs_2_), channel_id=1, source_target_pairs={{0,1},{1,0},{2,3},{3,2},{4,5},{5,4},{6,7},{7,6},{8,9},{9,8},{10,11... | collective-permute-start | bytes 2654216 | tf_op jit(solution)/shard_map/ppermute | solution.py:278
  49.0 1.3 %collective-permute-start.7 = (bf16[128,1536]{1,0:T(8,128)(2,1)S(1)}, bf16[128,1536]{1,0:T(8,128)(2,1)S(1)}, u32[]{:S(2)}, u32[]{:S(2)}) collective-permute-start(bf16[128,1536]{1,0:T(8,128)(2,1)S(1)} %copy-done.3), channel_id=1, source_target_pairs={{4,8},{8,4},{5,9},{9,5},{6,10},{10,6},{7,11},{11,7},{20,24},{24,20... | collective-permute-start | bytes 1179656 | tf_op jit(solution)/shard_map/ppermute | solution.py:298
  49.7 34.0 %collective-permute-start.3 = (bf16[384,1152]{1,0:T(8,128)(2,1)}, bf16[384,1152]{1,0:T(8,128)(2,1)S(1)}, u32[]{:S(2)}, u32[]{:S(2)}) collective-permute-start(bf16[384,1152]{1,0:T(8,128)(2,1)} %get-tuple-element.17.refs_4_), channel_id=1, source_target_pairs={{0,1},{1,0},{2,3},{3,2},{4,5},{5,4},{6,7},{7,6},{8,9},{9,8},{10,11... | collective-permute-start | bytes 2654216 | tf_op jit(solution)/shard_map/ppermute | solution.py:277
  49.8 46.7 %collective-permute-start.5 = (bf16[384,1152]{1,0:T(8,128)(2,1)S(1)}, bf16[384,1152]{1,0:T(8,128)(2,1)S(1)}, u32[]{:S(2)}, u32[]{:S(2)}) collective-permute-start(bf16[384,1152]{1,0:T(8,128)(2,1)S(1)} %collective-permute-done.4.refs_6_), channel_id=1, source_target_pairs={{0,1},{1,0},{2,3},{3,2},{4,5},{5,4},{6,7},{7,6},{8,9},{9,8},{10,11... | collective-permute-start | bytes 2654216 | tf_op jit(solution)/shard_map/ppermute | solution.py:278
  50.2 19.6 %collective-permute-start.8 = (bf16[128,1536]{1,0:T(8,128)(2,1)S(1)}, bf16[128,1536]{1,0:T(8,128)(2,1)S(1)}, u32[]{:S(2)}, u32[]{:S(2)}) collective-permute-start(bf16[128,1536]{1,0:T(8,128)(2,1)S(1)} %copy-done.3), channel_id=1, source_target_pairs={{0,8},{12,4},{1,9},{13,5},{2,10},{14,6},{3,11},{15,7},{16,24},{28,... | collective-permute-start | bytes 1179656 | tf_op jit(solution)/shard_map/ppermute | solution.py:297
  64.6 31.9 %copy-start.5 = (f32[1,1536]{1,0:T(1,128)S(1)}, f32[1,1536]{1,0:T(1,128)}, u32[]{:S(2)}) copy-start(f32[1,1536]{1,0:T(1,128)} %broadcast_in_dim.12.gain_ref.refs_13_) | copy-start | bytes 18436
  64.6 31.8 %copy-start.1 = (bf16[1,128,1536]{2,1,0:T(8,128)(2,1)S(1)}, bf16[1,128,1536]{2,1,0:T(8,128)(2,1)}, u32[]{:S(2)}) copy-start(bf16[1,128,1536]{2,1,0:T(8,128)(2,1)} %refs_12_.1) | copy-start | bytes 1179652
  64.7 31.8 %copy-start.2 = (bf16[384,1152]{1,0:T(8,128)(2,1)S(1)}, bf16[384,1152]{1,0:T(8,128)(2,1)}, u32[]{:S(2)}) copy-start(bf16[384,1152]{1,0:T(8,128)(2,1)} %get-tuple-element.17.refs_4_) | copy-start | bytes 2654212
  69.9 0.9 copy-start.4
  80.4 11.8 %collective-permute-start.12 = (bf16[128,1152]{1,0:T(8,128)(2,1)S(1)}, bf16[128,1152]{1,0:T(8,128)(2,1)S(1)}, u32[]{:S(2)}, u32[]{:S(2)}) collective-permute-start(bf16[128,1152]{1,0:T(8,128)(2,1)S(1)} %get-tuple-element.22), channel_id=1, source_target_pairs={{4,0},{8,12},{5,1},{9,13},{6,2},{10,14},{7,3},{11,15},{20,16},{24,... | collective-permute-start | bytes 884744 | tf_op jit(solution)/shard_map/ppermute | solution.py:316
  81.7 10.5 %collective-permute-start.13 = (bf16[128,1152]{1,0:T(8,128)(2,1)S(1)}, bf16[128,1152]{1,0:T(8,128)(2,1)S(1)}, u32[]{:S(2)}, u32[]{:S(2)}) collective-permute-start(bf16[128,1152]{1,0:T(8,128)(2,1)S(1)} %get-tuple-element.23), channel_id=1, source_target_pairs={{4,8},{8,4},{5,9},{9,5},{6,10},{10,6},{7,11},{11,7},{20,24},{24,20... | collective-permute-start | bytes 884744 | tf_op jit(solution)/shard_map/ppermute | solution.py:315
  82.3 14.1 %collective-permute-start.14 = (bf16[128,1152]{1,0:T(8,128)(2,1)S(1)}, bf16[128,1152]{1,0:T(8,128)(2,1)S(1)}, u32[]{:S(2)}, u32[]{:S(2)}) collective-permute-start(bf16[128,1152]{1,0:T(8,128)(2,1)S(1)} %get-tuple-element.24), channel_id=1, source_target_pairs={{4,12},{8,0},{5,13},{9,1},{6,14},{10,2},{7,15},{11,3},{20,28},{24,... | collective-permute-start | bytes 884744 | tf_op jit(solution)/shard_map/ppermute | solution.py:314

commit v2 on v0

--- a/solution.py
+++ b/solution.py
@@ -1,14 +1,441 @@
+import functools
 import math
 
 import jax
 import jax.numpy as jnp
 from jax import lax
+from jax.experimental import pallas as pl
+from jax.experimental.pallas import tpu as pltpu
 from jax.sharding import PartitionSpec as P
 
 HEADS = 12
 HEAD_DIM = 64
 QBLOCK = 128
 HD = 768
+HALF = HD // 2
+EPSILON = 1e-06
+VMEM = pltpu.VMEM
+SMEM = pltpu.SMEM
+
+
+def half_index():
+    return lax.axis_index("seq") * 2 // lax.axis_size("seq")
+
+
+def cost(micros):
+    return pl.CostEstimate(flops=int(micros * 1.0e9), bytes_accessed=int(micros * 3.0e6), transcendentals=0)
+
+
+def spec(memory_space=VMEM):
+    return pl.BlockSpec(memory_space=memory_space)
+
+
+def norm_rows(rows):
+    mean_value = jnp.mean(rows, axis=-1, keepdims=True)
+    centered = rows - mean_value
+    variance = jnp.mean(centered * centered, axis=-1, keepdims=True)
+    inverse = lax.rsqrt(variance + EPSILON)
+    return centered * inverse, inverse
+
+
+def row_vector(ref):
+    return ref[...].reshape(1, ref.shape[0])
+
+
+def scale_block(codes, scale):
+    return (codes.astype(jnp.float32) * scale).astype(jnp.bfloat16)
+
+
+def first_kernel(
+    tokens_ref, gain_ref, shift_ref, scales_ref, codes_ref, grad_ref, layer_ref, out_scales_ref, out_codes_ref,
+    weight_out, near_out, far_out,
+    tokens, gain, shift, scales, codes, grad, layer, out_scales, out_codes, scaled, weight, sems
+):
+    half = half_index()
+    other = 1 - half
+    blocks = HALF // QBLOCK
+
+    def copy(source, target, at):
+        started = pltpu.make_async_copy(source, target, sems.at[at])
+        started.start()
+        return started
+
+    def columns(part):
+        return codes_ref.at[:, pl.ds(pl.multiple_of(part * HD + half * HALF, QBLOCK), HALF)]
+
+    def rows(which):
+        return out_codes_ref.at[pl.ds(pl.multiple_of(which * HALF, QBLOCK), HALF), :]
+
+    scales_copy = copy(scales_ref, scales, 0)
+    codes_copies = [copy(columns(part), codes.at[part], 1 + part) for part in range(3)]
+    tokens_copies = [
+        copy(tokens_ref, tokens, 4), copy(gain_ref, gain, 5), copy(shift_ref, shift, 6)
+    ]
+    grad_copies = [
+        copy(grad_ref, grad, 7), copy(layer_ref, layer, 8), copy(out_scales_ref, out_scales, 9)
+    ]
+    out_copies = [copy(rows(other), out_codes.at[0], 10), copy(rows(half), out_codes.at[1], 11)]
+
+    scales_copy.wait()
+    for part in range(3):
+        codes_copies[part].wait()
+        for r in range(codes_ref.shape[0] // QBLOCK):
+            for c in range(blocks):
+                scale = scales[r, (part * HD) // QBLOCK + half * blocks + c]
+                lines = slice(r * QBLOCK, (r + 1) * QBLOCK)
+                weight_out[lines, part * HALF + c * QBLOCK : part * HALF + (c + 1) * QBLOCK] = scale_block(
+                    codes[part, lines, c * QBLOCK : (c + 1) * QBLOCK], scale
+                )
+
+    for started in tokens_copies:
+        started.wait()
+    width = tokens.shape[2]
+    gain_row = row_vector(gain)
+    shift_row = row_vector(shift)
+    for r in range(0, tokens.shape[1], 16):
+        normed, _ = norm_rows(tokens[0, r : r + 16, :].astype(jnp.float32))
+        norm_out = (normed * gain_row + shift_row).astype(jnp.bfloat16)
+        near_out[r : r + 16, :width] = norm_out
+        far_out[r : r + 16, :width] = norm_out
+
+    for started in grad_copies:
+        started.wait()
+    scaled[...] = (grad[0].astype(jnp.float32) * row_vector(layer)).astype(jnp.bfloat16)
+    for i, (out_ref, which) in enumerate(((far_out, other), (near_out, half))):
+        out_copies[i].wait()
+        for r in range(blocks):
+            lines = slice(r * QBLOCK, (r + 1) * QBLOCK)
+            for c in range(width // QBLOCK):
+                at = slice(c * QBLOCK, (c + 1) * QBLOCK)
+                weight[lines, at] = scale_block(out_codes[i, lines, at], out_scales[which * blocks + r, c])
+        out_ref[:, width:] = dot_last(scaled[...], weight[...]).astype(jnp.bfloat16)
+
+
+def first_step(tokens, gain, shift, scales, codes, grad, layer_scale, out_scales, out_codes):
+    lines, width = tokens.shape[1:]
+    depth = codes.shape[0]
+    both = jax.ShapeDtypeStruct((lines, width + HALF), jnp.bfloat16)
+    return pl.pallas_call(
+        first_kernel,
+        out_shape=(jax.ShapeDtypeStruct((depth, 3 * HALF), jnp.bfloat16), both, both),
+        in_specs=[spec(pltpu.HBM)] * 9,
+        out_specs=(spec(),) * 3,
+        scratch_shapes=[
+            VMEM(tokens.shape, tokens.dtype),
+            VMEM(gain.shape, gain.dtype),
+            VMEM(shift.shape, shift.dtype),
+            SMEM(scales.shape, scales.dtype),
+            VMEM((3, depth, HALF), codes.dtype),
+            VMEM(grad.shape, grad.dtype),
+            VMEM(layer_scale.shape, layer_scale.dtype),
+            SMEM(out_scales.shape, out_scales.dtype),
+            VMEM((2, HALF, width), out_codes.dtype),
+            VMEM((lines, width), jnp.bfloat16),
+            VMEM((HALF, width), jnp.bfloat16),
+            pltpu.SemaphoreType.DMA((12,)),
+        ],
+        compiler_params=pltpu.CompilerParams(vmem_limit_bytes=60 * 2**20),
+        cost_estimate=cost(3),
+        name="first_weights_and_rows",
+    )(tokens, gain, shift, scales, codes, grad, layer_scale, out_scales, out_codes)
+
+
+def far_kernel(scales_ref, codes_ref, after_ref, weight_out, scales, codes, sems):
+    other = 1 - half_index()
+    blocks = HALF // QBLOCK
+    copies = [pltpu.make_async_copy(scales_ref, scales, sems.at[3])]
+    for part in range(3):
+        at = pl.ds(pl.multiple_of(part * HD + other * HALF, QBLOCK), HALF)
+        copies.append(pltpu.make_async_copy(codes_ref.at[:, at], codes.at[part], sems.at[part]))
+    for started in copies:
+        started.start()
+    for started in copies:
+        started.wait()
+    for part in range(3):
+        for r in range(codes_ref.shape[0] // QBLOCK):
+            for c in range(blocks):
+                scale = scales[r, (part * HD) // QBLOCK + other * blocks + c]
+                lines = slice(r * QBLOCK, (r + 1) * QBLOCK)
+                weight_out[lines, part * HALF + c * QBLOCK : part * HALF + (c + 1) * QBLOCK] = scale_block(
+                    codes[part, lines, c * QBLOCK : (c + 1) * QBLOCK], scale
+                )
+
+
+def far_step(scales, codes, after):
+    depth = codes.shape[0]
+    return pl.pallas_call(
+        far_kernel,
+        out_shape=jax.ShapeDtypeStruct((depth, 3 * HALF), jnp.bfloat16),
+        in_specs=[spec(pltpu.HBM), spec(pltpu.HBM), spec()],
+        out_specs=spec(),
+        scratch_shapes=[
+            SMEM(scales.shape, scales.dtype),
+            VMEM((3, depth, HALF), codes.dtype),
+            pltpu.SemaphoreType.DMA((4,)),
+        ],
+        compiler_params=pltpu.CompilerParams(vmem_limit_bytes=16 * 2**20),
+        cost_estimate=cost(0.01),
+        name="far_weight",
+    )(scales, codes, after)
+
+
+def dot_last(a, b):
+    return lax.dot_general(a, b, (((1,), (1,)), ((), ())), preferred_element_type=jnp.float32)
+
+
+def dot_plain(a, b):
+    return jnp.dot(a, b, preferred_element_type=jnp.float32)
+
+
+def norm_columns(norms, picks, depth):
+    mine = lax.axis_index("weight")
+    return jnp.concatenate(
+        [
+            jnp.concatenate(
+                [norm_ref[:, pl.ds(pl.multiple_of((mine ^ j) * depth, QBLOCK), depth)] for j in picks],
+                axis=1,
+            )
+            for norm_ref in norms
+        ],
+        axis=0,
+    )
+
+
+def project_kernel(*refs):
+    norms, weights, sums = refs[0:4], refs[4:7], refs[7]
+    rows = norm_columns(norms, range(3), weights[0].shape[0])
+    for part in range(3):
+        columns = jnp.concatenate([w[:, part * HALF : (part + 1) * HALF] for w in weights], axis=0)
+        sums[:, part * HALF : (part + 1) * HALF] = dot_plain(rows, columns)
+
+
+def project_step(norms, weights):
+    tokens = norms[0].shape[0]
+    return pl.pallas_call(
+        project_kernel,
+        out_shape=jax.ShapeDtypeStruct((tokens * len(norms), 3 * HALF), jnp.float32),
+        in_specs=[spec()] * 7,
+        out_specs=spec(),
+        compiler_params=pltpu.CompilerParams(vmem_limit_bytes=24 * 2**20),
+        cost_estimate=cost(6),
+        name="projection_part",
+    )(*norms, *weights)
+
+
+def finish_kernel(*refs):
+    norms = refs[0:4]
+    weight, sums, bias_ref, proj = refs[4:]
+    half = half_index()
+    rows = norm_columns(norms, (3,), weight.shape[0])
+    bias = row_vector(bias_ref)
+    for part in range(3):
+        at = slice(part * HALF, (part + 1) * HALF)
+        shift = jnp.where(
+            half == 0,
+            bias[:, part * HD : part * HD + HALF],
+            bias[:, part * HD + HALF : (part + 1) * HD],
+        )
+        value = (sums[:, at] + dot_plain(rows, weight[:, at]) + shift).astype(jnp.bfloat16)
+        if part == 0:
+            value = value * jnp.bfloat16(HEAD_DIM**-0.5)
+        proj[:, at] = value
+
+
+def finish_step(norms, weight, sums, bias):
+    return pl.pallas_call(
+        finish_kernel,
+        out_shape=jax.ShapeDtypeStruct(sums.shape, jnp.bfloat16),
+        in_specs=[spec()] * 7,
+        out_specs=spec(),
+        compiler_params=pltpu.CompilerParams(vmem_limit_bytes=24 * 2**20),
+        cost_estimate=cost(0.01),
+        name="projection",
+    )(*norms, weight, sums, bias)
+
+
+PAIR = 2 * HEAD_DIM
+
+
+def attention_kernel(pairs, *refs):
+    proj, grads, outs = refs[0], refs[1:5], refs[-4:]
+    total = proj.shape[0]
+    tokens = grads[0].shape[0]
+    low = lax.broadcasted_iota(jnp.int32, (total, PAIR), 1) < HEAD_DIM
+    zero = jnp.zeros((total, PAIR), jnp.bfloat16)
+    for place, t in enumerate(pairs):
+        query = proj[:, t * PAIR : (t + 1) * PAIR]
+        key = proj[:, HALF + t * PAIR : HALF + (t + 1) * PAIR]
+        value = proj[:, 2 * HALF + t * PAIR : 2 * HALF + (t + 1) * PAIR]
+        grad = jnp.concatenate(
+            [g[:, g.shape[1] - HALF + t * PAIR : g.shape[1] - HALF + (t + 1) * PAIR] for g in grads], axis=0
+        )
+        key_t = key.T
+        key_grad = value_grad = None
+        query_grad = []
+        for side in range(2):
+            mask = low if side == 0 else ~low
+            scores = dot_last(jnp.where(mask, key, zero), query)
+            dprob = dot_last(jnp.where(mask, value, zero), grad)
+            expo = jnp.exp(scores - jnp.max(scores, axis=0, keepdims=True))
+            scale = 1.0 / jnp.sum(expo, axis=0, keepdims=True)
+            delta = jnp.sum(expo * dprob, axis=0, keepdims=True) * scale
+            prob = expo * scale
+            dscore = (prob * (dprob - delta)).astype(jnp.bfloat16)
+            key_part = dot_plain(dscore, jnp.where(mask, query, zero))
+            value_part = dot_plain(prob.astype(jnp.bfloat16), jnp.where(mask, grad, zero))
+            key_grad = key_part if side == 0 else key_grad + key_part
+            value_grad = value_part if side == 0 else value_grad + value_part
+            query_grad.append(dot_plain(key_t[side * HEAD_DIM : (side + 1) * HEAD_DIM], dscore))
+        query_grad = jnp.concatenate(query_grad, axis=0).T * HEAD_DIM**-0.5
+        for part, piece in enumerate((query_grad, key_grad, value_grad)):
+            piece = piece.astype(jnp.bfloat16)
+            first = (part * len(pairs) + place) * PAIR
+            for i, out in enumerate(outs):
+                out[:, first : first + PAIR] = piece[i * tokens : (i + 1) * tokens]
+
+
+def attention_step(proj, grads, pairs, *after):
+    tokens = grads[0].shape[0]
+    out = jax.ShapeDtypeStruct((tokens, 3 * len(pairs) * PAIR), jnp.bfloat16)
+    return pl.pallas_call(
+        functools.partial(attention_kernel, pairs),
+        out_shape=(out,) * 4,
+        in_specs=[spec()] * 5 + [spec()] * len(after),
+        out_specs=(spec(),) * 4,
+        compiler_params=pltpu.CompilerParams(vmem_limit_bytes=24 * 2**20),
+        cost_estimate=cost(12),
+        name="attention",
+    )(proj, *grads, *after)
+
+
+def pick_grads(own_ref, back_ref, cross_ref, skip_ref):
+    place = lax.axis_index("seq")
+    middle = (place == 1) | (place == 2)
+    return (
+        jnp.where(middle, own_ref[...], back_ref[...]),
+        jnp.where(middle, cross_ref[...], skip_ref[...]),
+    )
+
+
+def part_kernel(*refs):
+    near_w, far_w, sums = refs[0:4], refs[4:7], refs[-1]
+    near, far = pick_grads(*refs[7:11])
+    mine = lax.axis_index("weight")
+    depth = near_w[0].shape[0]
+    for j in range(4):
+        value = dot_last(near, near_w[j][...])
+        if j < len(far_w):
+            value += dot_last(far, far_w[j][...])
+        sums[:, pl.ds(pl.multiple_of((mine ^ j) * depth, QBLOCK), depth)] = value
+
+
+def part_step(near_w, far_w, pieces):
+    rows = pieces[0].shape[0]
+    return pl.pallas_call(
+        part_kernel,
+        out_shape=jax.ShapeDtypeStruct((rows, 4 * near_w[0].shape[0]), jnp.float32),
+        in_specs=[spec()] * 11,
+        out_specs=spec(),
+        compiler_params=pltpu.CompilerParams(vmem_limit_bytes=24 * 2**20),
+        cost_estimate=cost(6),
+        name="grad_norm_part",
+    )(*near_w, *far_w, *pieces)
+
+
+def last_kernel(far_w, *refs):
+    sums, tokens_ref, gain_ref, out_ref, grad_norm = refs[4:]
+    _, far = pick_grads(*refs[0:4])
+    depth = far_w.shape[0]
+    at = pl.ds(pl.multiple_of((lax.axis_index("weight") ^ 3) * depth, QBLOCK), depth)
+    grad_norm[...] = sums[...]
+    grad_norm[:, at] += dot_last(far, far_w[...])
+    gain = row_vector(gain_ref)
+    for r in range(0, tokens_ref.shape[1], 16):
+        normed, inverse = norm_rows(tokens_ref[0, r : r + 16, :].astype(jnp.float32))
+        grad_hat = grad_norm[r : r + 16, :] * gain
+        first_mean = jnp.mean(grad_hat, axis=-1, keepdims=True)
+        second_mean = jnp.mean(grad_hat * normed, axis=-1, keepdims=True)
+        out_ref[0, r : r + 16, :] = inverse * (grad_hat - first_mean - normed * second_mean)
+
+
+def last_step(far_w, pieces, sums, tokens, gain):
+    return pl.pallas_call(
+        last_kernel,
+        out_shape=jax.ShapeDtypeStruct(tokens.shape, jnp.float32),
+        in_specs=[spec()] * 8,
+        out_specs=spec(),
+        scratch_shapes=[VMEM(tokens.shape[1:], jnp.float32)],
+        compiler_params=pltpu.CompilerParams(vmem_limit_bytes=24 * 2**20),
+        cost_estimate=cost(2),
+        name="input_grad",
+    )(far_w, *pieces, sums, tokens, gain)
+
+
+def pass_kernel(value_ref, *refs):
+    refs[-1][...] = value_ref[...]
+
+
+def pass_after(value, *after):
+    return pl.pallas_call(
+        pass_kernel,
+        out_shape=jax.ShapeDtypeStruct(value.shape, value.dtype),
+        in_specs=[spec()] * (1 + len(after)),
+        out_specs=spec(),
+        input_output_aliases={0: 0},
+        compiler_params=pltpu.CompilerParams(vmem_limit_bytes=16 * 2**20),
+        cost_estimate=cost(0.01),
+        name="pass_after",
+    )(value, *after)
+
+
+END_TO_MIDDLE = [(0, 1), (3, 2)]
+MIDDLE = [(1, 2), (2, 1)]
+END_TO_FAR = [(0, 2), (3, 1)]
+MIDDLE_TO_END = [(1, 0), (2, 3)]
+FAR_TO_END = [(1, 3), (2, 0)]
+
+
+def flip(bit):
+    return [(i, i ^ bit) for i in range(4)]
+
+
+def local_middle(
+    tokens,
+    upstream_grad,
+    norm_gain,
+    norm_bias,
+    input_codes,
+    input_scales,
+    input_bias,
+    output_codes,
+    output_scales,
+    layer_scale,
+):
+    near, both_near, both_other = first_step(
+        tokens, norm_gain, norm_bias, input_scales, input_codes, upstream_grad, layer_scale, output_scales, output_codes
+    )
+    both_mid = lax.ppermute(both_other, "seq", MIDDLE)
+    both_far = lax.ppermute(both_other, "seq", END_TO_FAR)
+    both_end = lax.ppermute(both_near, "seq", END_TO_MIDDLE)
+    near_across = lax.ppermute(near, "weight", flip(2))
+    near_beside = lax.ppermute(near, "weight", flip(1))
+    near_diagonal = lax.ppermute(near_across, "weight", flip(1))
+    far = far_step(input_scales, input_codes, near_across)
+    far_across = lax.ppermute(far, "weight", flip(2))
+    far_beside = lax.ppermute(far, "weight", flip(1))
+    rows = (both_near, both_end, both_mid, both_far)
+    sums = project_step(rows, (near, near_beside, near_across))
+    proj = finish_step(rows, near_diagonal, sums, input_bias)
+    own, end, mid, skip = attention_step(proj, rows, (0, 1, 2))
+    skip = lax.ppermute(skip, "seq", FAR_TO_END)
+    cross = lax.ppermute(mid, "seq", MIDDLE)
+    back = lax.ppermute(end, "seq", MIDDLE_TO_END)
+    pieces = (own, back, cross, skip)
+    far_across = pass_after(far_across, cross, skip, back)
+    far_diagonal = lax.ppermute(far_across, "weight", flip(1))
+    near_w = (near, near_beside, near_across, near_diagonal)
+    sums = part_step(near_w, (far, far_beside, far_across), pieces)
+    return last_step(far_diagonal, pieces, sums, tokens, norm_gain)
 
 
 def dequantize(codes, scales):
@@ -174,4 +601,6 @@
         P(),
     )
     out_specs = P(("groups", "weight"), "seq", None)
-    return jax.shard_map(local, mesh=mesh, in_specs=in_specs, out_specs=out_specs, check_vma=False)
+    fits = mesh.shape["seq"] == 4 and mesh.shape["weight"] == 4
+    plan = local_middle if fits else local
+    return jax.shard_map(plan, mesh=mesh, in_specs=in_specs, out_specs=out_specs, check_vma=False)

time: 168 us -> 70.3 us (0.42)
  waiting for transfers between devices: 113 us -> 35.1 us
  Pallas kernels: 0 us -> 18.2 us
  starting transfers between devices: 0.09 us -> 16.5 us
  local copies, waits for them, and re-layouts: 15.2 us -> 0.04 us
  between operations: 13.4 us -> 0.19 us
  matrix products: 11.1 us -> 0 us
  other arithmetic: 8.71 us -> 0 us
  blocking collectives: 6.11 us -> 0 us
    all_gather x2 -> x0, waiting for transfers between devices: 79 us -> none  [the longest x1 46.7 us: local(): lax.all_gather(input_codes.astype(jnp.float32), 'weight', axis=0, tiled=T...]
    ppermute x0 -> x12, waiting for transfers between devices: none -> 35.1 us  [the longest x1 13.1 us: local_middle(): skip = lax.ppermute(skip, 'seq', FAR_TO_END)]
    unnamed x4 -> x0, waiting for transfers between devices: 33.7 us -> none
    pallas_call x0 -> x8, Pallas kernels: none -> 18.2 us  [the longest x1 6.49 us: attention_step(): pl.pallas_call(functools.partial(attention_kernel, pairs), out_shape=(out...]
    ppermute x0 -> x12, starting transfers between devices: none -> 16.5 us  [the longest x1 3.97 us: local_middle(): both_far = lax.ppermute(both_other, 'seq', END_TO_FAR)]
    unnamed x31 -> x14, local copies, waits for them, and re-layouts: 12.1 us -> 0.04 us
    dot_general x8 -> x0, matrix products: 11.1 us -> none  [the longest x1 4.29 us: local(): jnp.dot(grad_proj, input_weight.T, preferred_element_type=jnp.float32)]
    all_gather x1 -> x0, blocking collectives: 6.11 us -> none  [local(): lax.all_gather(input_scales, 'weight', axis=0, tiled=True)]
  transfers between devices with their start and end apart: 3 -> 12, of which waited for: 3 -> 6; matrix products, arithmetic and copies ran while one was open for 3% -> 0% of each run, Pallas kernels for 0% -> 18%
where the time goes in v2:
time: 70.3 us; the launch traced here: 70.1 us
  waiting for transfers between devices  35.1 us (50%)
  Pallas kernels  18.2 us (26%)
  starting transfers between devices  16.5 us (23%)
    ppermute x1, waiting for transfers between devices, local_middle(): skip = lax.ppermute(skip, 'seq', FAR_TO_END)  13.1 us
    ppermute x1, waiting for transfers between devices, local_middle(): near_across = lax.ppermute(near, 'weight', flip(2))  11.7 us
    pallas_call x1, Pallas kernels, attention_step(): pl.pallas_call(functools.partial(attention_kernel, pairs), out_shape=(out...  6.49 us
    ppermute x1, waiting for transfers between devices, local_middle(): far_across = lax.ppermute(far, 'weight', flip(2))  4.45 us
    pallas_call x1, Pallas kernels, first_step(): pl.pallas_call(first_kernel, out_shape=(jax.ShapeDtypeStruct((depth, 3 *...  4.22 us
    ppermute x1, starting transfers between devices, local_middle(): both_far = lax.ppermute(both_other, 'seq', END_TO_FAR)  3.97 us
    ppermute x1, starting transfers between devices, local_middle(): both_end = lax.ppermute(both_near, 'seq', END_TO_MIDDLE)  3.5 us
    ppermute x1, starting transfers between devices, local_middle(): near_across = lax.ppermute(near, 'weight', flip(2))  3.01 us
  transfers between devices with their start and end apart: 12, of which 6 were waited for; matrix products, arithmetic and copies ran while one was open for 0% of the time, Pallas kernels for 18%

profile of v2, /device:TPU:0, one launch (start us, length us, event | category | flops | bytes accessed | tf_op | source)
XLA Modules:
  0.0 70.1 jit_solution(12651147609484914040)
XLA Ops:
  0.0 4.2 %first_weights_and_rows.1 = (bf16[384,1152]{1,0:T(8,128)(2,1)}, bf16[128,1920]{1,0:T(8,128)(2,1)}, bf16[128,1920]{1,0:T(8,128)(2,1)}) custom-call(bf16[1,128,1536]{2,1,0:T(8,128)(2,1)} %refs_5_.1, f32[1536]{0:T(1024)} %refs_6_.3, f32[1536]{0:T(1024)} %shift_ref.1, f32[3,18]{1,0:T(4,128)} %scales_ref.3, bf16[384,2304]{1,0:T(8,128)(2,1)} %codes_ref.3, ...), custom_call_target="tpu_custom_call" | custom-call | flops 3000000000 | bytes 9000000 | tf_op jit(solution)/shard_map/first_weights_and_rows/pallas_call | solution.py:118
  4.2 0.0 copy-start.1
  4.3 3.0 %collective-permute-start = (bf16[384,1152]{1,0:T(8,128)(2,1)}, bf16[384,1152]{1,0:T(8,128)(2,1)S(1)}, u32[]{:S(2)}, u32[]{:S(2)}) collective-permute-start(bf16[384,1152]{1,0:T(8,128)(2,1)} %get-tuple-element.12.refs_4_.refs_0_), channel_id=1, source_target_pairs={{0,2},{1,3},{2,0},{3,1},{4,6},{5,7},{6,4},{7,5},{8,10},{9,11},{10,... | collective-permute-start | bytes 2654216 | tf_op jit(solution)/shard_map/ppermute | solution.py:420
  7.3 3.5 %collective-permute-start.2 = (bf16[128,1920]{1,0:T(8,128)(2,1)}, bf16[128,1920]{1,0:T(8,128)(2,1)S(1)}, u32[]{:S(2)}, u32[]{:S(2)}) collective-permute-start(bf16[128,1920]{1,0:T(8,128)(2,1)} %get-tuple-element.13.refs_0_.refs_1_), channel_id=1, source_target_pairs={{0,4},{12,8},{1,5},{13,9},{2,6},{14,10},{3,7},{15,11},{16,20},{28,... | collective-permute-start | bytes 1474568 | tf_op jit(solution)/shard_map/ppermute | solution.py:419
  10.8 0.7 collective-permute-start.3
  11.5 4.0 %collective-permute-start.4 = (bf16[128,1920]{1,0:T(8,128)(2,1)}, bf16[128,1920]{1,0:T(8,128)(2,1)S(1)}, u32[]{:S(2)}, u32[]{:S(2)}) collective-permute-start(bf16[128,1920]{1,0:T(8,128)(2,1)} %get-tuple-element.14), channel_id=1, source_target_pairs={{0,8},{12,4},{1,9},{13,5},{2,10},{14,6},{3,11},{15,7},{16,24},{28,... | collective-permute-start | bytes 1474568 | tf_op jit(solution)/shard_map/ppermute | solution.py:418
  15.5 11.7 %collective-permute-done.after_ref.refs_6_.refs_2_ = bf16[384,1152]{1,0:T(8,128)(2,1)S(1)} collective-permute-done((bf16[384,1152]{1,0:T(8,128)(2,1)}, bf16[384,1152]{1,0:T(8,128)(2,1)S(1)}, u32[]{:S(2)}, u32[]{:S(2)}) %collective-permute-start) | collective-permute-done | bytes 884768 | tf_op jit(solution)/shard_map/ppermute | solution.py:420
  27.1 0.0 collective-permute-start.5
  27.1 0.8 %far_weight.1.refs_4_ = bf16[384,1152]{1,0:T(8,128)(2,1)S(1)} custom-call(f32[3,18]{1,0:T(4,128)S(1)} %copy-done.3, bf16[384,2304]{1,0:T(8,128)(2,1)S(1)} %copy-done, bf16[384,1152]{1,0:T(8,128)(2,1)S(1)} %collective-permute-done.after_ref.refs_6_.refs_2_), custom_call_target="tpu_custom_call" | custom-call | flops 10000000 | bytes 30000 | tf_op jit(solution)/shard_map/far_weight/pallas_call | solution.py:166
  27.9 0.0 copy-start.2
  27.9 0.0 collective-permute-done.2.refs_1_.refs_2_
  27.9 1.8 %collective-permute-start.1 = (bf16[384,1152]{1,0:T(8,128)(2,1)S(1)}, bf16[384,1152]{1,0:T(8,128)(2,1)S(1)}, u32[]{:S(2)}, u32[]{:S(2)}) collective-permute-start(bf16[384,1152]{1,0:T(8,128)(2,1)S(1)} %far_weight.1.refs_4_), channel_id=1, source_target_pairs={{0,2},{1,3},{2,0},{3,1},{4,6},{5,7},{6,4},{7,5},{8,10},{9,11},{10,... | collective-permute-start | bytes 2654216 | tf_op jit(solution)/shard_map/ppermute | solution.py:424
  29.7 0.0 collective-permute-done.3.refs_2_.refs_3_
  29.8 0.2 collective-permute-start.11
  30.0 2.8 %collective-permute-done.4.refs_3_.refs_4_ = bf16[128,1920]{1,0:T(8,128)(2,1)S(1)} collective-permute-done((bf16[128,1920]{1,0:T(8,128)(2,1)}, bf16[128,1920]{1,0:T(8,128)(2,1)S(1)}, u32[]{:S(2)}, u32[]{:S(2)}) %collective-permute-start.4) | collective-permute-done | bytes 491552 | tf_op jit(solution)/shard_map/ppermute | solution.py:418
  32.8 2.1 %projection_part.1.refs_5_ = f32[512,1152]{1,0:T(8,128)S(1)} custom-call(bf16[128,1920]{1,0:T(8,128)(2,1)S(1)} %copy-done.1, bf16[128,1920]{1,0:T(8,128)(2,1)S(1)} %collective-permute-done.2.refs_1_.refs_2_, bf16[128,1920]{1,0:T(8,128)(2,1)S(1)} %collective-permute-done.3.refs_2_.refs_3_, bf16[128,1920]{1,0:T(8,128)(2,1)S(1)} %collective-permute-done.4.refs_3_.refs_4_, ...), custom_call_target="tpu_custom_call" | custom-call | flops 6000000000 | bytes 18000000 | tf_op jit(solution)/shard_map/projection_part/pallas_call | solution.py:214
  34.9 0.9 %projection.1.refs_0_ = bf16[512,1152]{1,0:T(8,128)(2,1)S(1)} custom-call(bf16[128,1920]{1,0:T(8,128)(2,1)S(1)} %copy-done.1, bf16[128,1920]{1,0:T(8,128)(2,1)S(1)} %collective-permute-done.2.refs_1_.refs_2_, bf16[128,1920]{1,0:T(8,128)(2,1)S(1)} %collective-permute-done.3.refs_2_.refs_3_, bf16[128,1920]{1,0:T(8,128)(2,1)S(1)} %collective-permute-done.4.refs_3_.refs_4_, ...), custom_call_target="tpu_custom_call" | custom-call | flops 10000000 | bytes 30000 | tf_op jit(solution)/shard_map/projection/pallas_call | solution.py:245
  35.8 6.5 %attention.1 = (bf16[128,1152]{1,0:T(8,128)(2,1)S(1)}, bf16[128,1152]{1,0:T(8,128)(2,1)S(1)}, bf16[128,1152]{1,0:T(8,128)(2,1)S(1)}, bf16[128,1152]{1,0:T(8,128)(2,1)S(1)}) custom-call(bf16[512,1152]{1,0:T(8,128)(2,1)S(1)} %projection.1.refs_0_, bf16[128,1920]{1,0:T(8,128)(2,1)S(1)} %copy-done.1, ...), custom_call_target="tpu_custom_call" | custom-call | flops 12000000000 | bytes 36000000 | tf_op jit(solution)/shard_map/attention/pallas_call | solution.py:300
  42.3 0.7 collective-permute-start.7
  43.0 1.3 %collective-permute-start.8 = (bf16[128,1152]{1,0:T(8,128)(2,1)S(1)}, bf16[128,1152]{1,0:T(8,128)(2,1)S(1)}, u32[]{:S(2)}, u32[]{:S(2)}) collective-permute-start(bf16[128,1152]{1,0:T(8,128)(2,1)S(1)} %get-tuple-element.16), channel_id=1, source_target_pairs={{4,12},{8,0},{5,13},{9,1},{6,14},{10,2},{7,15},{11,3},{20,28},{24,... | collective-permute-start | bytes 884744 | tf_op jit(solution)/shard_map/ppermute | solution.py:430
  44.3 1.3 %collective-permute-start.9 = (bf16[128,1152]{1,0:T(8,128)(2,1)S(1)}, bf16[128,1152]{1,0:T(8,128)(2,1)S(1)}, u32[]{:S(2)}, u32[]{:S(2)}) collective-permute-start(bf16[128,1152]{1,0:T(8,128)(2,1)S(1)} %get-tuple-element.17), channel_id=1, source_target_pairs={{4,0},{8,12},{5,1},{9,13},{6,2},{10,14},{7,3},{11,15},{20,16},{24,... | collective-permute-start | bytes 884744 | tf_op jit(solution)/shard_map/ppermute | solution.py:432
  45.6 4.5 %collective-permute-done.1.value_ref = bf16[384,1152]{1,0:T(8,128)(2,1)S(1)} collective-permute-done((bf16[384,1152]{1,0:T(8,128)(2,1)S(1)}, bf16[384,1152]{1,0:T(8,128)(2,1)S(1)}, u32[]{:S(2)}, u32[]{:S(2)}) %collective-permute-start.1) | collective-permute-done | bytes 884768 | tf_op jit(solution)/shard_map/ppermute | solution.py:424
  50.1 0.0 collective-permute-done.7.refs_0_.refs_9_.refs_2_
  50.1 13.1 %collective-permute-done.8.refs_1_.refs_10_.refs_3_ = bf16[128,1152]{1,0:T(8,128)(2,1)S(1)} collective-permute-done((bf16[128,1152]{1,0:T(8,128)(2,1)S(1)}, bf16[128,1152]{1,0:T(8,128)(2,1)S(1)}, u32[]{:S(2)}, u32[]{:S(2)}) %collective-permute-start.8) | collective-permute-done | bytes 294944 | tf_op jit(solution)/shard_map/ppermute | solution.py:430
  63.1 2.6 %collective-permute-done.9.refs_2_.refs_8_.refs_1_ = bf16[128,1152]{1,0:T(8,128)(2,1)S(1)} collective-permute-done((bf16[128,1152]{1,0:T(8,128)(2,1)S(1)}, bf16[128,1152]{1,0:T(8,128)(2,1)S(1)}, u32[]{:S(2)}, u32[]{:S(2)}) %collective-permute-start.9) | collective-permute-done | bytes 294944 | tf_op jit(solution)/shard_map/ppermute | solution.py:432
  65.8 0.1 pass_after.1.refs_6_
  65.9 0.1 collective-permute-start.10
  66.0 0.0 copy-start.5
  66.0 0.0 copy-start.6
  66.0 1.9 %grad_norm_part.1.refs_4_ = f32[128,1536]{1,0:T(8,128)S(1)} custom-call(bf16[384,1152]{1,0:T(8,128)(2,1)S(1)} %copy-done.4, bf16[384,1152]{1,0:T(8,128)(2,1)S(1)} %collective-permute-done.6.refs_5_.refs_1_, bf16[384,1152]{1,0:T(8,128)(2,1)S(1)} %collective-permute-done.after_ref.refs_6_.refs_2_, ...), custom_call_target="tpu_custom_call" | custom-call | flops 6000000000 | bytes 18000000 | tf_op jit(solution)/shard_map/grad_norm_part/pallas_call | solution.py:334
  67.9 0.5 collective-permute-done.10.far_w
  68.4 1.7 %input_grad.1 = f32[1,128,1536]{2,1,0:T(8,128)} custom-call(bf16[384,1152]{1,0:T(8,128)(2,1)S(1)} %collective-permute-done.10.far_w, bf16[128,1152]{1,0:T(8,128)(2,1)S(1)} %get-tuple-element.18.refs_7_.refs_0_, bf16[128,1152]{1,0:T(8,128)(2,1)S(1)} %collective-permute-done.9.refs_2_.refs_8_.refs_1_, ...), custom_call_target="tpu_custom_call" | custom-call | flops 2000000000 | bytes 6000000 | tf_op jit(solution)/shard_map/input_grad/pallas_call | solution.py:362
  (14 shorter events, 0.0 us)
Async XLA Ops:
  0.0 27.1 %copy-start = (bf16[384,2304]{1,0:T(8,128)(2,1)S(1)}, bf16[384,2304]{1,0:T(8,128)(2,1)}, u32[]{:S(2)}) copy-start(bf16[384,2304]{1,0:T(8,128)(2,1)} %codes_ref.3) | copy-start | bytes 5308420
  0.0 27.1 %copy-start.3 = (f32[3,18]{1,0:T(4,128)S(1)}, f32[3,18]{1,0:T(4,128)}, u32[]{:S(2)}) copy-start(f32[3,18]{1,0:T(4,128)} %scales_ref.3) | copy-start | bytes 652
  4.2 28.6 %copy-start.1 = (bf16[128,1920]{1,0:T(8,128)(2,1)S(1)}, bf16[128,1920]{1,0:T(8,128)(2,1)}, u32[]{:S(2)}) copy-start(bf16[128,1920]{1,0:T(8,128)(2,1)} %get-tuple-element.13.refs_0_.refs_1_) | copy-start | bytes 1474564
  4.2 28.5 %copy-start.4 = (bf16[384,1152]{1,0:T(8,128)(2,1)S(1)}, bf16[384,1152]{1,0:T(8,128)(2,1)}, u32[]{:S(2)}) copy-start(bf16[384,1152]{1,0:T(8,128)(2,1)} %get-tuple-element.12.refs_4_.refs_0_) | copy-start | bytes 2654212
  4.3 22.9 %collective-permute-start = (bf16[384,1152]{1,0:T(8,128)(2,1)}, bf16[384,1152]{1,0:T(8,128)(2,1)S(1)}, u32[]{:S(2)}, u32[]{:S(2)}) collective-permute-start(bf16[384,1152]{1,0:T(8,128)(2,1)} %get-tuple-element.12.refs_4_.refs_0_), channel_id=1, source_target_pairs={{0,2},{1,3},{2,0},{3,1},{4,6},{5,7},{6,4},{7,5},{8,10},{9,11},{10,... | collective-permute-start | bytes 2654216 | tf_op jit(solution)/shard_map/ppermute | solution.py:420
  7.3 25.5 %collective-permute-start.6 = (bf16[384,1152]{1,0:T(8,128)(2,1)}, bf16[384,1152]{1,0:T(8,128)(2,1)S(1)}, u32[]{:S(2)}, u32[]{:S(2)}) collective-permute-start(bf16[384,1152]{1,0:T(8,128)(2,1)} %get-tuple-element.12.refs_4_.refs_0_), channel_id=1, source_target_pairs={{0,1},{1,0},{2,3},{3,2},{4,5},{5,4},{6,7},{7,6},{8,9},{9,8},{10,11... | collective-permute-start | bytes 2654216 | tf_op jit(solution)/shard_map/ppermute | solution.py:421
  7.3 20.7 %collective-permute-start.2 = (bf16[128,1920]{1,0:T(8,128)(2,1)}, bf16[128,1920]{1,0:T(8,128)(2,1)S(1)}, u32[]{:S(2)}, u32[]{:S(2)}) collective-permute-start(bf16[128,1920]{1,0:T(8,128)(2,1)} %get-tuple-element.13.refs_0_.refs_1_), channel_id=1, source_target_pairs={{0,4},{12,8},{1,5},{13,9},{2,6},{14,10},{3,7},{15,11},{16,20},{28,... | collective-permute-start | bytes 1474568 | tf_op jit(solution)/shard_map/ppermute | solution.py:419
  10.8 19.0 %collective-permute-start.3 = (bf16[128,1920]{1,0:T(8,128)(2,1)}, bf16[128,1920]{1,0:T(8,128)(2,1)S(1)}, u32[]{:S(2)}, u32[]{:S(2)}) collective-permute-start(bf16[128,1920]{1,0:T(8,128)(2,1)} %get-tuple-element.14), channel_id=1, source_target_pairs={{4,8},{8,4},{5,9},{9,5},{6,10},{10,6},{7,11},{11,7},{20,24},{24,20... | collective-permute-start | bytes 1474568 | tf_op jit(solution)/shard_map/ppermute | solution.py:417
  11.5 21.3 %collective-permute-start.4 = (bf16[128,1920]{1,0:T(8,128)(2,1)}, bf16[128,1920]{1,0:T(8,128)(2,1)S(1)}, u32[]{:S(2)}, u32[]{:S(2)}) collective-permute-start(bf16[128,1920]{1,0:T(8,128)(2,1)} %get-tuple-element.14), channel_id=1, source_target_pairs={{0,8},{12,4},{1,9},{13,5},{2,10},{14,6},{3,11},{15,7},{16,24},{28,... | collective-permute-start | bytes 1474568 | tf_op jit(solution)/shard_map/ppermute | solution.py:418
  27.1 7.8 %collective-permute-start.5 = (bf16[384,1152]{1,0:T(8,128)(2,1)S(1)}, bf16[384,1152]{1,0:T(8,128)(2,1)S(1)}, u32[]{:S(2)}, u32[]{:S(2)}) collective-permute-start(bf16[384,1152]{1,0:T(8,128)(2,1)S(1)} %collective-permute-done.after_ref.refs_6_.refs_2_), channel_id=1, source_target_pairs={{0,1},{1,0},{2,3},{3,2},{4,5},{5,4},{6,7},{7,6},{8,9},{9,8},{10,11... | collective-permute-start | bytes 2654216 | tf_op jit(solution)/shard_map/ppermute | solution.py:422
  27.9 7.0 %copy-start.2 = (f32[2304]{0:T(1024)S(1)}, f32[2304]{0:T(1024)}, u32[]{:S(2)}) copy-start(f32[2304]{0:T(1024)} %refs_6_.2) | copy-start | bytes 27652
  27.9 22.1 %collective-permute-start.1 = (bf16[384,1152]{1,0:T(8,128)(2,1)S(1)}, bf16[384,1152]{1,0:T(8,128)(2,1)S(1)}, u32[]{:S(2)}, u32[]{:S(2)}) collective-permute-start(bf16[384,1152]{1,0:T(8,128)(2,1)S(1)} %far_weight.1.refs_4_), channel_id=1, source_target_pairs={{0,2},{1,3},{2,0},{3,1},{4,6},{5,7},{6,4},{7,5},{8,10},{9,11},{10,... | collective-permute-start | bytes 2654216 | tf_op jit(solution)/shard_map/ppermute | solution.py:424
  29.8 36.2 %collective-permute-start.11 = (bf16[384,1152]{1,0:T(8,128)(2,1)S(1)}, bf16[384,1152]{1,0:T(8,128)(2,1)S(1)}, u32[]{:S(2)}, u32[]{:S(2)}) collective-permute-start(bf16[384,1152]{1,0:T(8,128)(2,1)S(1)} %far_weight.1.refs_4_), channel_id=1, source_target_pairs={{0,1},{1,0},{2,3},{3,2},{4,5},{5,4},{6,7},{7,6},{8,9},{9,8},{10,11... | collective-permute-start | bytes 2654216 | tf_op jit(solution)/shard_map/ppermute | solution.py:425
  42.3 7.7 %collective-permute-start.7 = (bf16[128,1152]{1,0:T(8,128)(2,1)S(1)}, bf16[128,1152]{1,0:T(8,128)(2,1)S(1)}, u32[]{:S(2)}, u32[]{:S(2)}) collective-permute-start(bf16[128,1152]{1,0:T(8,128)(2,1)S(1)} %get-tuple-element.15), channel_id=1, source_target_pairs={{4,8},{8,4},{5,9},{9,5},{6,10},{10,6},{7,11},{11,7},{20,24},{24,20... | collective-permute-start | bytes 884744 | tf_op jit(solution)/shard_map/ppermute | solution.py:431
  43.0 20.1 %collective-permute-start.8 = (bf16[128,1152]{1,0:T(8,128)(2,1)S(1)}, bf16[128,1152]{1,0:T(8,128)(2,1)S(1)}, u32[]{:S(2)}, u32[]{:S(2)}) collective-permute-start(bf16[128,1152]{1,0:T(8,128)(2,1)S(1)} %get-tuple-element.16), channel_id=1, source_target_pairs={{4,12},{8,0},{5,13},{9,1},{6,14},{10,2},{7,15},{11,3},{20,28},{24,... | collective-permute-start | bytes 884744 | tf_op jit(solution)/shard_map/ppermute | solution.py:430
  44.3 21.5 %collective-permute-start.9 = (bf16[128,1152]{1,0:T(8,128)(2,1)S(1)}, bf16[128,1152]{1,0:T(8,128)(2,1)S(1)}, u32[]{:S(2)}, u32[]{:S(2)}) collective-permute-start(bf16[128,1152]{1,0:T(8,128)(2,1)S(1)} %get-tuple-element.17), channel_id=1, source_target_pairs={{4,0},{8,12},{5,1},{9,13},{6,2},{10,14},{7,3},{11,15},{20,16},{24,... | collective-permute-start | bytes 884744 | tf_op jit(solution)/shard_map/ppermute | solution.py:432
  65.9 2.5 %collective-permute-start.10 = (bf16[384,1152]{1,0:T(8,128)(2,1)S(1)}, bf16[384,1152]{1,0:T(8,128)(2,1)S(1)}, u32[]{:S(2)}, u32[]{:S(2)}) collective-permute-start(bf16[384,1152]{1,0:T(8,128)(2,1)S(1)} %pass_after.1.refs_6_), channel_id=1, source_target_pairs={{0,1},{1,0},{2,3},{3,2},{4,5},{5,4},{6,7},{7,6},{8,9},{9,8},{10,11... | collective-permute-start | bytes 2654216 | tf_op jit(solution)/shard_map/ppermute | solution.py:435
  66.0 2.4 %copy-start.5 = (bf16[1,128,1536]{2,1,0:T(8,128)(2,1)S(1)}, bf16[1,128,1536]{2,1,0:T(8,128)(2,1)}, u32[]{:S(2)}) copy-start(bf16[1,128,1536]{2,1,0:T(8,128)(2,1)} %refs_5_.1) | copy-start | bytes 1179652
  66.0 2.4 %copy-start.6 = (f32[1536]{0:T(1024)S(1)}, f32[1536]{0:T(1024)}, u32[]{:S(2)}) copy-start(f32[1536]{0:T(1024)} %refs_6_.3) | copy-start | bytes 18436

commit v3 on v2

--- a/solution.py
+++ b/solution.py
@@ -201,32 +201,10 @@
     )
 
 
-def project_kernel(*refs):
-    norms, weights, sums = refs[0:4], refs[4:7], refs[7]
-    rows = norm_columns(norms, range(3), weights[0].shape[0])
-    for part in range(3):
-        columns = jnp.concatenate([w[:, part * HALF : (part + 1) * HALF] for w in weights], axis=0)
-        sums[:, part * HALF : (part + 1) * HALF] = dot_plain(rows, columns)
-
-
-def project_step(norms, weights):
-    tokens = norms[0].shape[0]
-    return pl.pallas_call(
-        project_kernel,
-        out_shape=jax.ShapeDtypeStruct((tokens * len(norms), 3 * HALF), jnp.float32),
-        in_specs=[spec()] * 7,
-        out_specs=spec(),
-        compiler_params=pltpu.CompilerParams(vmem_limit_bytes=24 * 2**20),
-        cost_estimate=cost(6),
-        name="projection_part",
-    )(*norms, *weights)
-
-
-def finish_kernel(*refs):
-    norms = refs[0:4]
-    weight, sums, bias_ref, proj = refs[4:]
+def project_kernel(first, *refs):
+    norms, weights, bias_ref, proj = refs[0:2], refs[2:7], refs[7], refs[-1]
     half = half_index()
-    rows = norm_columns(norms, (3,), weight.shape[0])
+    rows = norm_columns(norms, range(4), weights[0].shape[0])
     bias = row_vector(bias_ref)
     for part in range(3):
         at = slice(part * HALF, (part + 1) * HALF)
@@ -235,22 +213,26 @@
             bias[:, part * HD : part * HD + HALF],
             bias[:, part * HD + HALF : (part + 1) * HD],
         )
-        value = (sums[:, at] + dot_plain(rows, weight[:, at]) + shift).astype(jnp.bfloat16)
+        columns = jnp.concatenate([w[:, at] for w in weights], axis=0)
+        value = (dot_plain(rows, columns) + shift).astype(jnp.bfloat16)
         if part == 0:
             value = value * jnp.bfloat16(HEAD_DIM**-0.5)
-        proj[:, at] = value
-
-
-def finish_step(norms, weight, sums, bias):
-    return pl.pallas_call(
-        finish_kernel,
-        out_shape=jax.ShapeDtypeStruct(sums.shape, jnp.bfloat16),
-        in_specs=[spec()] * 7,
+        proj[first : first + rows.shape[0], at] = value
+
+
+def project_step(norms, weights, bias, *before):
+    tokens = norms[0].shape[0]
+    first = 2 * tokens * len(before)
+    return pl.pallas_call(
+        functools.partial(project_kernel, first),
+        out_shape=jax.ShapeDtypeStruct((4 * tokens, 3 * HALF), jnp.bfloat16),
+        in_specs=[spec()] * (8 + len(before)),
         out_specs=spec(),
+        input_output_aliases={8: 0} if before else {},
         compiler_params=pltpu.CompilerParams(vmem_limit_bytes=24 * 2**20),
         cost_estimate=cost(0.01),
         name="projection",
-    )(*norms, weight, sums, bias)
+    )(*norms, *weights, bias, *before)
 
 
 PAIR = 2 * HEAD_DIM
@@ -308,67 +290,110 @@
     )(proj, *grads, *after)
 
 
-def pick_grads(own_ref, back_ref, cross_ref, skip_ref):
+def join_halves(weights):
+    return [w[...] for w in weights[:3]] + [jnp.concatenate([w[...] for w in weights[3:]], axis=0)]
+
+
+def on_middle():
     place = lax.axis_index("seq")
-    middle = (place == 1) | (place == 2)
-    return (
-        jnp.where(middle, own_ref[...], back_ref[...]),
-        jnp.where(middle, cross_ref[...], skip_ref[...]),
-    )
-
-
-def part_kernel(*refs):
-    near_w, far_w, sums = refs[0:4], refs[4:7], refs[-1]
-    near, far = pick_grads(*refs[7:11])
+    return (place == 1) | (place == 2)
+
+
+def early_kernel(*refs):
+    near_w, far_w = join_halves(refs[0:5]), refs[5:8]
+    own_ref, skip_ref, tokens_ref, sums, normed_out, inverse_out = refs[8:]
+    middle = on_middle()
     mine = lax.axis_index("weight")
-    depth = near_w[0].shape[0]
-    for j in range(4):
-        value = dot_last(near, near_w[j][...])
-        if j < len(far_w):
-            value += dot_last(far, far_w[j][...])
-        sums[:, pl.ds(pl.multiple_of((mine ^ j) * depth, QBLOCK), depth)] = value
-
-
-def part_step(near_w, far_w, pieces):
-    rows = pieces[0].shape[0]
-    return pl.pallas_call(
-        part_kernel,
-        out_shape=jax.ShapeDtypeStruct((rows, 4 * near_w[0].shape[0]), jnp.float32),
-        in_specs=[spec()] * 11,
-        out_specs=spec(),
-        compiler_params=pltpu.CompilerParams(vmem_limit_bytes=24 * 2**20),
-        cost_estimate=cost(6),
-        name="grad_norm_part",
-    )(*near_w, *far_w, *pieces)
-
-
-def last_kernel(far_w, *refs):
-    sums, tokens_ref, gain_ref, out_ref, grad_norm = refs[4:]
-    _, far = pick_grads(*refs[0:4])
-    depth = far_w.shape[0]
-    at = pl.ds(pl.multiple_of((lax.axis_index("weight") ^ 3) * depth, QBLOCK), depth)
-    grad_norm[...] = sums[...]
-    grad_norm[:, at] += dot_last(far, far_w[...])
-    gain = row_vector(gain_ref)
+    depth = far_w[0].shape[0]
+
+    def fill(value_ref, weights, far):
+        value = value_ref[...]
+        for j in range(4):
+            at = pl.ds(pl.multiple_of((mine ^ j) * depth, QBLOCK), depth)
+            if j < len(weights):
+                sums[:, at] = dot_last(value, weights[j][...] if far else weights[j])
+            else:
+                sums[:, at] = jnp.zeros((value.shape[0], depth), jnp.float32)
+
+    pl.when(middle)(lambda: fill(own_ref, near_w, False))
+    pl.when(jnp.logical_not(middle))(lambda: fill(skip_ref, far_w, True))
     for r in range(0, tokens_ref.shape[1], 16):
         normed, inverse = norm_rows(tokens_ref[0, r : r + 16, :].astype(jnp.float32))
+        normed_out[r : r + 16, :] = normed
+        inverse_out[r : r + 16, :] = jnp.broadcast_to(inverse, (16, QBLOCK))
+
+
+def early_step(near_w, far_w, own, skip, tokens):
+    rows, width = tokens.shape[1:]
+    full = jax.ShapeDtypeStruct((rows, width), jnp.float32)
+    return pl.pallas_call(
+        early_kernel,
+        out_shape=(full, full, jax.ShapeDtypeStruct((rows, QBLOCK), jnp.float32)),
+        in_specs=[spec()] * 11,
+        out_specs=(spec(),) * 3,
+        compiler_params=pltpu.CompilerParams(vmem_limit_bytes=24 * 2**20),
+        cost_estimate=cost(20),
+        name="grad_norm_part",
+    )(*near_w, *far_w, own, skip, tokens)
+
+
+def last_kernel(*refs):
+    near_w, far_w = join_halves(refs[0:5]), refs[5:9]
+    cross_ref, back_ref, skip_ref, sums, normed_ref, inverse_ref, gain_ref, out_ref, grad_norm = refs[9:]
+    middle = on_middle()
+    mine = lax.axis_index("weight")
+    depth = far_w[0].shape[0]
+
+    def fill(value_ref, weights, far):
+        value = value_ref[...]
+        for j in range(4):
+            at = pl.ds(pl.multiple_of((mine ^ j) * depth, QBLOCK), depth)
+            total = sums[:, at] + dot_last(value, weights[j][...] if far else weights[j])
+            if j == 3 and not far:
+                total += dot_last(skip_ref[...], far_w[3][...])
+            grad_norm[:, at] = total
+
+    pl.when(middle)(lambda: fill(cross_ref, far_w, True))
+    pl.when(jnp.logical_not(middle))(lambda: fill(back_ref, near_w, False))
+    gain = row_vector(gain_ref)
+    for r in range(0, normed_ref.shape[0], 16):
+        normed = normed_ref[r : r + 16, :]
         grad_hat = grad_norm[r : r + 16, :] * gain
         first_mean = jnp.mean(grad_hat, axis=-1, keepdims=True)
         second_mean = jnp.mean(grad_hat * normed, axis=-1, keepdims=True)
-        out_ref[0, r : r + 16, :] = inverse * (grad_hat - first_mean - normed * second_mean)
-
-
-def last_step(far_w, pieces, sums, tokens, gain):
+        out_ref[0, r : r + 16, :] = inverse_ref[r : r + 16, :1] * (grad_hat - first_mean - normed * second_mean)
+
+
+def last_step(near_w, far_w, cross, back, skip, sums, normed, inverse, gain):
     return pl.pallas_call(
         last_kernel,
-        out_shape=jax.ShapeDtypeStruct(tokens.shape, jnp.float32),
-        in_specs=[spec()] * 8,
+        out_shape=jax.ShapeDtypeStruct((1, *normed.shape), jnp.float32),
+        in_specs=[spec()] * 16,
         out_specs=spec(),
-        scratch_shapes=[VMEM(tokens.shape[1:], jnp.float32)],
+        scratch_shapes=[VMEM(normed.shape, jnp.float32)],
         compiler_params=pltpu.CompilerParams(vmem_limit_bytes=24 * 2**20),
         cost_estimate=cost(2),
         name="input_grad",
-    )(far_w, *pieces, sums, tokens, gain)
+    )(*near_w, *far_w, cross, back, skip, sums, normed, inverse, gain)
+
+
+def split_kernel(value_ref, upper_ref, lower_ref):
+    middle = upper_ref.shape[0]
+    upper_ref[...] = value_ref[:middle]
+    lower_ref[...] = value_ref[middle:]
+
+
+def split_step(value):
+    half = jax.ShapeDtypeStruct((value.shape[0] // 2, value.shape[1]), value.dtype)
+    return pl.pallas_call(
+        split_kernel,
+        out_shape=(half, half),
+        in_specs=[spec()],
+        out_specs=(spec(), spec()),
+        compiler_params=pltpu.CompilerParams(vmem_limit_bytes=16 * 2**20),
+        cost_estimate=cost(0.01),
+        name="split_rows",
+    )(value)
 
 
 def pass_kernel(value_ref, *refs):
@@ -419,23 +444,22 @@
     both_end = lax.ppermute(both_near, "seq", END_TO_MIDDLE)
     near_across = lax.ppermute(near, "weight", flip(2))
     near_beside = lax.ppermute(near, "weight", flip(1))
-    near_diagonal = lax.ppermute(near_across, "weight", flip(1))
+    near_diagonal = [lax.ppermute(w, "weight", flip(1)) for w in split_step(near_across)]
     far = far_step(input_scales, input_codes, near_across)
     far_across = lax.ppermute(far, "weight", flip(2))
-    far_beside = lax.ppermute(far, "weight", flip(1))
     rows = (both_near, both_end, both_mid, both_far)
-    sums = project_step(rows, (near, near_beside, near_across))
-    proj = finish_step(rows, near_diagonal, sums, input_bias)
+    near_w = (near, near_beside, near_across, *near_diagonal)
+    proj = project_step(rows[:2], near_w, input_bias)
+    proj = project_step(rows[2:], near_w, input_bias, proj)
     own, end, mid, skip = attention_step(proj, rows, (0, 1, 2))
     skip = lax.ppermute(skip, "seq", FAR_TO_END)
     cross = lax.ppermute(mid, "seq", MIDDLE)
     back = lax.ppermute(end, "seq", MIDDLE_TO_END)
-    pieces = (own, back, cross, skip)
-    far_across = pass_after(far_across, cross, skip, back)
-    far_diagonal = lax.ppermute(far_across, "weight", flip(1))
-    near_w = (near, near_beside, near_across, near_diagonal)
-    sums = part_step(near_w, (far, far_beside, far_across), pieces)
-    return last_step(far_diagonal, pieces, sums, tokens, norm_gain)
+    far_beside = lax.ppermute(pass_after(far, own), "weight", flip(1))
+    far_w = (far, far_beside, far_across)
+    early = early_step(near_w, far_w, own, skip, tokens)
+    far_diagonal = lax.ppermute(pass_after(far_across, skip), "weight", flip(1))
+    return last_step(near_w, (*far_w, far_diagonal), cross, back, skip, *early, norm_gain)
 
 
 def dequantize(codes, scales):

time: 70.3 us -> 63.9 us (0.909)
  waiting for transfers between devices: 35.1 us -> 27 us
  Pallas kernels: 18.2 us -> 19 us
  starting transfers between devices: 16.5 us -> 17.3 us
    ppermute x1, waiting for transfers between devices: 13.1 us -> 4.36 us  [local_middle(): skip = lax.ppermute(skip, 'seq', FAR_TO_END)]
    ppermute x1, waiting for transfers between devices: 2.8 us -> 0.01 us  [local_middle(): both_far = lax.ppermute(both_other, 'seq', END_TO_FAR)]
    ppermute x1, waiting for transfers between devices: 4.45 us -> 6.64 us  [local_middle(): far_across = lax.ppermute(far, 'weight', flip(2))]
    ppermute x1, waiting for transfers between devices: 2.63 us -> 4.36 us  [local_middle(): back = lax.ppermute(end, 'seq', MIDDLE_TO_END)]
    pallas_call x4 -> x5, Pallas kernels: 6.57 us -> 7.19 us  [the longest x1 2.84 us: last_step(): pl.pallas_call(last_kernel, out_shape=jax.ShapeDtypeStruct((1, *normed.sh...]
  transfers between devices with their start and end apart: 12 -> 13, of which waited for: 6 -> 4; matrix products, arithmetic and copies ran while one was open for 0% -> 0% of each run, Pallas kernels for 18% -> 19%
where the time goes in v3:
time: 63.9 us; the launch traced here: 63.7 us
  waiting for transfers between devices  27 us (42%)
  Pallas kernels  19 us (30%)
  starting transfers between devices  17.3 us (27%)
    ppermute x1, waiting for transfers between devices, local_middle(): near_across = lax.ppermute(near, 'weight', flip(2))  11.6 us
    ppermute x1, waiting for transfers between devices, local_middle(): far_across = lax.ppermute(far, 'weight', flip(2))  6.64 us
    pallas_call x1, Pallas kernels, attention_step(): pl.pallas_call(functools.partial(attention_kernel, pairs), out_shape=(out...  6.53 us
    ppermute x1, waiting for transfers between devices, local_middle(): back = lax.ppermute(end, 'seq', MIDDLE_TO_END)  4.36 us
    ppermute x1, waiting for transfers between devices, local_middle(): skip = lax.ppermute(skip, 'seq', FAR_TO_END)  4.36 us
    pallas_call x1, Pallas kernels, first_step(): pl.pallas_call(first_kernel, out_shape=(jax.ShapeDtypeStruct((depth, 3 *...  4.23 us
    ppermute x1, starting transfers between devices, local_middle(): both_far = lax.ppermute(both_other, 'seq', END_TO_FAR)  3.97 us
    ppermute x1, starting transfers between devices, local_middle(): both_end = lax.ppermute(both_near, 'seq', END_TO_MIDDLE)  3.5 us
  transfers between devices with their start and end apart: 13, of which 4 were waited for; matrix products, arithmetic and copies ran while one was open for 0% of the time, Pallas kernels for 19%

profile of v3, /device:TPU:0, one launch (start us, length us, event | category | flops | bytes accessed | tf_op | source)
XLA Modules:
  0.0 63.7 jit_solution(4306989207546198632)
XLA Ops:
  0.0 4.2 %first_weights_and_rows.1 = (bf16[384,1152]{1,0:T(8,128)(2,1)}, bf16[128,1920]{1,0:T(8,128)(2,1)}, bf16[128,1920]{1,0:T(8,128)(2,1)}) custom-call(bf16[1,128,1536]{2,1,0:T(8,128)(2,1)} %refs_10_.1, f32[1536]{0:T(1024)} %refs_15_.1, f32[1536]{0:T(1024)} %shift_ref.1, f32[3,18]{1,0:T(4,128)} %scales_ref.3, bf16[384,2304]{1,0:T(8,128)(2,1)} %codes_ref.3, ...), custom_call_target="tpu_custom_call" | custom-call | flops 3000000000 | bytes 9000000 | tf_op jit(solution)/shard_map/first_weights_and_rows/pallas_call | solution.py:118
  4.2 3.0 %collective-permute-start.1 = (bf16[384,1152]{1,0:T(8,128)(2,1)}, bf16[384,1152]{1,0:T(8,128)(2,1)S(1)}, u32[]{:S(2)}, u32[]{:S(2)}) collective-permute-start(bf16[384,1152]{1,0:T(8,128)(2,1)} %get-tuple-element.17.refs_2_.refs_0_), channel_id=1, source_target_pairs={{0,2},{1,3},{2,0},{3,1},{4,6},{5,7},{6,4},{7,5},{8,10},{9,11},{10,... | collective-permute-start | bytes 2654216 | tf_op jit(solution)/shard_map/ppermute | solution.py:445
  7.3 3.5 %collective-permute-start.6 = (bf16[128,1920]{1,0:T(8,128)(2,1)}, bf16[128,1920]{1,0:T(8,128)(2,1)S(1)}, u32[]{:S(2)}, u32[]{:S(2)}) collective-permute-start(bf16[128,1920]{1,0:T(8,128)(2,1)} %get-tuple-element.21.refs_0_.refs_1_), channel_id=1, source_target_pairs={{0,4},{12,8},{1,5},{13,9},{2,6},{14,10},{3,7},{15,11},{16,20},{28,... | collective-permute-start | bytes 1474568 | tf_op jit(solution)/shard_map/ppermute | solution.py:444
  10.8 0.1 collective-permute-start
  10.8 0.7 %collective-permute-start.4 = (bf16[128,1920]{1,0:T(8,128)(2,1)}, bf16[128,1920]{1,0:T(8,128)(2,1)S(1)}, u32[]{:S(2)}, u32[]{:S(2)}) collective-permute-start(bf16[128,1920]{1,0:T(8,128)(2,1)} %get-tuple-element.20), channel_id=1, source_target_pairs={{4,8},{8,4},{5,9},{9,5},{6,10},{10,6},{7,11},{11,7},{20,24},{24,20... | collective-permute-start | bytes 1474568 | tf_op jit(solution)/shard_map/ppermute | solution.py:442
  11.5 4.0 %collective-permute-start.5 = (bf16[128,1920]{1,0:T(8,128)(2,1)}, bf16[128,1920]{1,0:T(8,128)(2,1)S(1)}, u32[]{:S(2)}, u32[]{:S(2)}) collective-permute-start(bf16[128,1920]{1,0:T(8,128)(2,1)} %get-tuple-element.20), channel_id=1, source_target_pairs={{0,8},{12,4},{1,9},{13,5},{2,10},{14,6},{3,11},{15,7},{16,24},{28,... | collective-permute-start | bytes 1474568 | tf_op jit(solution)/shard_map/ppermute | solution.py:443
  15.5 11.6 %collective-permute-done.1.value_ref.after_ref.refs_4_.refs_2_ = bf16[384,1152]{1,0:T(8,128)(2,1)S(1)} collective-permute-done((bf16[384,1152]{1,0:T(8,128)(2,1)}, bf16[384,1152]{1,0:T(8,128)(2,1)S(1)}, u32[]{:S(2)}, u32[]{:S(2)}) %collective-permute-start.1) | collective-permute-done | bytes 884768 | tf_op jit(solution)/shard_map/ppermute | solution.py:445
  27.1 0.1 split_rows.1
  27.2 0.1 collective-permute-start.2
  27.3 0.5 collective-permute-start.3
  27.8 0.8 %far_weight.1.refs_5_ = bf16[384,1152]{1,0:T(8,128)(2,1)S(1)} custom-call(f32[3,18]{1,0:T(4,128)S(1)} %copy-done.5, bf16[384,2304]{1,0:T(8,128)(2,1)S(1)} %copy-done.1, bf16[384,1152]{1,0:T(8,128)(2,1)S(1)} %collective-permute-done.1.value_ref.after_ref.refs_4_.refs_2_), custom_call_target="tpu_custom_call" | custom-call | flops 10000000 | bytes 30000 | tf_op jit(solution)/shard_map/far_weight/pallas_call | solution.py:166
  28.6 0.0 copy-start.2
  28.6 0.0 copy-start.3
  28.6 0.1 copy.15.value_ref
  28.7 1.8 %collective-permute-start.8 = (bf16[384,1152]{1,0:T(8,128)(2,1)S(1)}, bf16[384,1152]{1,0:T(8,128)(2,1)S(1)}, u32[]{:S(2)}, u32[]{:S(2)}) collective-permute-start(bf16[384,1152]{1,0:T(8,128)(2,1)S(1)} %far_weight.1.refs_5_), channel_id=1, source_target_pairs={{0,2},{1,3},{2,0},{3,1},{4,6},{5,7},{6,4},{7,5},{8,10},{9,11},{10,... | collective-permute-start | bytes 2654216 | tf_op jit(solution)/shard_map/ppermute | solution.py:449
  30.5 1.4 %projection.2.refs_8_ = bf16[512,1152]{1,0:T(8,128)(2,1)S(1)} custom-call(bf16[128,1920]{1,0:T(8,128)(2,1)S(1)} %copy-done.2, bf16[128,1920]{1,0:T(8,128)(2,1)S(1)} %collective-permute-done.6.refs_1_.refs_2_, bf16[384,1152]{1,0:T(8,128)(2,1)S(1)} %copy-done, bf16[384,1152]{1,0:T(8,128)(2,1)S(1)} %collective-permute-done.refs_3_.refs_1_, ...), custom_call_target="tpu_custom_call" | custom-call | flops 10000000 | bytes 30000 | tf_op jit(solution)/shard_map/projection/pallas_call | solution.py:226
  32.0 1.4 %projection.3.refs_0_ = bf16[512,1152]{1,0:T(8,128)(2,1)S(1)} custom-call(bf16[128,1920]{1,0:T(8,128)(2,1)S(1)} %collective-permute-done.4.refs_0_.refs_3_, bf16[128,1920]{1,0:T(8,128)(2,1)S(1)} %collective-permute-done.5.refs_1_.refs_4_, bf16[384,1152]{1,0:T(8,128)(2,1)S(1)} %copy-done, ...), custom_call_target="tpu_custom_call", output_to_operand_aliasing={{}: (8, {})} | custom-call | flops 10000000 | bytes 30000 | tf_op jit(solution)/shard_map/projection/pallas_call | solution.py:226
  33.4 6.5 %attention.1 = (bf16[128,1152]{1,0:T(8,128)(2,1)S(1)}, bf16[128,1152]{1,0:T(8,128)(2,1)S(1)}, bf16[128,1152]{1,0:T(8,128)(2,1)S(1)}, bf16[128,1152]{1,0:T(8,128)(2,1)S(1)}) custom-call(bf16[512,1152]{1,0:T(8,128)(2,1)S(1)} %projection.3.refs_0_, bf16[128,1920]{1,0:T(8,128)(2,1)S(1)} %copy-done.2, ...), custom_call_target="tpu_custom_call" | custom-call | flops 12000000000 | bytes 36000000 | tf_op jit(solution)/shard_map/attention/pallas_call | solution.py:282
  39.9 0.1 pass_after.2
  40.0 0.1 collective-permute-start.7
  40.1 1.3 %collective-permute-start.9 = (bf16[128,1152]{1,0:T(8,128)(2,1)S(1)}, bf16[128,1152]{1,0:T(8,128)(2,1)S(1)}, u32[]{:S(2)}, u32[]{:S(2)}) collective-permute-start(bf16[128,1152]{1,0:T(8,128)(2,1)S(1)} %get-tuple-element.23), channel_id=1, source_target_pairs={{4,12},{8,0},{5,13},{9,1},{6,14},{10,2},{7,15},{11,3},{20,28},{24,... | collective-permute-start | bytes 884744 | tf_op jit(solution)/shard_map/ppermute | solution.py:455
  41.4 0.7 %collective-permute-start.11 = (bf16[128,1152]{1,0:T(8,128)(2,1)S(1)}, bf16[128,1152]{1,0:T(8,128)(2,1)S(1)}, u32[]{:S(2)}, u32[]{:S(2)}) collective-permute-start(bf16[128,1152]{1,0:T(8,128)(2,1)S(1)} %get-tuple-element.24), channel_id=1, source_target_pairs={{4,8},{8,4},{5,9},{9,5},{6,10},{10,6},{7,11},{11,7},{20,24},{24,20... | collective-permute-start | bytes 884744 | tf_op jit(solution)/shard_map/ppermute | solution.py:456
  42.1 0.0 copy-start.6
  42.1 1.6 %collective-permute-start.12 = (bf16[128,1152]{1,0:T(8,128)(2,1)S(1)}, bf16[128,1152]{1,0:T(8,128)(2,1)S(1)}, u32[]{:S(2)}, u32[]{:S(2)}) collective-permute-start(bf16[128,1152]{1,0:T(8,128)(2,1)S(1)} %get-tuple-element.25), channel_id=1, source_target_pairs={{4,0},{8,12},{5,1},{9,13},{6,2},{10,14},{7,3},{11,15},{20,16},{24,... | collective-permute-start | bytes 884744 | tf_op jit(solution)/shard_map/ppermute | solution.py:457
  43.7 6.6 %collective-permute-done.8.refs_7_ = bf16[384,1152]{1,0:T(8,128)(2,1)S(1)} collective-permute-done((bf16[384,1152]{1,0:T(8,128)(2,1)S(1)}, bf16[384,1152]{1,0:T(8,128)(2,1)S(1)}, u32[]{:S(2)}, u32[]{:S(2)}) %collective-permute-start.8) | collective-permute-done | bytes 884768 | tf_op jit(solution)/shard_map/ppermute | solution.py:449
  50.4 0.1 copy.16.value_ref
  50.5 4.4 %collective-permute-done.9.refs_0_.refs_9_.refs_11_ = bf16[128,1152]{1,0:T(8,128)(2,1)S(1)} collective-permute-done((bf16[128,1152]{1,0:T(8,128)(2,1)S(1)}, bf16[128,1152]{1,0:T(8,128)(2,1)S(1)}, u32[]{:S(2)}, u32[]{:S(2)}) %collective-permute-start.9) | collective-permute-done | bytes 294944 | tf_op jit(solution)/shard_map/ppermute | solution.py:455
  54.8 0.1 pass_after.3
  55.0 0.1 collective-permute-start.10
  55.1 1.5 %grad_norm_part.1 = (f32[128,1536]{1,0:T(8,128)S(1)}, f32[128,1536]{1,0:T(8,128)S(1)}, f32[128,128]{1,0:T(8,128)S(1)}) custom-call(bf16[384,1152]{1,0:T(8,128)(2,1)S(1)} %copy-done, bf16[384,1152]{1,0:T(8,128)(2,1)S(1)} %collective-permute-done.refs_3_.refs_1_, bf16[384,1152]{1,0:T(8,128)(2,1)S(1)} %collective-permute-done.1.value_ref.after_ref.refs_4_.refs_2_, ...), custom_call_target="tpu_custom_call" | custom-call | flops 20000000000 | bytes 60000000 | tf_op jit(solution)/shard_map/grad_norm_part/pallas_call | solution.py:329
  56.5 4.4 %collective-permute-done.12.refs_10_ = bf16[128,1152]{1,0:T(8,128)(2,1)S(1)} collective-permute-done((bf16[128,1152]{1,0:T(8,128)(2,1)S(1)}, bf16[128,1152]{1,0:T(8,128)(2,1)S(1)}, u32[]{:S(2)}, u32[]{:S(2)}) %collective-permute-start.12) | collective-permute-done | bytes 294944 | tf_op jit(solution)/shard_map/ppermute | solution.py:457
  60.9 2.8 %input_grad.1 = f32[1,128,1536]{2,1,0:T(8,128)} custom-call(bf16[384,1152]{1,0:T(8,128)(2,1)S(1)} %copy-done, bf16[384,1152]{1,0:T(8,128)(2,1)S(1)} %collective-permute-done.refs_3_.refs_1_, bf16[384,1152]{1,0:T(8,128)(2,1)S(1)} %collective-permute-done.1.value_ref.after_ref.refs_4_.refs_2_, bf16[192,1152]{1,0:T(8,128)(2,1)S(1)} %collective-permute-done.2.refs_5_.refs_3_, ...), custom_call_target="tpu_custom_call" | custom-call | flops 2000000000 | bytes 6000000 | tf_op jit(solution)/shard_map/input_grad/pallas_call | solution.py:368
  (20 shorter events, 0.0 us)
Async XLA Ops:
  0.0 27.8 %copy-start.5 = (f32[3,18]{1,0:T(4,128)S(1)}, f32[3,18]{1,0:T(4,128)}, u32[]{:S(2)}) copy-start(f32[3,18]{1,0:T(4,128)} %scales_ref.3) | copy-start | bytes 652
  0.0 27.8 %copy-start.1 = (bf16[384,2304]{1,0:T(8,128)(2,1)S(1)}, bf16[384,2304]{1,0:T(8,128)(2,1)}, u32[]{:S(2)}) copy-start(bf16[384,2304]{1,0:T(8,128)(2,1)} %codes_ref.3) | copy-start | bytes 5308420
  4.2 22.9 %collective-permute-start.1 = (bf16[384,1152]{1,0:T(8,128)(2,1)}, bf16[384,1152]{1,0:T(8,128)(2,1)S(1)}, u32[]{:S(2)}, u32[]{:S(2)}) collective-permute-start(bf16[384,1152]{1,0:T(8,128)(2,1)} %get-tuple-element.17.refs_2_.refs_0_), channel_id=1, source_target_pairs={{0,2},{1,3},{2,0},{3,1},{4,6},{5,7},{6,4},{7,5},{8,10},{9,11},{10,... | collective-permute-start | bytes 2654216 | tf_op jit(solution)/shard_map/ppermute | solution.py:445
  7.3 20.0 %collective-permute-start.6 = (bf16[128,1920]{1,0:T(8,128)(2,1)}, bf16[128,1920]{1,0:T(8,128)(2,1)S(1)}, u32[]{:S(2)}, u32[]{:S(2)}) collective-permute-start(bf16[128,1920]{1,0:T(8,128)(2,1)} %get-tuple-element.21.refs_0_.refs_1_), channel_id=1, source_target_pairs={{0,4},{12,8},{1,5},{13,9},{2,6},{14,10},{3,7},{15,11},{16,20},{28,... | collective-permute-start | bytes 1474568 | tf_op jit(solution)/shard_map/ppermute | solution.py:444
  10.8 17.9 %collective-permute-start = (bf16[384,1152]{1,0:T(8,128)(2,1)}, bf16[384,1152]{1,0:T(8,128)(2,1)S(1)}, u32[]{:S(2)}, u32[]{:S(2)}) collective-permute-start(bf16[384,1152]{1,0:T(8,128)(2,1)} %get-tuple-element.17.refs_2_.refs_0_), channel_id=1, source_target_pairs={{0,1},{1,0},{2,3},{3,2},{4,5},{5,4},{6,7},{7,6},{8,9},{9,8},{10,11... | collective-permute-start | bytes 2654216 | tf_op jit(solution)/shard_map/ppermute | solution.py:446
  10.8 21.1 %collective-permute-start.4 = (bf16[128,1920]{1,0:T(8,128)(2,1)}, bf16[128,1920]{1,0:T(8,128)(2,1)S(1)}, u32[]{:S(2)}, u32[]{:S(2)}) collective-permute-start(bf16[128,1920]{1,0:T(8,128)(2,1)} %get-tuple-element.20), channel_id=1, source_target_pairs={{4,8},{8,4},{5,9},{9,5},{6,10},{10,6},{7,11},{11,7},{20,24},{24,20... | collective-permute-start | bytes 1474568 | tf_op jit(solution)/shard_map/ppermute | solution.py:442
  11.5 20.4 %collective-permute-start.5 = (bf16[128,1920]{1,0:T(8,128)(2,1)}, bf16[128,1920]{1,0:T(8,128)(2,1)S(1)}, u32[]{:S(2)}, u32[]{:S(2)}) collective-permute-start(bf16[128,1920]{1,0:T(8,128)(2,1)} %get-tuple-element.20), channel_id=1, source_target_pairs={{0,8},{12,4},{1,9},{13,5},{2,10},{14,6},{3,11},{15,7},{16,24},{28,... | collective-permute-start | bytes 1474568 | tf_op jit(solution)/shard_map/ppermute | solution.py:443
  27.2 3.3 %collective-permute-start.2 = (bf16[192,1152]{1,0:T(8,128)(2,1)S(1)}, bf16[192,1152]{1,0:T(8,128)(2,1)S(1)}, u32[]{:S(2)}, u32[]{:S(2)}) collective-permute-start(bf16[192,1152]{1,0:T(8,128)(2,1)S(1)} %get-tuple-element.18), channel_id=1, source_target_pairs={{0,1},{1,0},{2,3},{3,2},{4,5},{5,4},{6,7},{7,6},{8,9},{9,8},{10,11... | collective-permute-start | bytes 1327112 | tf_op jit(solution)/shard_map/ppermute | solution.py:447
  27.3 3.2 %collective-permute-start.3 = (bf16[192,1152]{1,0:T(8,128)(2,1)S(1)}, bf16[192,1152]{1,0:T(8,128)(2,1)S(1)}, u32[]{:S(2)}, u32[]{:S(2)}) collective-permute-start(bf16[192,1152]{1,0:T(8,128)(2,1)S(1)} %get-tuple-element.19), channel_id=1, source_target_pairs={{0,1},{1,0},{2,3},{3,2},{4,5},{5,4},{6,7},{7,6},{8,9},{9,8},{10,11... | collective-permute-start | bytes 1327112 | tf_op jit(solution)/shard_map/ppermute | solution.py:447
  28.6 1.9 %copy-start = (bf16[384,1152]{1,0:T(8,128)(2,1)S(1)}, bf16[384,1152]{1,0:T(8,128)(2,1)}, u32[]{:S(2)}) copy-start(bf16[384,1152]{1,0:T(8,128)(2,1)} %get-tuple-element.17.refs_2_.refs_0_) | copy-start | bytes 2654212
  28.6 1.9 %copy-start.2 = (bf16[128,1920]{1,0:T(8,128)(2,1)S(1)}, bf16[128,1920]{1,0:T(8,128)(2,1)}, u32[]{:S(2)}) copy-start(bf16[128,1920]{1,0:T(8,128)(2,1)} %get-tuple-element.21.refs_0_.refs_1_) | copy-start | bytes 1474564
  28.6 1.9 %copy-start.3 = (f32[2304]{0:T(1024)S(1)}, f32[2304]{0:T(1024)}, u32[]{:S(2)}) copy-start(f32[2304]{0:T(1024)} %refs_7_.3) | copy-start | bytes 27652
  28.7 21.7 %collective-permute-start.8 = (bf16[384,1152]{1,0:T(8,128)(2,1)S(1)}, bf16[384,1152]{1,0:T(8,128)(2,1)S(1)}, u32[]{:S(2)}, u32[]{:S(2)}) collective-permute-start(bf16[384,1152]{1,0:T(8,128)(2,1)S(1)} %far_weight.1.refs_5_), channel_id=1, source_target_pairs={{0,2},{1,3},{2,0},{3,1},{4,6},{5,7},{6,4},{7,5},{8,10},{9,11},{10,... | collective-permute-start | bytes 2654216 | tf_op jit(solution)/shard_map/ppermute | solution.py:449
  40.0 15.0 %collective-permute-start.7 = (bf16[384,1152]{1,0:T(8,128)(2,1)S(1)}, bf16[384,1152]{1,0:T(8,128)(2,1)S(1)}, u32[]{:S(2)}, u32[]{:S(2)}) collective-permute-start(bf16[384,1152]{1,0:T(8,128)(2,1)S(1)} %pass_after.2), channel_id=1, source_target_pairs={{0,1},{1,0},{2,3},{3,2},{4,5},{5,4},{6,7},{7,6},{8,9},{9,8},{10,11... | collective-permute-start | bytes 2654216 | tf_op jit(solution)/shard_map/ppermute | solution.py:458
  40.1 14.7 %collective-permute-start.9 = (bf16[128,1152]{1,0:T(8,128)(2,1)S(1)}, bf16[128,1152]{1,0:T(8,128)(2,1)S(1)}, u32[]{:S(2)}, u32[]{:S(2)}) collective-permute-start(bf16[128,1152]{1,0:T(8,128)(2,1)S(1)} %get-tuple-element.23), channel_id=1, source_target_pairs={{4,12},{8,0},{5,13},{9,1},{6,14},{10,2},{7,15},{11,3},{20,28},{24,... | collective-permute-start | bytes 884744 | tf_op jit(solution)/shard_map/ppermute | solution.py:455
  41.4 15.1 %collective-permute-start.11 = (bf16[128,1152]{1,0:T(8,128)(2,1)S(1)}, bf16[128,1152]{1,0:T(8,128)(2,1)S(1)}, u32[]{:S(2)}, u32[]{:S(2)}) collective-permute-start(bf16[128,1152]{1,0:T(8,128)(2,1)S(1)} %get-tuple-element.24), channel_id=1, source_target_pairs={{4,8},{8,4},{5,9},{9,5},{6,10},{10,6},{7,11},{11,7},{20,24},{24,20... | collective-permute-start | bytes 884744 | tf_op jit(solution)/shard_map/ppermute | solution.py:456
  42.1 12.9 %copy-start.6 = (bf16[1,128,1536]{2,1,0:T(8,128)(2,1)S(1)}, bf16[1,128,1536]{2,1,0:T(8,128)(2,1)}, u32[]{:S(2)}) copy-start(bf16[1,128,1536]{2,1,0:T(8,128)(2,1)} %refs_10_.1) | copy-start | bytes 1179652
  42.1 18.8 %collective-permute-start.12 = (bf16[128,1152]{1,0:T(8,128)(2,1)S(1)}, bf16[128,1152]{1,0:T(8,128)(2,1)S(1)}, u32[]{:S(2)}, u32[]{:S(2)}) collective-permute-start(bf16[128,1152]{1,0:T(8,128)(2,1)S(1)} %get-tuple-element.25), channel_id=1, source_target_pairs={{4,0},{8,12},{5,1},{9,13},{6,2},{10,14},{7,3},{11,15},{20,16},{24,... | collective-permute-start | bytes 884744 | tf_op jit(solution)/shard_map/ppermute | solution.py:457
  54.9 5.9 %copy-start.4 = (f32[1536]{0:T(1024)S(1)}, f32[1536]{0:T(1024)}, u32[]{:S(2)}) copy-start(f32[1536]{0:T(1024)} %refs_15_.1) | copy-start | bytes 18436
  55.0 5.9 %collective-permute-start.10 = (bf16[384,1152]{1,0:T(8,128)(2,1)S(1)}, bf16[384,1152]{1,0:T(8,128)(2,1)S(1)}, u32[]{:S(2)}, u32[]{:S(2)}) collective-permute-start(bf16[384,1152]{1,0:T(8,128)(2,1)S(1)} %pass_after.3), channel_id=1, source_target_pairs={{0,1},{1,0},{2,3},{3,2},{4,5},{5,4},{6,7},{7,6},{8,9},{9,8},{10,11... | collective-permute-start | bytes 2654216 | tf_op jit(solution)/shard_map/ppermute | solution.py:461

commit v4 on v3

--- a/solution.py
+++ b/solution.py
@@ -238,8 +238,8 @@
 PAIR = 2 * HEAD_DIM
 
 
-def attention_kernel(pairs, *refs):
-    proj, grads, outs = refs[0], refs[1:5], refs[-4:]
+def attention_kernel(pairs, held, *refs):
+    proj, grads, before, outs = refs[0], refs[1:5], refs[5:-4], refs[-4:]
     total = proj.shape[0]
     tokens = grads[0].shape[0]
     low = lax.broadcasted_iota(jnp.int32, (total, PAIR), 1) < HEAD_DIM
@@ -271,27 +271,42 @@
         query_grad = jnp.concatenate(query_grad, axis=0).T * HEAD_DIM**-0.5
         for part, piece in enumerate((query_grad, key_grad, value_grad)):
             piece = piece.astype(jnp.bfloat16)
-            first = (part * len(pairs) + place) * PAIR
             for i, out in enumerate(outs):
+                whole = out.shape[1] == 3 * HALF
+                first = part * HALF + t * PAIR if whole else (part * len(pairs) + place) * PAIR
                 out[:, first : first + PAIR] = piece[i * tokens : (i + 1) * tokens]
-
-
-def attention_step(proj, grads, pairs, *after):
+    for old, out in zip(before[:3] if held else (), outs):
+        for part in range(3):
+            out[:, part * HALF : part * HALF + held] = old[:, part * held : (part + 1) * held]
+
+
+def attention_step(proj, grads, pairs, before=(), after=()):
     tokens = grads[0].shape[0]
-    out = jax.ShapeDtypeStruct((tokens, 3 * len(pairs) * PAIR), jnp.bfloat16)
-    return pl.pallas_call(
-        functools.partial(attention_kernel, pairs),
-        out_shape=(out,) * 4,
-        in_specs=[spec()] * 5 + [spec()] * len(after),
+    widths = [3 * len(pairs) * PAIR] * 4
+    for i in range(len(before)):
+        widths[i] = 3 * HALF
+    held = before[0].shape[1] // 3 if before else 0
+    return pl.pallas_call(
+        functools.partial(attention_kernel, pairs, held),
+        out_shape=tuple(jax.ShapeDtypeStruct((tokens, width), jnp.bfloat16) for width in widths),
+        in_specs=[spec()] * (5 + len(before) + len(after)),
         out_specs=(spec(),) * 4,
         compiler_params=pltpu.CompilerParams(vmem_limit_bytes=24 * 2**20),
         cost_estimate=cost(12),
         name="attention",
-    )(proj, *grads, *after)
+    )(proj, *grads, *before, *after)
 
 
 def join_halves(weights):
     return [w[...] for w in weights[:3]] + [jnp.concatenate([w[...] for w in weights[3:]], axis=0)]
+
+
+def join_skip(first, second):
+    wide, narrow = first.shape[1] // 3, second.shape[1] // 3
+    pieces = []
+    for part in range(3):
+        pieces += [first[:, part * wide : (part + 1) * wide], second[:, part * narrow : (part + 1) * narrow]]
+    return jnp.concatenate(pieces, axis=1)
 
 
 def on_middle():
@@ -300,30 +315,29 @@
 
 
 def early_kernel(*refs):
-    near_w, far_w = join_halves(refs[0:5]), refs[5:8]
-    own_ref, skip_ref, tokens_ref, sums, normed_out, inverse_out = refs[8:]
+    near_w, far_w = join_halves(refs[0:5]), {0: refs[5], 2: refs[6]}
+    own_ref, skip_first, skip_second, tokens_ref, sums, normed_out, inverse_out = refs[7:]
     middle = on_middle()
     mine = lax.axis_index("weight")
     depth = far_w[0].shape[0]
 
-    def fill(value_ref, weights, far):
-        value = value_ref[...]
+    def fill(value, weights, far):
         for j in range(4):
             at = pl.ds(pl.multiple_of((mine ^ j) * depth, QBLOCK), depth)
-            if j < len(weights):
+            if not far or j in weights:
                 sums[:, at] = dot_last(value, weights[j][...] if far else weights[j])
             else:
                 sums[:, at] = jnp.zeros((value.shape[0], depth), jnp.float32)
 
-    pl.when(middle)(lambda: fill(own_ref, near_w, False))
-    pl.when(jnp.logical_not(middle))(lambda: fill(skip_ref, far_w, True))
+    pl.when(middle)(lambda: fill(own_ref[...], near_w, False))
+    pl.when(jnp.logical_not(middle))(lambda: fill(join_skip(skip_first, skip_second), far_w, True))
     for r in range(0, tokens_ref.shape[1], 16):
         normed, inverse = norm_rows(tokens_ref[0, r : r + 16, :].astype(jnp.float32))
         normed_out[r : r + 16, :] = normed
         inverse_out[r : r + 16, :] = jnp.broadcast_to(inverse, (16, QBLOCK))
 
 
-def early_step(near_w, far_w, own, skip, tokens):
+def early_step(near_w, far_w, own, skips, tokens):
     rows, width = tokens.shape[1:]
     full = jax.ShapeDtypeStruct((rows, width), jnp.float32)
     return pl.pallas_call(
@@ -332,26 +346,50 @@
         in_specs=[spec()] * 11,
         out_specs=(spec(),) * 3,
         compiler_params=pltpu.CompilerParams(vmem_limit_bytes=24 * 2**20),
-        cost_estimate=cost(20),
+        cost_estimate=cost(50),
         name="grad_norm_part",
-    )(*near_w, *far_w, own, skip, tokens)
+    )(*near_w, *far_w, own, *skips, tokens)
+
+
+def pair_part_kernel(pair, skip_first, skip_second, sums, out_ref):
+    mine = lax.axis_index("weight")
+    depth = pair.shape[0] // 2
+    out_ref[...] = sums[...]
+
+    @pl.when(jnp.logical_not(on_middle()))
+    def _():
+        for i, j in enumerate((1, 3)):
+            at = pl.ds(pl.multiple_of((mine ^ j) * depth, QBLOCK), depth)
+            out_ref[:, at] = sums[:, at] + dot_last(
+                join_skip(skip_first, skip_second), pair[i * depth : (i + 1) * depth]
+            )
+
+
+def pair_part_step(pair, skips, sums):
+    return pl.pallas_call(
+        pair_part_kernel,
+        out_shape=jax.ShapeDtypeStruct(sums.shape, sums.dtype),
+        in_specs=[spec()] * 4,
+        out_specs=spec(),
+        compiler_params=pltpu.CompilerParams(vmem_limit_bytes=24 * 2**20),
+        cost_estimate=cost(0.01),
+        name="pair_part",
+    )(pair, *skips, sums)
 
 
 def last_kernel(*refs):
-    near_w, far_w = join_halves(refs[0:5]), refs[5:9]
-    cross_ref, back_ref, skip_ref, sums, normed_ref, inverse_ref, gain_ref, out_ref, grad_norm = refs[9:]
+    near_w, pair = join_halves(refs[0:5]), refs[7]
+    back_ref, cross_ref, sums, normed_ref, inverse_ref, gain_ref, out_ref, grad_norm = refs[8:]
     middle = on_middle()
     mine = lax.axis_index("weight")
-    depth = far_w[0].shape[0]
+    depth = refs[5].shape[0]
+    far_w = (refs[5], pair.at[:depth], refs[6], pair.at[depth:])
 
     def fill(value_ref, weights, far):
         value = value_ref[...]
         for j in range(4):
             at = pl.ds(pl.multiple_of((mine ^ j) * depth, QBLOCK), depth)
-            total = sums[:, at] + dot_last(value, weights[j][...] if far else weights[j])
-            if j == 3 and not far:
-                total += dot_last(skip_ref[...], far_w[3][...])
-            grad_norm[:, at] = total
+            grad_norm[:, at] = sums[:, at] + dot_last(value, weights[j][...] if far else weights[j])
 
     pl.when(middle)(lambda: fill(cross_ref, far_w, True))
     pl.when(jnp.logical_not(middle))(lambda: fill(back_ref, near_w, False))
@@ -364,17 +402,17 @@
         out_ref[0, r : r + 16, :] = inverse_ref[r : r + 16, :1] * (grad_hat - first_mean - normed * second_mean)
 
 
-def last_step(near_w, far_w, cross, back, skip, sums, normed, inverse, gain):
+def last_step(near_w, far_w, back, cross, sums, normed, inverse, gain):
     return pl.pallas_call(
         last_kernel,
         out_shape=jax.ShapeDtypeStruct((1, *normed.shape), jnp.float32),
-        in_specs=[spec()] * 16,
+        in_specs=[spec()] * 14,
         out_specs=spec(),
         scratch_shapes=[VMEM(normed.shape, jnp.float32)],
         compiler_params=pltpu.CompilerParams(vmem_limit_bytes=24 * 2**20),
         cost_estimate=cost(2),
         name="input_grad",
-    )(*near_w, *far_w, cross, back, skip, sums, normed, inverse, gain)
+    )(*near_w, *far_w, back, cross, sums, normed, inverse, gain)
 
 
 def split_kernel(value_ref, upper_ref, lower_ref):
@@ -396,21 +434,22 @@
     )(value)
 
 
-def pass_kernel(value_ref, *refs):
-    refs[-1][...] = value_ref[...]
-
-
-def pass_after(value, *after):
-    return pl.pallas_call(
-        pass_kernel,
-        out_shape=jax.ShapeDtypeStruct(value.shape, value.dtype),
-        in_specs=[spec()] * (1 + len(after)),
+def pair_kernel(first_ref, second_ref, after_ref, out_ref):
+    middle = first_ref.shape[0]
+    out_ref[:middle] = first_ref[...]
+    out_ref[middle:] = second_ref[...]
+
+
+def pair_step(first, second, after):
+    return pl.pallas_call(
+        pair_kernel,
+        out_shape=jax.ShapeDtypeStruct((2 * first.shape[0], first.shape[1]), first.dtype),
+        in_specs=[spec()] * 3,
         out_specs=spec(),
-        input_output_aliases={0: 0},
         compiler_params=pltpu.CompilerParams(vmem_limit_bytes=16 * 2**20),
         cost_estimate=cost(0.01),
-        name="pass_after",
-    )(value, *after)
+        name="chip_weight",
+    )(first, second, after)
 
 
 END_TO_MIDDLE = [(0, 1), (3, 2)]
@@ -451,15 +490,19 @@
     near_w = (near, near_beside, near_across, *near_diagonal)
     proj = project_step(rows[:2], near_w, input_bias)
     proj = project_step(rows[2:], near_w, input_bias, proj)
-    own, end, mid, skip = attention_step(proj, rows, (0, 1, 2))
-    skip = lax.ppermute(skip, "seq", FAR_TO_END)
+    grads = (both_near, both_end, both_mid, both_far)
+    *kept, skip_first = attention_step(proj, grads, (0, 1), after=(far,))
+    skip_first = lax.ppermute(skip_first, "seq", FAR_TO_END)
+    own, end, mid, skip_second = attention_step(proj, grads, (2,), kept)
+    skip_second = lax.ppermute(skip_second, "seq", FAR_TO_END)
     cross = lax.ppermute(mid, "seq", MIDDLE)
     back = lax.ppermute(end, "seq", MIDDLE_TO_END)
-    far_beside = lax.ppermute(pass_after(far, own), "weight", flip(1))
-    far_w = (far, far_beside, far_across)
-    early = early_step(near_w, far_w, own, skip, tokens)
-    far_diagonal = lax.ppermute(pass_after(far_across, skip), "weight", flip(1))
-    return last_step(near_w, (*far_w, far_diagonal), cross, back, skip, *early, norm_gain)
+    far_pair = lax.ppermute(pair_step(far, far_across, skip_second), "weight", flip(1))
+    far_w = (far, far_across)
+    skips = (skip_first, skip_second)
+    sums, normed, inverse = early_step(near_w, far_w, own, skips, tokens)
+    sums = pair_part_step(far_pair, skips, sums)
+    return last_step(near_w, (*far_w, far_pair), back, cross, sums, normed, inverse, norm_gain)
 
 
 def dequantize(codes, scales):

time: 63.9 us -> 60.7 us (0.950)
  waiting for transfers between devices: 27 us -> 22.1 us
  starting transfers between devices: 17.3 us -> 18.6 us
    ppermute x1, waiting for transfers between devices: 6.64 us -> 0.01 us  [local_middle(): far_across = lax.ppermute(far, 'weight', flip(2))]
    ppermute x3, waiting for transfers between devices: 4.36 us -> 8.84 us  [the longest x1 6.39 us: local_middle(): skip_second = lax.ppermute(skip_second, 'seq', FAR_TO_END)]
    ppermute x1, waiting for transfers between devices: 4.36 us -> 1.61 us  [local_middle(): back = lax.ppermute(end, 'seq', MIDDLE_TO_END)]
    ppermute x3, starting transfers between devices: 1.43 us -> 2.66 us  [the longest x1 1.29 us: local_middle(): skip_first = lax.ppermute(skip_first, 'seq', FAR_TO_END)]
    pallas_call x3 -> x4, Pallas kernels: 6.78 us -> 7.86 us  [the longest x2 7.03 us: attention_step(): pl.pallas_call(functools.partial(attention_kernel, pairs, held), out_shap...]
  transfers between devices with their start and end apart: 13 -> 13, of which waited for: 4 -> 4; matrix products, arithmetic and copies ran while one was open for 0% -> 0% of each run, Pallas kernels for 19% -> 21%
where the time goes in v4:
time: 60.7 us; the launch traced here: 60.5 us
  waiting for transfers between devices  22.1 us (36%)
  Pallas kernels  19.5 us (32%)
  starting transfers between devices  18.6 us (31%)
    ppermute x1, waiting for transfers between devices, local_middle(): near_across = lax.ppermute(near, 'weight', flip(2))  11.6 us
    pallas_call x2, Pallas kernels, attention_step(): pl.pallas_call(functools.partial(attention_kernel, pairs, held), out_shap...  7.03 us
    ppermute x1, waiting for transfers between devices, local_middle(): skip_second = lax.ppermute(skip_second, 'seq', FAR_TO_END)  6.39 us
    pallas_call x1, Pallas kernels, first_step(): pl.pallas_call(first_kernel, out_shape=(jax.ShapeDtypeStruct((depth, 3 *...  4.22 us
    ppermute x1, starting transfers between devices, local_middle(): both_far = lax.ppermute(both_other, 'seq', END_TO_FAR)  3.97 us
    ppermute x1, starting transfers between devices, local_middle(): both_end = lax.ppermute(both_near, 'seq', END_TO_MIDDLE)  3.5 us
    ppermute x1, starting transfers between devices, local_middle(): near_across = lax.ppermute(near, 'weight', flip(2))  3.02 us
    pallas_call x2, Pallas kernels, project_step(): pl.pallas_call(functools.partial(project_kernel, first), out_shape=jax.Sh...  2.81 us
  transfers between devices with their start and end apart: 13, of which 4 were waited for; matrix products, arithmetic and copies ran while one was open for 0% of the time, Pallas kernels for 21%

profile of v4, /device:TPU:0, one launch (start us, length us, event | category | flops | bytes accessed | tf_op | source)
XLA Modules:
  0.0 60.5 jit_solution(7712198574160133569)
XLA Ops:
  0.0 4.2 %first_weights_and_rows.1 = (bf16[384,1152]{1,0:T(8,128)(2,1)}, bf16[128,1920]{1,0:T(8,128)(2,1)}, bf16[128,1920]{1,0:T(8,128)(2,1)}) custom-call(bf16[1,128,1536]{2,1,0:T(8,128)(2,1)} %refs_10_.1, f32[1536]{0:T(1024)} %refs_13_.1, f32[1536]{0:T(1024)} %shift_ref.1, f32[3,18]{1,0:T(4,128)} %scales_ref.3, bf16[384,2304]{1,0:T(8,128)(2,1)} %codes_ref.3, ...), custom_call_target="tpu_custom_call" | custom-call | flops 3000000000 | bytes 9000000 | tf_op jit(solution)/shard_map/first_weights_and_rows/pallas_call | solution.py:118
  4.2 3.0 %collective-permute-start.1 = (bf16[384,1152]{1,0:T(8,128)(2,1)}, bf16[384,1152]{1,0:T(8,128)(2,1)S(1)}, u32[]{:S(2)}, u32[]{:S(2)}) collective-permute-start(bf16[384,1152]{1,0:T(8,128)(2,1)} %get-tuple-element.21.refs_2_.refs_0_), channel_id=1, source_target_pairs={{0,2},{1,3},{2,0},{3,1},{4,6},{5,7},{6,4},{7,5},{8,10},{9,11},{10,... | collective-permute-start | bytes 2654216 | tf_op jit(solution)/shard_map/ppermute | solution.py:484
  7.3 3.5 %collective-permute-start.7 = (bf16[128,1920]{1,0:T(8,128)(2,1)}, bf16[128,1920]{1,0:T(8,128)(2,1)S(1)}, u32[]{:S(2)}, u32[]{:S(2)}) collective-permute-start(bf16[128,1920]{1,0:T(8,128)(2,1)} %get-tuple-element.25.refs_0_.refs_1_), channel_id=1, source_target_pairs={{0,4},{12,8},{1,5},{13,9},{2,6},{14,10},{3,7},{15,11},{16,20},{28,... | collective-permute-start | bytes 1474568 | tf_op jit(solution)/shard_map/ppermute | solution.py:483
  10.8 0.1 collective-permute-start
  10.8 0.7 %collective-permute-start.5 = (bf16[128,1920]{1,0:T(8,128)(2,1)}, bf16[128,1920]{1,0:T(8,128)(2,1)S(1)}, u32[]{:S(2)}, u32[]{:S(2)}) collective-permute-start(bf16[128,1920]{1,0:T(8,128)(2,1)} %get-tuple-element.24), channel_id=1, source_target_pairs={{4,8},{8,4},{5,9},{9,5},{6,10},{10,6},{7,11},{11,7},{20,24},{24,20... | collective-permute-start | bytes 1474568 | tf_op jit(solution)/shard_map/ppermute | solution.py:481
  11.5 4.0 %collective-permute-start.6 = (bf16[128,1920]{1,0:T(8,128)(2,1)}, bf16[128,1920]{1,0:T(8,128)(2,1)S(1)}, u32[]{:S(2)}, u32[]{:S(2)}) collective-permute-start(bf16[128,1920]{1,0:T(8,128)(2,1)} %get-tuple-element.24), channel_id=1, source_target_pairs={{0,8},{12,4},{1,9},{13,5},{2,10},{14,6},{3,11},{15,7},{16,24},{28,... | collective-permute-start | bytes 1474568 | tf_op jit(solution)/shard_map/ppermute | solution.py:482
  15.5 11.6 %collective-permute-done.1.value_ref.after_ref.refs_4_.refs_2_ = bf16[384,1152]{1,0:T(8,128)(2,1)S(1)} collective-permute-done((bf16[384,1152]{1,0:T(8,128)(2,1)}, bf16[384,1152]{1,0:T(8,128)(2,1)S(1)}, u32[]{:S(2)}, u32[]{:S(2)}) %collective-permute-start.1) | collective-permute-done | bytes 884768 | tf_op jit(solution)/shard_map/ppermute | solution.py:484
  27.1 0.1 split_rows.1
  27.2 0.1 collective-permute-start.2
  27.3 0.0 copy-start.2
  27.3 0.0 copy-start.3
  27.3 0.5 collective-permute-start.3
  27.8 0.8 %far_weight.1.refs_5_.first_ref = bf16[384,1152]{1,0:T(8,128)(2,1)S(1)} custom-call(f32[3,18]{1,0:T(4,128)S(1)} %copy-done.5, bf16[384,2304]{1,0:T(8,128)(2,1)S(1)} %copy-done.1, bf16[384,1152]{1,0:T(8,128)(2,1)S(1)} %collective-permute-done.1.value_ref.after_ref.refs_4_.refs_2_), custom_call_target="tpu_custom_call" | custom-call | flops 10000000 | bytes 30000 | tf_op jit(solution)/shard_map/far_weight/pallas_call | solution.py:166
  28.6 1.8 %collective-permute-start.4 = (bf16[384,1152]{1,0:T(8,128)(2,1)S(1)}, bf16[384,1152]{1,0:T(8,128)(2,1)S(1)}, u32[]{:S(2)}, u32[]{:S(2)}) collective-permute-start(bf16[384,1152]{1,0:T(8,128)(2,1)S(1)} %far_weight.1.refs_5_.first_ref), channel_id=1, source_target_pairs={{0,2},{1,3},{2,0},{3,1},{4,6},{5,7},{6,4},{7,5},{8,10},{9,11},{10,... | collective-permute-start | bytes 2654216 | tf_op jit(solution)/shard_map/ppermute | solution.py:488
  30.5 1.4 %projection.2.refs_8_ = bf16[512,1152]{1,0:T(8,128)(2,1)S(1)} custom-call(bf16[128,1920]{1,0:T(8,128)(2,1)S(1)} %copy-done.2, bf16[128,1920]{1,0:T(8,128)(2,1)S(1)} %collective-permute-done.7.refs_1_.refs_2_, bf16[384,1152]{1,0:T(8,128)(2,1)S(1)} %copy-done, bf16[384,1152]{1,0:T(8,128)(2,1)S(1)} %collective-permute-done.refs_3_.refs_1_, ...), custom_call_target="tpu_custom_call" | custom-call | flops 10000000 | bytes 30000 | tf_op jit(solution)/shard_map/projection/pallas_call | solution.py:226
  31.9 1.4 %projection.3.refs_0_ = bf16[512,1152]{1,0:T(8,128)(2,1)S(1)} custom-call(bf16[128,1920]{1,0:T(8,128)(2,1)S(1)} %collective-permute-done.5.refs_0_.refs_3_, bf16[128,1920]{1,0:T(8,128)(2,1)S(1)} %collective-permute-done.6.refs_1_.refs_4_, bf16[384,1152]{1,0:T(8,128)(2,1)S(1)} %copy-done, ...), custom_call_target="tpu_custom_call", output_to_operand_aliasing={{}: (8, {})} | custom-call | flops 10000000 | bytes 30000 | tf_op jit(solution)/shard_map/projection/pallas_call | solution.py:226
  33.3 4.5 %attention.2 = (bf16[128,768]{1,0:T(8,128)(2,1)S(1)}, bf16[128,768]{1,0:T(8,128)(2,1)S(1)}, bf16[128,768]{1,0:T(8,128)(2,1)S(1)}, bf16[128,768]{1,0:T(8,128)(2,1)S(1)}) custom-call(bf16[512,1152]{1,0:T(8,128)(2,1)S(1)} %projection.3.refs_0_, bf16[128,1920]{1,0:T(8,128)(2,1)S(1)} %copy-done.2, bf16[128,1920]{1,0:T(8,128)(2,1)S(1)} %collective-permute-done.7.refs_1_.refs_2_, ...), custom_call_target="tpu_custom_call" | custom-call | flops 12000000000 | bytes 36000000 | tf_op jit(solution)/shard_map/attention/pallas_call | solution.py:289
  37.8 1.3 %collective-permute-start.12 = (bf16[128,768]{1,0:T(8,128)(2,1)S(1)}, bf16[128,768]{1,0:T(8,128)(2,1)S(1)}, u32[]{:S(2)}, u32[]{:S(2)}) collective-permute-start(bf16[128,768]{1,0:T(8,128)(2,1)S(1)} %get-tuple-element.32), channel_id=1, source_target_pairs={{4,12},{8,0},{5,13},{9,1},{6,14},{10,2},{7,15},{11,3},{20,28},{24,... | collective-permute-start | bytes 589832 | tf_op jit(solution)/shard_map/ppermute | solution.py:495
  39.1 2.5 %attention.3 = (bf16[128,1152]{1,0:T(8,128)(2,1)S(1)}, bf16[128,1152]{1,0:T(8,128)(2,1)S(1)}, bf16[128,1152]{1,0:T(8,128)(2,1)S(1)}, bf16[128,384]{1,0:T(8,128)(2,1)S(1)}) custom-call(bf16[512,1152]{1,0:T(8,128)(2,1)S(1)} %projection.3.refs_0_, bf16[128,1920]{1,0:T(8,128)(2,1)S(1)} %copy-done.2, ...), custom_call_target="tpu_custom_call" | custom-call | flops 12000000000 | bytes 36000000 | tf_op jit(solution)/shard_map/attention/pallas_call | solution.py:289
  41.7 1.3 %collective-permute-start.8 = (bf16[128,384]{1,0:T(8,128)(2,1)S(1)}, bf16[128,384]{1,0:T(8,128)(2,1)S(1)}, u32[]{:S(2)}, u32[]{:S(2)}) collective-permute-start(bf16[128,384]{1,0:T(8,128)(2,1)S(1)} %get-tuple-element.29), channel_id=1, source_target_pairs={{4,12},{8,0},{5,13},{9,1},{6,14},{10,2},{7,15},{11,3},{20,28},{24,... | collective-permute-start | bytes 294920 | tf_op jit(solution)/shard_map/ppermute | solution.py:497
  43.0 1.3 %collective-permute-start.10 = (bf16[128,1152]{1,0:T(8,128)(2,1)S(1)}, bf16[128,1152]{1,0:T(8,128)(2,1)S(1)}, u32[]{:S(2)}, u32[]{:S(2)}) collective-permute-start(bf16[128,1152]{1,0:T(8,128)(2,1)S(1)} %get-tuple-element.30), channel_id=1, source_target_pairs={{4,0},{8,12},{5,1},{9,13},{6,2},{10,14},{7,3},{11,15},{20,16},{24,... | collective-permute-start | bytes 884744 | tf_op jit(solution)/shard_map/ppermute | solution.py:499
  44.3 0.0 copy-start.6
  44.3 1.0 %collective-permute-start.11 = (bf16[128,1152]{1,0:T(8,128)(2,1)S(1)}, bf16[128,1152]{1,0:T(8,128)(2,1)S(1)}, u32[]{:S(2)}, u32[]{:S(2)}) collective-permute-start(bf16[128,1152]{1,0:T(8,128)(2,1)S(1)} %get-tuple-element.31), channel_id=1, source_target_pairs={{4,8},{8,4},{5,9},{9,5},{6,10},{10,6},{7,11},{11,7},{20,24},{24,20... | collective-permute-start | bytes 884744 | tf_op jit(solution)/shard_map/ppermute | solution.py:498
  45.3 6.4 %collective-permute-done.8.after_ref.refs_9_.skip_second = bf16[128,384]{1,0:T(8,128)(2,1)S(1)} collective-permute-done((bf16[128,384]{1,0:T(8,128)(2,1)S(1)}, bf16[128,384]{1,0:T(8,128)(2,1)S(1)}, u32[]{:S(2)}, u32[]{:S(2)}) %collective-permute-start.8) | collective-permute-done | bytes 98336 | tf_op jit(solution)/shard_map/ppermute | solution.py:497
  51.7 0.0 collective-permute-done.4.second_ref.refs_6_
  51.7 0.1 chip_weight.1
  51.8 0.1 collective-permute-start.9
  51.9 1.2 %grad_norm_part.1 = (f32[128,1536]{1,0:T(8,128)S(1)}, f32[128,1536]{1,0:T(8,128)S(1)}, f32[128,128]{1,0:T(8,128)S(1)}) custom-call(bf16[384,1152]{1,0:T(8,128)(2,1)S(1)} %copy-done, bf16[384,1152]{1,0:T(8,128)(2,1)S(1)} %collective-permute-done.refs_3_.refs_1_, bf16[384,1152]{1,0:T(8,128)(2,1)S(1)} %collective-permute-done.1.value_ref.after_ref.refs_4_.refs_2_, ...), custom_call_target="tpu_custom_call" | custom-call | flops 49999998976 | bytes 150000000 | tf_op jit(solution)/shard_map/grad_norm_part/pallas_call | solution.py:343
  53.1 2.4 %collective-permute-done.9.pair.refs_7_ = bf16[768,1152]{1,0:T(8,128)(2,1)S(1)} collective-permute-done((bf16[768,1152]{1,0:T(8,128)(2,1)S(1)}, bf16[768,1152]{1,0:T(8,128)(2,1)S(1)}, u32[]{:S(2)}, u32[]{:S(2)}) %collective-permute-start.9) | collective-permute-done | bytes 1769504 | tf_op jit(solution)/shard_map/ppermute | solution.py:500
  55.6 0.7 %pair_part.1.refs_10_ = f32[128,1536]{1,0:T(8,128)S(1)} custom-call(bf16[768,1152]{1,0:T(8,128)(2,1)S(1)} %collective-permute-done.9.pair.refs_7_, bf16[128,768]{1,0:T(8,128)(2,1)S(1)} %collective-permute-done.12.refs_8_.skip_first, bf16[128,384]{1,0:T(8,128)(2,1)S(1)} %collective-permute-done.8.after_ref.refs_9_.skip_second, ...), custom_call_target="tpu_custom_call" | custom-call | flops 10000000 | bytes 30000 | tf_op jit(solution)/shard_map/pair_part/pallas_call | solution.py:369
  56.3 1.6 %collective-permute-done.10.refs_8_ = bf16[128,1152]{1,0:T(8,128)(2,1)S(1)} collective-permute-done((bf16[128,1152]{1,0:T(8,128)(2,1)S(1)}, bf16[128,1152]{1,0:T(8,128)(2,1)S(1)}, u32[]{:S(2)}, u32[]{:S(2)}) %collective-permute-start.10) | collective-permute-done | bytes 294944 | tf_op jit(solution)/shard_map/ppermute | solution.py:499
  57.9 2.6 %input_grad.1 = f32[1,128,1536]{2,1,0:T(8,128)} custom-call(bf16[384,1152]{1,0:T(8,128)(2,1)S(1)} %copy-done, bf16[384,1152]{1,0:T(8,128)(2,1)S(1)} %collective-permute-done.refs_3_.refs_1_, bf16[384,1152]{1,0:T(8,128)(2,1)S(1)} %collective-permute-done.1.value_ref.after_ref.refs_4_.refs_2_, bf16[192,1152]{1,0:T(8,128)(2,1)S(1)} %collective-permute-done.2.refs_5_.refs_3_, ...), custom_call_target="tpu_custom_call" | custom-call | flops 2000000000 | bytes 6000000 | tf_op jit(solution)/shard_map/input_grad/pallas_call | solution.py:406
  (19 shorter events, 0.0 us)
Async XLA Ops:
  0.0 27.8 %copy-start.5 = (f32[3,18]{1,0:T(4,128)S(1)}, f32[3,18]{1,0:T(4,128)}, u32[]{:S(2)}) copy-start(f32[3,18]{1,0:T(4,128)} %scales_ref.3) | copy-start | bytes 652
  0.0 27.8 %copy-start.1 = (bf16[384,2304]{1,0:T(8,128)(2,1)S(1)}, bf16[384,2304]{1,0:T(8,128)(2,1)}, u32[]{:S(2)}) copy-start(bf16[384,2304]{1,0:T(8,128)(2,1)} %codes_ref.3) | copy-start | bytes 5308420
  4.2 22.9 %collective-permute-start.1 = (bf16[384,1152]{1,0:T(8,128)(2,1)}, bf16[384,1152]{1,0:T(8,128)(2,1)S(1)}, u32[]{:S(2)}, u32[]{:S(2)}) collective-permute-start(bf16[384,1152]{1,0:T(8,128)(2,1)} %get-tuple-element.21.refs_2_.refs_0_), channel_id=1, source_target_pairs={{0,2},{1,3},{2,0},{3,1},{4,6},{5,7},{6,4},{7,5},{8,10},{9,11},{10,... | collective-permute-start | bytes 2654216 | tf_op jit(solution)/shard_map/ppermute | solution.py:484
  7.3 20.0 %collective-permute-start.7 = (bf16[128,1920]{1,0:T(8,128)(2,1)}, bf16[128,1920]{1,0:T(8,128)(2,1)S(1)}, u32[]{:S(2)}, u32[]{:S(2)}) collective-permute-start(bf16[128,1920]{1,0:T(8,128)(2,1)} %get-tuple-element.25.refs_0_.refs_1_), channel_id=1, source_target_pairs={{0,4},{12,8},{1,5},{13,9},{2,6},{14,10},{3,7},{15,11},{16,20},{28,... | collective-permute-start | bytes 1474568 | tf_op jit(solution)/shard_map/ppermute | solution.py:483
  10.8 17.9 %collective-permute-start = (bf16[384,1152]{1,0:T(8,128)(2,1)}, bf16[384,1152]{1,0:T(8,128)(2,1)S(1)}, u32[]{:S(2)}, u32[]{:S(2)}) collective-permute-start(bf16[384,1152]{1,0:T(8,128)(2,1)} %get-tuple-element.21.refs_2_.refs_0_), channel_id=1, source_target_pairs={{0,1},{1,0},{2,3},{3,2},{4,5},{5,4},{6,7},{7,6},{8,9},{9,8},{10,11... | collective-permute-start | bytes 2654216 | tf_op jit(solution)/shard_map/ppermute | solution.py:485
  10.8 21.0 %collective-permute-start.5 = (bf16[128,1920]{1,0:T(8,128)(2,1)}, bf16[128,1920]{1,0:T(8,128)(2,1)S(1)}, u32[]{:S(2)}, u32[]{:S(2)}) collective-permute-start(bf16[128,1920]{1,0:T(8,128)(2,1)} %get-tuple-element.24), channel_id=1, source_target_pairs={{4,8},{8,4},{5,9},{9,5},{6,10},{10,6},{7,11},{11,7},{20,24},{24,20... | collective-permute-start | bytes 1474568 | tf_op jit(solution)/shard_map/ppermute | solution.py:481
  11.5 20.4 %collective-permute-start.6 = (bf16[128,1920]{1,0:T(8,128)(2,1)}, bf16[128,1920]{1,0:T(8,128)(2,1)S(1)}, u32[]{:S(2)}, u32[]{:S(2)}) collective-permute-start(bf16[128,1920]{1,0:T(8,128)(2,1)} %get-tuple-element.24), channel_id=1, source_target_pairs={{0,8},{12,4},{1,9},{13,5},{2,10},{14,6},{3,11},{15,7},{16,24},{28,... | collective-permute-start | bytes 1474568 | tf_op jit(solution)/shard_map/ppermute | solution.py:482
  27.2 3.3 %collective-permute-start.2 = (bf16[192,1152]{1,0:T(8,128)(2,1)S(1)}, bf16[192,1152]{1,0:T(8,128)(2,1)S(1)}, u32[]{:S(2)}, u32[]{:S(2)}) collective-permute-start(bf16[192,1152]{1,0:T(8,128)(2,1)S(1)} %get-tuple-element.22), channel_id=1, source_target_pairs={{0,1},{1,0},{2,3},{3,2},{4,5},{5,4},{6,7},{7,6},{8,9},{9,8},{10,11... | collective-permute-start | bytes 1327112 | tf_op jit(solution)/shard_map/ppermute | solution.py:486
  27.3 3.2 %copy-start = (bf16[384,1152]{1,0:T(8,128)(2,1)S(1)}, bf16[384,1152]{1,0:T(8,128)(2,1)}, u32[]{:S(2)}) copy-start(bf16[384,1152]{1,0:T(8,128)(2,1)} %get-tuple-element.21.refs_2_.refs_0_) | copy-start | bytes 2654212
  27.3 3.2 %copy-start.2 = (bf16[128,1920]{1,0:T(8,128)(2,1)S(1)}, bf16[128,1920]{1,0:T(8,128)(2,1)}, u32[]{:S(2)}) copy-start(bf16[128,1920]{1,0:T(8,128)(2,1)} %get-tuple-element.25.refs_0_.refs_1_) | copy-start | bytes 1474564
  27.3 3.2 %copy-start.3 = (f32[2304]{0:T(1024)S(1)}, f32[2304]{0:T(1024)}, u32[]{:S(2)}) copy-start(f32[2304]{0:T(1024)} %refs_7_.3) | copy-start | bytes 27652
  27.3 3.1 %collective-permute-start.3 = (bf16[192,1152]{1,0:T(8,128)(2,1)S(1)}, bf16[192,1152]{1,0:T(8,128)(2,1)S(1)}, u32[]{:S(2)}, u32[]{:S(2)}) collective-permute-start(bf16[192,1152]{1,0:T(8,128)(2,1)S(1)} %get-tuple-element.23), channel_id=1, source_target_pairs={{0,1},{1,0},{2,3},{3,2},{4,5},{5,4},{6,7},{7,6},{8,9},{9,8},{10,11... | collective-permute-start | bytes 1327112 | tf_op jit(solution)/shard_map/ppermute | solution.py:486
  28.6 23.0 %collective-permute-start.4 = (bf16[384,1152]{1,0:T(8,128)(2,1)S(1)}, bf16[384,1152]{1,0:T(8,128)(2,1)S(1)}, u32[]{:S(2)}, u32[]{:S(2)}) collective-permute-start(bf16[384,1152]{1,0:T(8,128)(2,1)S(1)} %far_weight.1.refs_5_.first_ref), channel_id=1, source_target_pairs={{0,2},{1,3},{2,0},{3,1},{4,6},{5,7},{6,4},{7,5},{8,10},{9,11},{10,... | collective-permute-start | bytes 2654216 | tf_op jit(solution)/shard_map/ppermute | solution.py:488
  37.8 14.0 %collective-permute-start.12 = (bf16[128,768]{1,0:T(8,128)(2,1)S(1)}, bf16[128,768]{1,0:T(8,128)(2,1)S(1)}, u32[]{:S(2)}, u32[]{:S(2)}) collective-permute-start(bf16[128,768]{1,0:T(8,128)(2,1)S(1)} %get-tuple-element.32), channel_id=1, source_target_pairs={{4,12},{8,0},{5,13},{9,1},{6,14},{10,2},{7,15},{11,3},{20,28},{24,... | collective-permute-start | bytes 589832 | tf_op jit(solution)/shard_map/ppermute | solution.py:495
  41.7 10.0 %collective-permute-start.8 = (bf16[128,384]{1,0:T(8,128)(2,1)S(1)}, bf16[128,384]{1,0:T(8,128)(2,1)S(1)}, u32[]{:S(2)}, u32[]{:S(2)}) collective-permute-start(bf16[128,384]{1,0:T(8,128)(2,1)S(1)} %get-tuple-element.29), channel_id=1, source_target_pairs={{4,12},{8,0},{5,13},{9,1},{6,14},{10,2},{7,15},{11,3},{20,28},{24,... | collective-permute-start | bytes 294920 | tf_op jit(solution)/shard_map/ppermute | solution.py:497
  43.0 14.9 %collective-permute-start.10 = (bf16[128,1152]{1,0:T(8,128)(2,1)S(1)}, bf16[128,1152]{1,0:T(8,128)(2,1)S(1)}, u32[]{:S(2)}, u32[]{:S(2)}) collective-permute-start(bf16[128,1152]{1,0:T(8,128)(2,1)S(1)} %get-tuple-element.30), channel_id=1, source_target_pairs={{4,0},{8,12},{5,1},{9,13},{6,2},{10,14},{7,3},{11,15},{20,16},{24,... | collective-permute-start | bytes 884744 | tf_op jit(solution)/shard_map/ppermute | solution.py:499
  44.3 7.6 %copy-start.6 = (bf16[1,128,1536]{2,1,0:T(8,128)(2,1)S(1)}, bf16[1,128,1536]{2,1,0:T(8,128)(2,1)}, u32[]{:S(2)}) copy-start(bf16[1,128,1536]{2,1,0:T(8,128)(2,1)} %refs_10_.1) | copy-start | bytes 1179652
  44.3 13.6 %collective-permute-start.11 = (bf16[128,1152]{1,0:T(8,128)(2,1)S(1)}, bf16[128,1152]{1,0:T(8,128)(2,1)S(1)}, u32[]{:S(2)}, u32[]{:S(2)}) collective-permute-start(bf16[128,1152]{1,0:T(8,128)(2,1)S(1)} %get-tuple-element.31), channel_id=1, source_target_pairs={{4,8},{8,4},{5,9},{9,5},{6,10},{10,6},{7,11},{11,7},{20,24},{24,20... | collective-permute-start | bytes 884744 | tf_op jit(solution)/shard_map/ppermute | solution.py:498
  51.8 3.8 %collective-permute-start.9 = (bf16[768,1152]{1,0:T(8,128)(2,1)S(1)}, bf16[768,1152]{1,0:T(8,128)(2,1)S(1)}, u32[]{:S(2)}, u32[]{:S(2)}) collective-permute-start(bf16[768,1152]{1,0:T(8,128)(2,1)S(1)} %chip_weight.1), channel_id=1, source_target_pairs={{0,1},{1,0},{2,3},{3,2},{4,5},{5,4},{6,7},{7,6},{8,9},{9,8},{10,11... | collective-permute-start | bytes 5308424 | tf_op jit(solution)/shard_map/ppermute | solution.py:500
  55.5 2.3 %copy-start.4 = (f32[1536]{0:T(1024)S(1)}, f32[1536]{0:T(1024)}, u32[]{:S(2)}) copy-start(f32[1536]{0:T(1024)} %refs_13_.1) | copy-start | bytes 18436

commit v5 on v4

--- a/solution.py
+++ b/solution.py
@@ -49,7 +49,7 @@
 def first_kernel(
     tokens_ref, gain_ref, shift_ref, scales_ref, codes_ref, grad_ref, layer_ref, out_scales_ref, out_codes_ref,
     weight_out, near_out, far_out,
-    tokens, gain, shift, scales, codes, grad, layer, out_scales, out_codes, scaled, weight, sems
+    tokens, gain, shift, scales, codes, grad, layer, out_scales, out_codes, scaled, weight, far, sems
 ):
     half = half_index()
     other = 1 - half
@@ -96,12 +96,12 @@
         normed, _ = norm_rows(tokens[0, r : r + 16, :].astype(jnp.float32))
         norm_out = (normed * gain_row + shift_row).astype(jnp.bfloat16)
         near_out[r : r + 16, :width] = norm_out
-        far_out[r : r + 16, :width] = norm_out
+        far[r : r + 16, :width] = norm_out
 
     for started in grad_copies:
         started.wait()
     scaled[...] = (grad[0].astype(jnp.float32) * row_vector(layer)).astype(jnp.bfloat16)
-    for i, (out_ref, which) in enumerate(((far_out, other), (near_out, half))):
+    for i, (out_ref, which) in enumerate(((far, other), (near_out, half))):
         out_copies[i].wait()
         for r in range(blocks):
             lines = slice(r * QBLOCK, (r + 1) * QBLOCK)
@@ -109,17 +109,23 @@
                 at = slice(c * QBLOCK, (c + 1) * QBLOCK)
                 weight[lines, at] = scale_block(out_codes[i, lines, at], out_scales[which * blocks + r, c])
         out_ref[:, width:] = dot_last(scaled[...], weight[...]).astype(jnp.bfloat16)
+        if out_ref is far:
+            far_copy = copy(far, far_out, 12)
+    far_copy.wait()
 
 
 def first_step(tokens, gain, shift, scales, codes, grad, layer_scale, out_scales, out_codes):
     lines, width = tokens.shape[1:]
     depth = codes.shape[0]
-    both = jax.ShapeDtypeStruct((lines, width + HALF), jnp.bfloat16)
     return pl.pallas_call(
         first_kernel,
-        out_shape=(jax.ShapeDtypeStruct((depth, 3 * HALF), jnp.bfloat16), both, both),
+        out_shape=(
+            VMEM((depth, 3 * HALF), jnp.bfloat16),
+            VMEM((lines, width + HALF), jnp.bfloat16),
+            jax.ShapeDtypeStruct((lines, width + HALF), jnp.bfloat16),
+        ),
         in_specs=[spec(pltpu.HBM)] * 9,
-        out_specs=(spec(),) * 3,
+        out_specs=(spec(), spec(), spec(pltpu.HBM)),
         scratch_shapes=[
             VMEM(tokens.shape, tokens.dtype),
             VMEM(gain.shape, gain.dtype),
@@ -132,7 +138,8 @@
             VMEM((2, HALF, width), out_codes.dtype),
             VMEM((lines, width), jnp.bfloat16),
             VMEM((HALF, width), jnp.bfloat16),
-            pltpu.SemaphoreType.DMA((12,)),
+            VMEM((lines, width + HALF), jnp.bfloat16),
+            pltpu.SemaphoreType.DMA((13,)),
         ],
         compiler_params=pltpu.CompilerParams(vmem_limit_bytes=60 * 2**20),
         cost_estimate=cost(3),
@@ -238,43 +245,71 @@
 PAIR = 2 * HEAD_DIM
 
 
+def soft_part(scores, dprob):
+    expo = jnp.exp(scores - jnp.max(scores, axis=0, keepdims=True))
+    scale = 1.0 / jnp.sum(expo, axis=0, keepdims=True)
+    delta = jnp.sum(expo * dprob, axis=0, keepdims=True) * scale
+    prob = (expo * scale).astype(jnp.bfloat16)
+    return prob, prob * (dprob - delta).astype(jnp.bfloat16)
+
+
 def attention_kernel(pairs, held, *refs):
     proj, grads, before, outs = refs[0], refs[1:5], refs[5:-4], refs[-4:]
     total = proj.shape[0]
     tokens = grads[0].shape[0]
     low = lax.broadcasted_iota(jnp.int32, (total, PAIR), 1) < HEAD_DIM
     zero = jnp.zeros((total, PAIR), jnp.bfloat16)
-    for place, t in enumerate(pairs):
-        query = proj[:, t * PAIR : (t + 1) * PAIR]
-        key = proj[:, HALF + t * PAIR : HALF + (t + 1) * PAIR]
-        value = proj[:, 2 * HALF + t * PAIR : 2 * HALF + (t + 1) * PAIR]
+
+    def load(t):
+        query, key, value = (proj[:, part * HALF + t * PAIR : part * HALF + (t + 1) * PAIR] for part in range(3))
         grad = jnp.concatenate(
             [g[:, g.shape[1] - HALF + t * PAIR : g.shape[1] - HALF + (t + 1) * PAIR] for g in grads], axis=0
         )
-        key_t = key.T
-        key_grad = value_grad = None
-        query_grad = []
-        for side in range(2):
-            mask = low if side == 0 else ~low
-            scores = dot_last(jnp.where(mask, key, zero), query)
-            dprob = dot_last(jnp.where(mask, value, zero), grad)
-            expo = jnp.exp(scores - jnp.max(scores, axis=0, keepdims=True))
-            scale = 1.0 / jnp.sum(expo, axis=0, keepdims=True)
-            delta = jnp.sum(expo * dprob, axis=0, keepdims=True) * scale
-            prob = expo * scale
-            dscore = (prob * (dprob - delta)).astype(jnp.bfloat16)
-            key_part = dot_plain(dscore, jnp.where(mask, query, zero))
-            value_part = dot_plain(prob.astype(jnp.bfloat16), jnp.where(mask, grad, zero))
-            key_grad = key_part if side == 0 else key_grad + key_part
-            value_grad = value_part if side == 0 else value_grad + value_part
-            query_grad.append(dot_plain(key_t[side * HEAD_DIM : (side + 1) * HEAD_DIM], dscore))
-        query_grad = jnp.concatenate(query_grad, axis=0).T * HEAD_DIM**-0.5
-        for part, piece in enumerate((query_grad, key_grad, value_grad)):
+        return query, key, value, grad
+
+    def mask(side, value):
+        return jnp.where(low, value, zero) if side == 0 else jnp.where(low, zero, value)
+
+    def before_soft(t, side):
+        query, key, value, grad = load(t)
+        return dot_last(mask(side, key), query), dot_last(mask(side, value), grad)
+
+    def after_soft(t, side, prob, dscore):
+        query, key, _, grad = load(t)
+        key_t = key.T[side * HEAD_DIM : (side + 1) * HEAD_DIM]
+        return (
+            dot_plain(key_t, dscore),
+            dot_plain(dscore, mask(side, query)),
+            dot_plain(prob, mask(side, grad)),
+        )
+
+    def store(t, first, second):
+        place = pairs.index(t)
+        query_grad = jnp.concatenate([first[0], second[0]], axis=0).T * HEAD_DIM**-0.5
+        for part, piece in enumerate((query_grad, first[1] + second[1], first[2] + second[2])):
             piece = piece.astype(jnp.bfloat16)
             for i, out in enumerate(outs):
                 whole = out.shape[1] == 3 * HALF
-                first = part * HALF + t * PAIR if whole else (part * len(pairs) + place) * PAIR
-                out[:, first : first + PAIR] = piece[i * tokens : (i + 1) * tokens]
+                at = part * HALF + t * PAIR if whole else (part * len(pairs) + place) * PAIR
+                out[:, at : at + PAIR] = piece[i * tokens : (i + 1) * tokens]
+
+    heads = [(t, side) for t in pairs for side in range(2)]
+    done = {}
+
+    def finish(t, side, *soft):
+        done[t, side] = after_soft(t, side, *soft)
+        if side == 1:
+            store(t, done[t, 0], done[t, 1])
+
+    ready, behind = before_soft(*heads[0]), None
+    for i, head in enumerate(heads):
+        now = ready
+        if i + 1 < len(heads):
+            ready = before_soft(*heads[i + 1])
+        if behind is not None:
+            finish(*behind)
+        behind = (*head, *soft_part(*now))
+    finish(*behind)
     for old, out in zip(before[:3] if held else (), outs):
         for part in range(3):
             out[:, part * HALF : part * HALF + held] = old[:, part * held : (part + 1) * held]

time: 60.7 us -> 59 us (0.972)
  Pallas kernels: 19.5 us -> 17.6 us
    pallas_call x2, Pallas kernels: 7.03 us -> 5.7 us  [attention_step(): pl.pallas_call(functools.partial(attention_kernel, pairs, held), out_shap...]
    ppermute x1, waiting for transfers between devices: 6.39 us -> 7.32 us  [local_middle(): skip_second = lax.ppermute(skip_second, 'seq', FAR_TO_END)]
    pallas_call x1, Pallas kernels: 4.22 us -> 3.44 us  [first_step(): pl.pallas_call(first_kernel, out_shape=(VMEM((depth, 3 * HALF), jnp.bfloa...]
  transfers between devices with their start and end apart: 13 -> 13, of which waited for: 4 -> 4; matrix products, arithmetic and copies ran while one was open for 0% -> 0% of each run, Pallas kernels for 21% -> 20%
where the time goes in v5:
time: 59 us; the launch traced here: 58.8 us
  waiting for transfers between devices  22.6 us (38%)
  starting transfers between devices  18.4 us (31%)
  Pallas kernels  17.6 us (30%)
    ppermute x1, waiting for transfers between devices, local_middle(): near_across = lax.ppermute(near, 'weight', flip(2))  11.4 us
    ppermute x1, waiting for transfers between devices, local_middle(): skip_second = lax.ppermute(skip_second, 'seq', FAR_TO_END)  7.32 us
    pallas_call x2, Pallas kernels, attention_step(): pl.pallas_call(functools.partial(attention_kernel, pairs, held), out_shap...  5.7 us
    ppermute x1, starting transfers between devices, local_middle(): both_far = lax.ppermute(both_other, 'seq', END_TO_FAR)  3.97 us
    ppermute x1, starting transfers between devices, local_middle(): both_end = lax.ppermute(both_near, 'seq', END_TO_MIDDLE)  3.5 us
    pallas_call x1, Pallas kernels, first_step(): pl.pallas_call(first_kernel, out_shape=(VMEM((depth, 3 * HALF), jnp.bfloa...  3.44 us
    ppermute x1, starting transfers between devices, local_middle(): near_across = lax.ppermute(near, 'weight', flip(2))  3 us
    pallas_call x2, Pallas kernels, project_step(): pl.pallas_call(functools.partial(project_kernel, first), out_shape=jax.Sh...  2.81 us
  transfers between devices with their start and end apart: 13, of which 4 were waited for; matrix products, arithmetic and copies ran while one was open for 0% of the time, Pallas kernels for 20%

profile of v5, /device:TPU:0, one launch (start us, length us, event | category | flops | bytes accessed | tf_op | source)
XLA Modules:
  0.0 58.8 jit_solution(3079558453937803994)
XLA Ops:
  0.0 3.4 %first_weights_and_rows.1 = (bf16[384,1152]{1,0:T(8,128)(2,1)S(1)}, bf16[128,1920]{1,0:T(8,128)(2,1)S(1)}, bf16[128,1920]{1,0:T(8,128)(2,1)}) custom-call(bf16[1,128,1536]{2,1,0:T(8,128)(2,1)} %refs_10_.1, f32[1536]{0:T(1024)} %refs_13_.1, f32[1536]{0:T(1024)} %shift_ref.1, f32[3,18]{1,0:T(4,128)} %scales_ref.3, bf16[384,2304]{1,0:T(8,128)(2,1)} %codes_ref.3, ...), custom_call_target="tpu_custom_call" | custom-call | flops 3000000000 | bytes 9000000 | tf_op jit(solution)/shard_map/first_weights_and_rows/pallas_call | solution.py:120
  3.5 3.0 %collective-permute-start.1 = (bf16[384,1152]{1,0:T(8,128)(2,1)S(1)}, bf16[384,1152]{1,0:T(8,128)(2,1)S(1)}, u32[]{:S(2)}, u32[]{:S(2)}) collective-permute-start(bf16[384,1152]{1,0:T(8,128)(2,1)S(1)} %get-tuple-element.21.refs_2_.refs_0_), channel_id=1, source_target_pairs={{0,2},{1,3},{2,0},{3,1},{4,6},{5,7},{6,4},{7,5},{8,10},{9,11},{10,... | collective-permute-start | bytes 2654216 | tf_op jit(solution)/shard_map/ppermute | solution.py:519
  6.5 3.5 %collective-permute-start.7 = (bf16[128,1920]{1,0:T(8,128)(2,1)S(1)}, bf16[128,1920]{1,0:T(8,128)(2,1)S(1)}, u32[]{:S(2)}, u32[]{:S(2)}) collective-permute-start(bf16[128,1920]{1,0:T(8,128)(2,1)S(1)} %get-tuple-element.25.refs_0_.refs_1_), channel_id=1, source_target_pairs={{0,4},{12,8},{1,5},{13,9},{2,6},{14,10},{3,7},{15,11},{16,20},{28,... | collective-permute-start | bytes 1474568 | tf_op jit(solution)/shard_map/ppermute | solution.py:518
  10.0 0.1 collective-permute-start
  10.0 0.7 %collective-permute-start.5 = (bf16[128,1920]{1,0:T(8,128)(2,1)}, bf16[128,1920]{1,0:T(8,128)(2,1)S(1)}, u32[]{:S(2)}, u32[]{:S(2)}) collective-permute-start(bf16[128,1920]{1,0:T(8,128)(2,1)} %get-tuple-element.24), channel_id=1, source_target_pairs={{4,8},{8,4},{5,9},{9,5},{6,10},{10,6},{7,11},{11,7},{20,24},{24,20... | collective-permute-start | bytes 1474568 | tf_op jit(solution)/shard_map/ppermute | solution.py:516
  10.7 4.0 %collective-permute-start.6 = (bf16[128,1920]{1,0:T(8,128)(2,1)}, bf16[128,1920]{1,0:T(8,128)(2,1)S(1)}, u32[]{:S(2)}, u32[]{:S(2)}) collective-permute-start(bf16[128,1920]{1,0:T(8,128)(2,1)} %get-tuple-element.24), channel_id=1, source_target_pairs={{0,8},{12,4},{1,9},{13,5},{2,10},{14,6},{3,11},{15,7},{16,24},{28,... | collective-permute-start | bytes 1474568 | tf_op jit(solution)/shard_map/ppermute | solution.py:517
  14.7 11.4 %collective-permute-done.1.value_ref.after_ref.refs_4_.refs_2_ = bf16[384,1152]{1,0:T(8,128)(2,1)S(1)} collective-permute-done((bf16[384,1152]{1,0:T(8,128)(2,1)S(1)}, bf16[384,1152]{1,0:T(8,128)(2,1)S(1)}, u32[]{:S(2)}, u32[]{:S(2)}) %collective-permute-start.1) | collective-permute-done | bytes 884768 | tf_op jit(solution)/shard_map/ppermute | solution.py:519
  26.1 0.1 split_rows.1
  26.2 0.1 collective-permute-start.2
  26.3 0.0 copy-start.1
  26.3 0.5 collective-permute-start.3
  26.8 0.8 %far_weight.1.refs_5_.first_ref = bf16[384,1152]{1,0:T(8,128)(2,1)S(1)} custom-call(f32[3,18]{1,0:T(4,128)S(1)} %copy-done.3, bf16[384,2304]{1,0:T(8,128)(2,1)S(1)} %copy-done, bf16[384,1152]{1,0:T(8,128)(2,1)S(1)} %collective-permute-done.1.value_ref.after_ref.refs_4_.refs_2_), custom_call_target="tpu_custom_call" | custom-call | flops 10000000 | bytes 30000 | tf_op jit(solution)/shard_map/far_weight/pallas_call | solution.py:173
  27.5 0.0 collective-permute-done.refs_3_.refs_1_
  27.6 1.8 %collective-permute-start.4 = (bf16[384,1152]{1,0:T(8,128)(2,1)S(1)}, bf16[384,1152]{1,0:T(8,128)(2,1)S(1)}, u32[]{:S(2)}, u32[]{:S(2)}) collective-permute-start(bf16[384,1152]{1,0:T(8,128)(2,1)S(1)} %far_weight.1.refs_5_.first_ref), channel_id=1, source_target_pairs={{0,2},{1,3},{2,0},{3,1},{4,6},{5,7},{6,4},{7,5},{8,10},{9,11},{10,... | collective-permute-start | bytes 2654216 | tf_op jit(solution)/shard_map/ppermute | solution.py:523
  29.4 1.4 %projection.2.refs_8_ = bf16[512,1152]{1,0:T(8,128)(2,1)S(1)} custom-call(bf16[128,1920]{1,0:T(8,128)(2,1)S(1)} %get-tuple-element.25.refs_0_.refs_1_, bf16[128,1920]{1,0:T(8,128)(2,1)S(1)} %collective-permute-done.7.refs_1_.refs_2_, bf16[384,1152]{1,0:T(8,128)(2,1)S(1)} %get-tuple-element.21.refs_2_.refs_0_, ...), custom_call_target="tpu_custom_call" | custom-call | flops 10000000 | bytes 30000 | tf_op jit(solution)/shard_map/projection/pallas_call | solution.py:233
  30.8 0.0 collective-permute-done.6.refs_1_.refs_4_
  30.8 1.4 %projection.3.refs_0_ = bf16[512,1152]{1,0:T(8,128)(2,1)S(1)} custom-call(bf16[128,1920]{1,0:T(8,128)(2,1)S(1)} %collective-permute-done.5.refs_0_.refs_3_, bf16[128,1920]{1,0:T(8,128)(2,1)S(1)} %collective-permute-done.6.refs_1_.refs_4_, bf16[384,1152]{1,0:T(8,128)(2,1)S(1)} %get-tuple-element.21.refs_2_.refs_0_, ...), custom_call_target="tpu_custom_call", output_to_operand_aliasing={{}: (8, {})} | custom-call | flops 10000000 | bytes 30000 | tf_op jit(solution)/shard_map/projection/pallas_call | solution.py:233
  32.2 3.6 %attention.2 = (bf16[128,768]{1,0:T(8,128)(2,1)S(1)}, bf16[128,768]{1,0:T(8,128)(2,1)S(1)}, bf16[128,768]{1,0:T(8,128)(2,1)S(1)}, bf16[128,768]{1,0:T(8,128)(2,1)S(1)}) custom-call(bf16[512,1152]{1,0:T(8,128)(2,1)S(1)} %projection.3.refs_0_, bf16[128,1920]{1,0:T(8,128)(2,1)S(1)} %get-tuple-element.25.refs_0_.refs_1_, ...), custom_call_target="tpu_custom_call" | custom-call | flops 12000000000 | bytes 36000000 | tf_op jit(solution)/shard_map/attention/pallas_call | solution.py:324
  35.9 1.3 %collective-permute-start.12 = (bf16[128,768]{1,0:T(8,128)(2,1)S(1)}, bf16[128,768]{1,0:T(8,128)(2,1)S(1)}, u32[]{:S(2)}, u32[]{:S(2)}) collective-permute-start(bf16[128,768]{1,0:T(8,128)(2,1)S(1)} %get-tuple-element.32), channel_id=1, source_target_pairs={{4,12},{8,0},{5,13},{9,1},{6,14},{10,2},{7,15},{11,3},{20,28},{24,... | collective-permute-start | bytes 589832 | tf_op jit(solution)/shard_map/ppermute | solution.py:530
  37.2 2.1 %attention.3 = (bf16[128,1152]{1,0:T(8,128)(2,1)S(1)}, bf16[128,1152]{1,0:T(8,128)(2,1)S(1)}, bf16[128,1152]{1,0:T(8,128)(2,1)S(1)}, bf16[128,384]{1,0:T(8,128)(2,1)S(1)}) custom-call(bf16[512,1152]{1,0:T(8,128)(2,1)S(1)} %projection.3.refs_0_, bf16[128,1920]{1,0:T(8,128)(2,1)S(1)} %get-tuple-element.25.refs_0_.refs_1_, ...), custom_call_target="tpu_custom_call" | custom-call | flops 12000000000 | bytes 36000000 | tf_op jit(solution)/shard_map/attention/pallas_call | solution.py:324
  39.2 1.3 %collective-permute-start.8 = (bf16[128,384]{1,0:T(8,128)(2,1)S(1)}, bf16[128,384]{1,0:T(8,128)(2,1)S(1)}, u32[]{:S(2)}, u32[]{:S(2)}) collective-permute-start(bf16[128,384]{1,0:T(8,128)(2,1)S(1)} %get-tuple-element.29), channel_id=1, source_target_pairs={{4,12},{8,0},{5,13},{9,1},{6,14},{10,2},{7,15},{11,3},{20,28},{24,... | collective-permute-start | bytes 294920 | tf_op jit(solution)/shard_map/ppermute | solution.py:532
  40.5 1.3 %collective-permute-start.10 = (bf16[128,1152]{1,0:T(8,128)(2,1)S(1)}, bf16[128,1152]{1,0:T(8,128)(2,1)S(1)}, u32[]{:S(2)}, u32[]{:S(2)}) collective-permute-start(bf16[128,1152]{1,0:T(8,128)(2,1)S(1)} %get-tuple-element.30), channel_id=1, source_target_pairs={{4,0},{8,12},{5,1},{9,13},{6,2},{10,14},{7,3},{11,15},{20,16},{24,... | collective-permute-start | bytes 884744 | tf_op jit(solution)/shard_map/ppermute | solution.py:534
  41.8 0.0 copy-start.4
  41.8 0.8 %collective-permute-start.11 = (bf16[128,1152]{1,0:T(8,128)(2,1)S(1)}, bf16[128,1152]{1,0:T(8,128)(2,1)S(1)}, u32[]{:S(2)}, u32[]{:S(2)}) collective-permute-start(bf16[128,1152]{1,0:T(8,128)(2,1)S(1)} %get-tuple-element.31), channel_id=1, source_target_pairs={{4,8},{8,4},{5,9},{9,5},{6,10},{10,6},{7,11},{11,7},{20,24},{24,20... | collective-permute-start | bytes 884744 | tf_op jit(solution)/shard_map/ppermute | solution.py:533
  42.7 7.3 %collective-permute-done.8.after_ref.refs_9_.skip_second = bf16[128,384]{1,0:T(8,128)(2,1)S(1)} collective-permute-done((bf16[128,384]{1,0:T(8,128)(2,1)S(1)}, bf16[128,384]{1,0:T(8,128)(2,1)S(1)}, u32[]{:S(2)}, u32[]{:S(2)}) %collective-permute-start.8) | collective-permute-done | bytes 98336 | tf_op jit(solution)/shard_map/ppermute | solution.py:532
  50.0 0.1 chip_weight.1
  50.1 0.1 collective-permute-start.9
  50.2 1.4 %grad_norm_part.1 = (f32[128,1536]{1,0:T(8,128)S(1)}, f32[128,1536]{1,0:T(8,128)S(1)}, f32[128,128]{1,0:T(8,128)S(1)}) custom-call(bf16[384,1152]{1,0:T(8,128)(2,1)S(1)} %get-tuple-element.21.refs_2_.refs_0_, bf16[384,1152]{1,0:T(8,128)(2,1)S(1)} %collective-permute-done.refs_3_.refs_1_, ...), custom_call_target="tpu_custom_call" | custom-call | flops 49999998976 | bytes 150000000 | tf_op jit(solution)/shard_map/grad_norm_part/pallas_call | solution.py:378
  51.6 2.3 %collective-permute-done.9.pair.refs_7_ = bf16[768,1152]{1,0:T(8,128)(2,1)S(1)} collective-permute-done((bf16[768,1152]{1,0:T(8,128)(2,1)S(1)}, bf16[768,1152]{1,0:T(8,128)(2,1)S(1)}, u32[]{:S(2)}, u32[]{:S(2)}) %collective-permute-start.9) | collective-permute-done | bytes 1769504 | tf_op jit(solution)/shard_map/ppermute | solution.py:535
  53.9 0.7 %pair_part.1.refs_10_ = f32[128,1536]{1,0:T(8,128)S(1)} custom-call(bf16[768,1152]{1,0:T(8,128)(2,1)S(1)} %collective-permute-done.9.pair.refs_7_, bf16[128,768]{1,0:T(8,128)(2,1)S(1)} %collective-permute-done.12.refs_8_.skip_first, bf16[128,384]{1,0:T(8,128)(2,1)S(1)} %collective-permute-done.8.after_ref.refs_9_.skip_second, ...), custom_call_target="tpu_custom_call" | custom-call | flops 10000000 | bytes 30000 | tf_op jit(solution)/shard_map/pair_part/pallas_call | solution.py:404
  54.6 1.6 %collective-permute-done.10.refs_8_ = bf16[128,1152]{1,0:T(8,128)(2,1)S(1)} collective-permute-done((bf16[128,1152]{1,0:T(8,128)(2,1)S(1)}, bf16[128,1152]{1,0:T(8,128)(2,1)S(1)}, u32[]{:S(2)}, u32[]{:S(2)}) %collective-permute-start.10) | collective-permute-done | bytes 294944 | tf_op jit(solution)/shard_map/ppermute | solution.py:534
  56.2 2.6 %input_grad.1 = f32[1,128,1536]{2,1,0:T(8,128)} custom-call(bf16[384,1152]{1,0:T(8,128)(2,1)S(1)} %get-tuple-element.21.refs_2_.refs_0_, bf16[384,1152]{1,0:T(8,128)(2,1)S(1)} %collective-permute-done.refs_3_.refs_1_, bf16[384,1152]{1,0:T(8,128)(2,1)S(1)} %collective-permute-done.1.value_ref.after_ref.refs_4_.refs_2_, ...), custom_call_target="tpu_custom_call" | custom-call | flops 2000000000 | bytes 6000000 | tf_op jit(solution)/shard_map/input_grad/pallas_call | solution.py:441
  (15 shorter events, 0.0 us)
Async XLA Ops:
  0.0 26.8 %copy-start.3 = (f32[3,18]{1,0:T(4,128)S(1)}, f32[3,18]{1,0:T(4,128)}, u32[]{:S(2)}) copy-start(f32[3,18]{1,0:T(4,128)} %scales_ref.3) | copy-start | bytes 652
  0.0 26.8 %copy-start = (bf16[384,2304]{1,0:T(8,128)(2,1)S(1)}, bf16[384,2304]{1,0:T(8,128)(2,1)}, u32[]{:S(2)}) copy-start(bf16[384,2304]{1,0:T(8,128)(2,1)} %codes_ref.3) | copy-start | bytes 5308420
  3.5 22.7 %collective-permute-start.1 = (bf16[384,1152]{1,0:T(8,128)(2,1)S(1)}, bf16[384,1152]{1,0:T(8,128)(2,1)S(1)}, u32[]{:S(2)}, u32[]{:S(2)}) collective-permute-start(bf16[384,1152]{1,0:T(8,128)(2,1)S(1)} %get-tuple-element.21.refs_2_.refs_0_), channel_id=1, source_target_pairs={{0,2},{1,3},{2,0},{3,1},{4,6},{5,7},{6,4},{7,5},{8,10},{9,11},{10,... | collective-permute-start | bytes 2654216 | tf_op jit(solution)/shard_map/ppermute | solution.py:519
  6.5 19.8 %collective-permute-start.7 = (bf16[128,1920]{1,0:T(8,128)(2,1)S(1)}, bf16[128,1920]{1,0:T(8,128)(2,1)S(1)}, u32[]{:S(2)}, u32[]{:S(2)}) collective-permute-start(bf16[128,1920]{1,0:T(8,128)(2,1)S(1)} %get-tuple-element.25.refs_0_.refs_1_), channel_id=1, source_target_pairs={{0,4},{12,8},{1,5},{13,9},{2,6},{14,10},{3,7},{15,11},{16,20},{28,... | collective-permute-start | bytes 1474568 | tf_op jit(solution)/shard_map/ppermute | solution.py:518
  10.0 17.6 %collective-permute-start = (bf16[384,1152]{1,0:T(8,128)(2,1)S(1)}, bf16[384,1152]{1,0:T(8,128)(2,1)S(1)}, u32[]{:S(2)}, u32[]{:S(2)}) collective-permute-start(bf16[384,1152]{1,0:T(8,128)(2,1)S(1)} %get-tuple-element.21.refs_2_.refs_0_), channel_id=1, source_target_pairs={{0,1},{1,0},{2,3},{3,2},{4,5},{5,4},{6,7},{7,6},{8,9},{9,8},{10,11... | collective-permute-start | bytes 2654216 | tf_op jit(solution)/shard_map/ppermute | solution.py:520
  10.0 20.7 %collective-permute-start.5 = (bf16[128,1920]{1,0:T(8,128)(2,1)}, bf16[128,1920]{1,0:T(8,128)(2,1)S(1)}, u32[]{:S(2)}, u32[]{:S(2)}) collective-permute-start(bf16[128,1920]{1,0:T(8,128)(2,1)} %get-tuple-element.24), channel_id=1, source_target_pairs={{4,8},{8,4},{5,9},{9,5},{6,10},{10,6},{7,11},{11,7},{20,24},{24,20... | collective-permute-start | bytes 1474568 | tf_op jit(solution)/shard_map/ppermute | solution.py:516
  10.7 20.1 %collective-permute-start.6 = (bf16[128,1920]{1,0:T(8,128)(2,1)}, bf16[128,1920]{1,0:T(8,128)(2,1)S(1)}, u32[]{:S(2)}, u32[]{:S(2)}) collective-permute-start(bf16[128,1920]{1,0:T(8,128)(2,1)} %get-tuple-element.24), channel_id=1, source_target_pairs={{0,8},{12,4},{1,9},{13,5},{2,10},{14,6},{3,11},{15,7},{16,24},{28,... | collective-permute-start | bytes 1474568 | tf_op jit(solution)/shard_map/ppermute | solution.py:517
  26.2 3.2 %collective-permute-start.2 = (bf16[192,1152]{1,0:T(8,128)(2,1)S(1)}, bf16[192,1152]{1,0:T(8,128)(2,1)S(1)}, u32[]{:S(2)}, u32[]{:S(2)}) collective-permute-start(bf16[192,1152]{1,0:T(8,128)(2,1)S(1)} %get-tuple-element.22), channel_id=1, source_target_pairs={{0,1},{1,0},{2,3},{3,2},{4,5},{5,4},{6,7},{7,6},{8,9},{9,8},{10,11... | collective-permute-start | bytes 1327112 | tf_op jit(solution)/shard_map/ppermute | solution.py:521
  26.3 3.1 %copy-start.1 = (f32[2304]{0:T(1024)S(1)}, f32[2304]{0:T(1024)}, u32[]{:S(2)}) copy-start(f32[2304]{0:T(1024)} %refs_7_.3) | copy-start | bytes 27652
  26.3 3.1 %collective-permute-start.3 = (bf16[192,1152]{1,0:T(8,128)(2,1)S(1)}, bf16[192,1152]{1,0:T(8,128)(2,1)S(1)}, u32[]{:S(2)}, u32[]{:S(2)}) collective-permute-start(bf16[192,1152]{1,0:T(8,128)(2,1)S(1)} %get-tuple-element.23), channel_id=1, source_target_pairs={{0,1},{1,0},{2,3},{3,2},{4,5},{5,4},{6,7},{7,6},{8,9},{9,8},{10,11... | collective-permute-start | bytes 1327112 | tf_op jit(solution)/shard_map/ppermute | solution.py:521
  27.6 22.4 %collective-permute-start.4 = (bf16[384,1152]{1,0:T(8,128)(2,1)S(1)}, bf16[384,1152]{1,0:T(8,128)(2,1)S(1)}, u32[]{:S(2)}, u32[]{:S(2)}) collective-permute-start(bf16[384,1152]{1,0:T(8,128)(2,1)S(1)} %far_weight.1.refs_5_.first_ref), channel_id=1, source_target_pairs={{0,2},{1,3},{2,0},{3,1},{4,6},{5,7},{6,4},{7,5},{8,10},{9,11},{10,... | collective-permute-start | bytes 2654216 | tf_op jit(solution)/shard_map/ppermute | solution.py:523
  35.9 14.3 %collective-permute-start.12 = (bf16[128,768]{1,0:T(8,128)(2,1)S(1)}, bf16[128,768]{1,0:T(8,128)(2,1)S(1)}, u32[]{:S(2)}, u32[]{:S(2)}) collective-permute-start(bf16[128,768]{1,0:T(8,128)(2,1)S(1)} %get-tuple-element.32), channel_id=1, source_target_pairs={{4,12},{8,0},{5,13},{9,1},{6,14},{10,2},{7,15},{11,3},{20,28},{24,... | collective-permute-start | bytes 589832 | tf_op jit(solution)/shard_map/ppermute | solution.py:530
  39.2 10.8 %collective-permute-start.8 = (bf16[128,384]{1,0:T(8,128)(2,1)S(1)}, bf16[128,384]{1,0:T(8,128)(2,1)S(1)}, u32[]{:S(2)}, u32[]{:S(2)}) collective-permute-start(bf16[128,384]{1,0:T(8,128)(2,1)S(1)} %get-tuple-element.29), channel_id=1, source_target_pairs={{4,12},{8,0},{5,13},{9,1},{6,14},{10,2},{7,15},{11,3},{20,28},{24,... | collective-permute-start | bytes 294920 | tf_op jit(solution)/shard_map/ppermute | solution.py:532
  40.5 15.7 %collective-permute-start.10 = (bf16[128,1152]{1,0:T(8,128)(2,1)S(1)}, bf16[128,1152]{1,0:T(8,128)(2,1)S(1)}, u32[]{:S(2)}, u32[]{:S(2)}) collective-permute-start(bf16[128,1152]{1,0:T(8,128)(2,1)S(1)} %get-tuple-element.30), channel_id=1, source_target_pairs={{4,0},{8,12},{5,1},{9,13},{6,2},{10,14},{7,3},{11,15},{20,16},{24,... | collective-permute-start | bytes 884744 | tf_op jit(solution)/shard_map/ppermute | solution.py:534
  41.8 8.4 %copy-start.4 = (bf16[1,128,1536]{2,1,0:T(8,128)(2,1)S(1)}, bf16[1,128,1536]{2,1,0:T(8,128)(2,1)}, u32[]{:S(2)}) copy-start(bf16[1,128,1536]{2,1,0:T(8,128)(2,1)} %refs_10_.1) | copy-start | bytes 1179652
  41.8 14.4 %collective-permute-start.11 = (bf16[128,1152]{1,0:T(8,128)(2,1)S(1)}, bf16[128,1152]{1,0:T(8,128)(2,1)S(1)}, u32[]{:S(2)}, u32[]{:S(2)}) collective-permute-start(bf16[128,1152]{1,0:T(8,128)(2,1)S(1)} %get-tuple-element.31), channel_id=1, source_target_pairs={{4,8},{8,4},{5,9},{9,5},{6,10},{10,6},{7,11},{11,7},{20,24},{24,20... | collective-permute-start | bytes 884744 | tf_op jit(solution)/shard_map/ppermute | solution.py:533
  50.1 3.8 %collective-permute-start.9 = (bf16[768,1152]{1,0:T(8,128)(2,1)S(1)}, bf16[768,1152]{1,0:T(8,128)(2,1)S(1)}, u32[]{:S(2)}, u32[]{:S(2)}) collective-permute-start(bf16[768,1152]{1,0:T(8,128)(2,1)S(1)} %chip_weight.1), channel_id=1, source_target_pairs={{0,1},{1,0},{2,3},{3,2},{4,5},{5,4},{6,7},{7,6},{8,9},{9,8},{10,11... | collective-permute-start | bytes 5308424 | tf_op jit(solution)/shard_map/ppermute | solution.py:535
  53.9 2.3 %copy-start.2 = (f32[1536]{0:T(1024)S(1)}, f32[1536]{0:T(1024)}, u32[]{:S(2)}) copy-start(f32[1536]{0:T(1024)} %refs_13_.1) | copy-start | bytes 18436

commit v6 on v5

--- a/solution.py
+++ b/solution.py
@@ -13,6 +13,7 @@
 QBLOCK = 128
 HD = 768
 HALF = HD // 2
+ROWS_OUT = 32
 EPSILON = 1e-06
 VMEM = pltpu.VMEM
 SMEM = pltpu.SMEM
@@ -208,38 +209,39 @@
     )
 
 
-def project_kernel(first, *refs):
-    norms, weights, bias_ref, proj = refs[0:2], refs[2:7], refs[7], refs[-1]
+def project_part(norms, weights, bias_ref, proj, first, part):
     half = half_index()
     rows = norm_columns(norms, range(4), weights[0].shape[0])
     bias = row_vector(bias_ref)
+    at = slice(part * HALF, (part + 1) * HALF)
+    shift = jnp.where(
+        half == 0,
+        bias[:, part * HD : part * HD + HALF],
+        bias[:, part * HD + HALF : (part + 1) * HD],
+    )
+    columns = jnp.concatenate([w[:, at] for w in weights], axis=0)
+    value = (dot_plain(rows, columns) + shift).astype(jnp.bfloat16)
+    if part == 0:
+        value = value * jnp.bfloat16(HEAD_DIM**-0.5)
+    proj[first : first + rows.shape[0], at] = value
+
+
+def project_kernel(*refs):
     for part in range(3):
-        at = slice(part * HALF, (part + 1) * HALF)
-        shift = jnp.where(
-            half == 0,
-            bias[:, part * HD : part * HD + HALF],
-            bias[:, part * HD + HALF : (part + 1) * HD],
-        )
-        columns = jnp.concatenate([w[:, at] for w in weights], axis=0)
-        value = (dot_plain(rows, columns) + shift).astype(jnp.bfloat16)
-        if part == 0:
-            value = value * jnp.bfloat16(HEAD_DIM**-0.5)
-        proj[first : first + rows.shape[0], at] = value
-
-
-def project_step(norms, weights, bias, *before):
+        project_part(refs[0:2], refs[2:7], refs[7], refs[8], 0, part)
+
+
+def project_step(norms, weights, bias):
     tokens = norms[0].shape[0]
-    first = 2 * tokens * len(before)
-    return pl.pallas_call(
-        functools.partial(project_kernel, first),
+    return pl.pallas_call(
+        project_kernel,
         out_shape=jax.ShapeDtypeStruct((4 * tokens, 3 * HALF), jnp.bfloat16),
-        in_specs=[spec()] * (8 + len(before)),
+        in_specs=[spec()] * 8,
         out_specs=spec(),
-        input_output_aliases={8: 0} if before else {},
         compiler_params=pltpu.CompilerParams(vmem_limit_bytes=24 * 2**20),
         cost_estimate=cost(0.01),
         name="projection",
-    )(*norms, *weights, bias, *before)
+    )(*norms, *weights, bias)
 
 
 PAIR = 2 * HEAD_DIM
@@ -255,6 +257,24 @@
 
 def attention_kernel(pairs, held, *refs):
     proj, grads, before, outs = refs[0], refs[1:5], refs[5:-4], refs[-4:]
+    attention(pairs, held, proj, grads, before, outs)
+
+
+def project_attention_kernel(pairs, *refs):
+    norms, weights, bias_ref, proj_in, grads = refs[0:2], refs[2:7], refs[7], refs[8], refs[9:13]
+    proj, outs = refs[-5], refs[-4:]
+    tokens = norms[0].shape[0]
+    proj[: 2 * tokens] = proj_in[: 2 * tokens]
+
+    def project(part):
+        project_part(norms, weights, bias_ref, proj, 2 * tokens, part)
+
+    project(0)
+    project(1)
+    attention(pairs, 0, proj, grads, (), outs, lambda: project(2))
+
+
+def attention(pairs, held, proj, grads, before, outs, between=None):
     total = proj.shape[0]
     tokens = grads[0].shape[0]
     low = lax.broadcasted_iota(jnp.int32, (total, PAIR), 1) < HEAD_DIM
@@ -270,9 +290,13 @@
     def mask(side, value):
         return jnp.where(low, value, zero) if side == 0 else jnp.where(low, zero, value)
 
-    def before_soft(t, side):
+    def before_soft(t, side, between=None):
         query, key, value, grad = load(t)
-        return dot_last(mask(side, key), query), dot_last(mask(side, value), grad)
+        scores = dot_last(mask(side, key), query)
+        if between is not None:
+            between()
+            value = load(t)[2]
+        return scores, dot_last(mask(side, value), grad)
 
     def after_soft(t, side, prob, dscore):
         query, key, _, grad = load(t)
@@ -301,7 +325,7 @@
         if side == 1:
             store(t, done[t, 0], done[t, 1])
 
-    ready, behind = before_soft(*heads[0]), None
+    ready, behind = before_soft(*heads[0], between), None
     for i, head in enumerate(heads):
         now = ready
         if i + 1 < len(heads):
@@ -315,7 +339,22 @@
             out[:, part * HALF : part * HALF + held] = old[:, part * held : (part + 1) * held]
 
 
-def attention_step(proj, grads, pairs, before=(), after=()):
+def project_attention_step(norms, weights, bias, proj, grads, pairs, after):
+    tokens = grads[0].shape[0]
+    out = jax.ShapeDtypeStruct((tokens, 3 * len(pairs) * PAIR), jnp.bfloat16)
+    return pl.pallas_call(
+        functools.partial(project_attention_kernel, pairs),
+        out_shape=(jax.ShapeDtypeStruct(proj.shape, proj.dtype),) + (out,) * 4,
+        in_specs=[spec()] * 14,
+        out_specs=(spec(),) * 5,
+        input_output_aliases={8: 0},
+        compiler_params=pltpu.CompilerParams(vmem_limit_bytes=24 * 2**20),
+        cost_estimate=cost(12),
+        name="projection_attention",
+    )(*norms, *weights, bias, proj, *grads, after)
+
+
+def attention_step(proj, grads, pairs, before):
     tokens = grads[0].shape[0]
     widths = [3 * len(pairs) * PAIR] * 4
     for i in range(len(before)):
@@ -324,16 +363,16 @@
     return pl.pallas_call(
         functools.partial(attention_kernel, pairs, held),
         out_shape=tuple(jax.ShapeDtypeStruct((tokens, width), jnp.bfloat16) for width in widths),
-        in_specs=[spec()] * (5 + len(before) + len(after)),
+        in_specs=[spec()] * (5 + len(before)),
         out_specs=(spec(),) * 4,
         compiler_params=pltpu.CompilerParams(vmem_limit_bytes=24 * 2**20),
         cost_estimate=cost(12),
         name="attention",
-    )(proj, *grads, *before, *after)
-
-
-def join_halves(weights):
-    return [w[...] for w in weights[:3]] + [jnp.concatenate([w[...] for w in weights[3:]], axis=0)]
+    )(proj, *grads, *before)
+
+
+def near_shard(refs, j):
+    return refs[j][...] if j < 3 else jnp.concatenate([ref[...] for ref in refs[3:5]], axis=0)
 
 
 def join_skip(first, second):
@@ -350,7 +389,7 @@
 
 
 def early_kernel(*refs):
-    near_w, far_w = join_halves(refs[0:5]), {0: refs[5], 2: refs[6]}
+    near_w, far_w = refs[0:5], {0: refs[5], 2: refs[6]}
     own_ref, skip_first, skip_second, tokens_ref, sums, normed_out, inverse_out = refs[7:]
     middle = on_middle()
     mine = lax.axis_index("weight")
@@ -360,7 +399,7 @@
         for j in range(4):
             at = pl.ds(pl.multiple_of((mine ^ j) * depth, QBLOCK), depth)
             if not far or j in weights:
-                sums[:, at] = dot_last(value, weights[j][...] if far else weights[j])
+                sums[:, at] = dot_last(value, weights[j][...] if far else near_shard(weights, j))
             else:
                 sums[:, at] = jnp.zeros((value.shape[0], depth), jnp.float32)
 
@@ -413,28 +452,46 @@
 
 
 def last_kernel(*refs):
-    near_w, pair = join_halves(refs[0:5]), refs[7]
-    back_ref, cross_ref, sums, normed_ref, inverse_ref, gain_ref, out_ref, grad_norm = refs[8:]
+    near_w, pair = refs[0:5], refs[7]
+    back_ref, cross_ref, sums, normed_ref, inverse_ref, gain_ref, out_ref = refs[8:15]
+    gain, grad_hat, first_sum, second_sum, result, sems = refs[15:]
     middle = on_middle()
     mine = lax.axis_index("weight")
     depth = refs[5].shape[0]
     far_w = (refs[5], pair.at[:depth], refs[6], pair.at[depth:])
-
-    def fill(value_ref, weights, far):
+    gain[...] = row_vector(gain_ref)
+
+    def fill(value_ref, weight_of):
         value = value_ref[...]
+        first = second = jnp.zeros(first_sum.shape, jnp.float32)
         for j in range(4):
             at = pl.ds(pl.multiple_of((mine ^ j) * depth, QBLOCK), depth)
-            grad_norm[:, at] = sums[:, at] + dot_last(value, weights[j][...] if far else weights[j])
-
-    pl.when(middle)(lambda: fill(cross_ref, far_w, True))
-    pl.when(jnp.logical_not(middle))(lambda: fill(back_ref, near_w, False))
-    gain = row_vector(gain_ref)
-    for r in range(0, normed_ref.shape[0], 16):
-        normed = normed_ref[r : r + 16, :]
-        grad_hat = grad_norm[r : r + 16, :] * gain
-        first_mean = jnp.mean(grad_hat, axis=-1, keepdims=True)
-        second_mean = jnp.mean(grad_hat * normed, axis=-1, keepdims=True)
-        out_ref[0, r : r + 16, :] = inverse_ref[r : r + 16, :1] * (grad_hat - first_mean - normed * second_mean)
+            hat = (sums[:, at] + dot_last(value, weight_of(j))) * gain[:, at]
+            grad_hat[:, at] = hat
+            mixed = hat * normed_ref[:, at]
+            for c in range(0, depth, QBLOCK):
+                first += hat[:, c : c + QBLOCK]
+                second += mixed[:, c : c + QBLOCK]
+        first_sum[...] = first
+        second_sum[...] = second
+
+    pl.when(middle)(lambda: fill(cross_ref, lambda j: far_w[j][...]))
+    pl.when(jnp.logical_not(middle))(lambda: fill(back_ref, lambda j: near_shard(near_w, j)))
+    rows, width = normed_ref.shape
+    copies = []
+    for i, first in enumerate(range(0, rows, ROWS_OUT)):
+        for r in range(first, first + ROWS_OUT, 8):
+            at = slice(r, r + 8)
+            first_mean = jnp.sum(first_sum[at, :], axis=-1, keepdims=True) * (1.0 / width)
+            second_mean = jnp.sum(second_sum[at, :], axis=-1, keepdims=True) * (1.0 / width)
+            result[at, :] = inverse_ref[at, :1] * (
+                grad_hat[at, :] - first_mean - normed_ref[at, :] * second_mean
+            )
+        lines = pl.ds(first, ROWS_OUT)
+        copies.append(pltpu.make_async_copy(result.at[lines, :], out_ref.at[0, lines, :], sems.at[i]))
+        copies[-1].start()
+    for copy in copies:
+        copy.wait()
 
 
 def last_step(near_w, far_w, back, cross, sums, normed, inverse, gain):
@@ -442,8 +499,15 @@
         last_kernel,
         out_shape=jax.ShapeDtypeStruct((1, *normed.shape), jnp.float32),
         in_specs=[spec()] * 14,
-        out_specs=spec(),
-        scratch_shapes=[VMEM(normed.shape, jnp.float32)],
+        out_specs=spec(pltpu.HBM),
+        scratch_shapes=[
+            VMEM((1, normed.shape[1]), jnp.float32),
+            VMEM(normed.shape, jnp.float32),
+            VMEM((normed.shape[0], QBLOCK), jnp.float32),
+            VMEM((normed.shape[0], QBLOCK), jnp.float32),
+            VMEM(normed.shape, jnp.float32),
+            pltpu.SemaphoreType.DMA((normed.shape[0] // ROWS_OUT,)),
+        ],
         compiler_params=pltpu.CompilerParams(vmem_limit_bytes=24 * 2**20),
         cost_estimate=cost(2),
         name="input_grad",
@@ -524,9 +588,10 @@
     rows = (both_near, both_end, both_mid, both_far)
     near_w = (near, near_beside, near_across, *near_diagonal)
     proj = project_step(rows[:2], near_w, input_bias)
-    proj = project_step(rows[2:], near_w, input_bias, proj)
     grads = (both_near, both_end, both_mid, both_far)
-    *kept, skip_first = attention_step(proj, grads, (0, 1), after=(far,))
+    proj, *kept, skip_first = project_attention_step(
+        rows[2:], near_w, input_bias, proj, grads, (0, 1), far
+    )
     skip_first = lax.ppermute(skip_first, "seq", FAR_TO_END)
     own, end, mid, skip_second = attention_step(proj, grads, (2,), kept)
     skip_second = lax.ppermute(skip_second, "seq", FAR_TO_END)

time: 59 us -> 58.6 us (level)
  Pallas kernels: 17.6 us -> 16.8 us
    pallas_call x2 -> x1, Pallas kernels: 5.7 us -> 2.06 us  [attention_step(): pl.pallas_call(functools.partial(attention_kernel, pairs, held), out_shap...]
    pallas_call x2, Pallas kernels: 2.81 us -> 6.2 us  [the longest x1 4.79 us: project_attention_step(): pl.pallas_call(functools.partial(project_attention_kernel, pairs), out_sh...]
  transfers between devices with their start and end apart: 13 -> 13, of which waited for: 4 -> 4; matrix products, arithmetic and copies ran while one was open for 0% -> 0% of each run, Pallas kernels for 20% -> 19%
where the time goes in v6:
time: 58.6 us; the launch traced here: 58.4 us
  waiting for transfers between devices  22.8 us (39%)
  starting transfers between devices  18.4 us (31%)
  Pallas kernels  16.8 us (29%)
    ppermute x1, waiting for transfers between devices, local_middle(): near_across = lax.ppermute(near, 'weight', flip(2))  11.4 us
    ppermute x1, waiting for transfers between devices, local_middle(): skip_second = lax.ppermute(skip_second, 'seq', FAR_TO_END)  7.32 us
    pallas_call x1, Pallas kernels, project_attention_step(): pl.pallas_call(functools.partial(project_attention_kernel, pairs), out_sh...  4.79 us
    ppermute x1, starting transfers between devices, local_middle(): both_far = lax.ppermute(both_other, 'seq', END_TO_FAR)  3.97 us
    ppermute x1, starting transfers between devices, local_middle(): both_end = lax.ppermute(both_near, 'seq', END_TO_MIDDLE)  3.5 us
    pallas_call x1, Pallas kernels, first_step(): pl.pallas_call(first_kernel, out_shape=(VMEM((depth, 3 * HALF), jnp.bfloa...  3.44 us
    ppermute x1, starting transfers between devices, local_middle(): near_across = lax.ppermute(near, 'weight', flip(2))  3 us
    ppermute x1, waiting for transfers between devices, local_middle(): lax.ppermute(pair_step(far, far_across, skip_second), 'weight', flip(1))  2.5 us
  transfers between devices with their start and end apart: 13, of which 4 were waited for; matrix products, arithmetic and copies ran while one was open for 0% of the time, Pallas kernels for 19%

profile of v6, /device:TPU:0, one launch (start us, length us, event | category | flops | bytes accessed | tf_op | source)
XLA Modules:
  0.0 58.4 jit_solution(2438230023052793991)
XLA Ops:
  0.0 3.4 %first_weights_and_rows.1 = (bf16[384,1152]{1,0:T(8,128)(2,1)S(1)}, bf16[128,1920]{1,0:T(8,128)(2,1)S(1)}, bf16[128,1920]{1,0:T(8,128)(2,1)}) custom-call(bf16[1,128,1536]{2,1,0:T(8,128)(2,1)} %refs_10_.1, f32[1536]{0:T(1024)} %refs_13_.1, f32[1536]{0:T(1024)} %shift_ref.1, f32[3,18]{1,0:T(4,128)} %scales_ref.3, bf16[384,2304]{1,0:T(8,128)(2,1)} %codes_ref.3, ...), custom_call_target="tpu_custom_call" | custom-call | flops 3000000000 | bytes 9000000 | tf_op jit(solution)/shard_map/first_weights_and_rows/pallas_call | solution.py:121
  3.5 3.0 %collective-permute-start.1 = (bf16[384,1152]{1,0:T(8,128)(2,1)S(1)}, bf16[384,1152]{1,0:T(8,128)(2,1)S(1)}, u32[]{:S(2)}, u32[]{:S(2)}) collective-permute-start(bf16[384,1152]{1,0:T(8,128)(2,1)S(1)} %get-tuple-element.22.refs_2_.refs_0_), channel_id=1, source_target_pairs={{0,2},{1,3},{2,0},{3,1},{4,6},{5,7},{6,4},{7,5},{8,10},{9,11},{10,... | collective-permute-start | bytes 2654216 | tf_op jit(solution)/shard_map/ppermute | solution.py:583
  6.5 3.5 %collective-permute-start.7 = (bf16[128,1920]{1,0:T(8,128)(2,1)S(1)}, bf16[128,1920]{1,0:T(8,128)(2,1)S(1)}, u32[]{:S(2)}, u32[]{:S(2)}) collective-permute-start(bf16[128,1920]{1,0:T(8,128)(2,1)S(1)} %get-tuple-element.26.refs_0_.refs_9_.refs_1_), channel_id=1, source_target_pairs={{0,4},{12,8},{1,5},{13,9},{2,6},{14,10},{3,7},{15,11},{16,20},{28,... | collective-permute-start | bytes 1474568 | tf_op jit(solution)/shard_map/ppermute | solution.py:582
  10.0 0.1 collective-permute-start
  10.0 0.7 %collective-permute-start.5 = (bf16[128,1920]{1,0:T(8,128)(2,1)}, bf16[128,1920]{1,0:T(8,128)(2,1)S(1)}, u32[]{:S(2)}, u32[]{:S(2)}) collective-permute-start(bf16[128,1920]{1,0:T(8,128)(2,1)} %get-tuple-element.25), channel_id=1, source_target_pairs={{4,8},{8,4},{5,9},{9,5},{6,10},{10,6},{7,11},{11,7},{20,24},{24,20... | collective-permute-start | bytes 1474568 | tf_op jit(solution)/shard_map/ppermute | solution.py:580
  10.7 4.0 %collective-permute-start.6 = (bf16[128,1920]{1,0:T(8,128)(2,1)}, bf16[128,1920]{1,0:T(8,128)(2,1)S(1)}, u32[]{:S(2)}, u32[]{:S(2)}) collective-permute-start(bf16[128,1920]{1,0:T(8,128)(2,1)} %get-tuple-element.25), channel_id=1, source_target_pairs={{0,8},{12,4},{1,9},{13,5},{2,10},{14,6},{3,11},{15,7},{16,24},{28,... | collective-permute-start | bytes 1474568 | tf_op jit(solution)/shard_map/ppermute | solution.py:581
  14.7 11.4 %collective-permute-done.1.value_ref.after_ref.refs_4_.refs_2_ = bf16[384,1152]{1,0:T(8,128)(2,1)S(1)} collective-permute-done((bf16[384,1152]{1,0:T(8,128)(2,1)S(1)}, bf16[384,1152]{1,0:T(8,128)(2,1)S(1)}, u32[]{:S(2)}, u32[]{:S(2)}) %collective-permute-start.1) | collective-permute-done | bytes 884768 | tf_op jit(solution)/shard_map/ppermute | solution.py:583
  26.1 0.1 split_rows.1
  26.2 0.1 collective-permute-start.2
  26.2 0.0 collective-permute-done.7.refs_1_.refs_10_.refs_2_
  26.3 0.0 copy-start.1
  26.3 0.5 collective-permute-start.3
  26.8 0.8 %far_weight.1.refs_13_.first_ref.refs_5_ = bf16[384,1152]{1,0:T(8,128)(2,1)S(1)} custom-call(f32[3,18]{1,0:T(4,128)S(1)} %copy-done.3, bf16[384,2304]{1,0:T(8,128)(2,1)S(1)} %copy-done, bf16[384,1152]{1,0:T(8,128)(2,1)S(1)} %collective-permute-done.1.value_ref.after_ref.refs_4_.refs_2_), custom_call_target="tpu_custom_call" | custom-call | flops 10000000 | bytes 30000 | tf_op jit(solution)/shard_map/far_weight/pallas_call | solution.py:174
  27.6 1.8 %collective-permute-start.4 = (bf16[384,1152]{1,0:T(8,128)(2,1)S(1)}, bf16[384,1152]{1,0:T(8,128)(2,1)S(1)}, u32[]{:S(2)}, u32[]{:S(2)}) collective-permute-start(bf16[384,1152]{1,0:T(8,128)(2,1)S(1)} %far_weight.1.refs_13_.first_ref.refs_5_), channel_id=1, source_target_pairs={{0,2},{1,3},{2,0},{3,1},{4,6},{5,7},{6,4},{7,5},{8,10},{9,11},{10,... | collective-permute-start | bytes 2654216 | tf_op jit(solution)/shard_map/ppermute | solution.py:587
  29.4 0.0 collective-permute-done.2.refs_5_.refs_3_
  29.4 1.4 %projection.1.refs_8_ = bf16[512,1152]{1,0:T(8,128)(2,1)S(1)} custom-call(bf16[128,1920]{1,0:T(8,128)(2,1)S(1)} %get-tuple-element.26.refs_0_.refs_9_.refs_1_, bf16[128,1920]{1,0:T(8,128)(2,1)S(1)} %collective-permute-done.7.refs_1_.refs_10_.refs_2_, bf16[384,1152]{1,0:T(8,128)(2,1)S(1)} %get-tuple-element.22.refs_2_.refs_0_, ...), custom_call_target="tpu_custom_call" | custom-call | flops 10000000 | bytes 30000 | tf_op jit(solution)/shard_map/projection/pallas_call | solution.py:236
  30.8 0.0 collective-permute-done.6.refs_1_.refs_12_.refs_4_
  30.8 4.8 %projection_attention.1 = (bf16[512,1152]{1,0:T(8,128)(2,1)S(1)}, bf16[128,768]{1,0:T(8,128)(2,1)S(1)}, bf16[128,768]{1,0:T(8,128)(2,1)S(1)}, bf16[128,768]{1,0:T(8,128)(2,1)S(1)}, bf16[128,768]{1,0:T(8,128)(2,1)S(1)}) custom-call(bf16[128,1920]{1,0:T(8,128)(2,1)S(1)} %collective-permute-done.5.refs_0_.refs_11_.refs_3_, ...), custom_call_target="tpu_custom_call", output_to_operand_aliasing={{0}: (8, {})} | custom-call | flops 12000000000 | bytes 36000000 | tf_op jit(solution)/shard_map/projection_attention/pallas_call | solution.py:345
  35.6 1.3 %collective-permute-start.12 = (bf16[128,768]{1,0:T(8,128)(2,1)S(1)}, bf16[128,768]{1,0:T(8,128)(2,1)S(1)}, u32[]{:S(2)}, u32[]{:S(2)}) collective-permute-start(bf16[128,768]{1,0:T(8,128)(2,1)S(1)} %get-tuple-element.34), channel_id=1, source_target_pairs={{4,12},{8,0},{5,13},{9,1},{6,14},{10,2},{7,15},{11,3},{20,28},{24,... | collective-permute-start | bytes 589832 | tf_op jit(solution)/shard_map/ppermute | solution.py:595
  36.9 2.1 %attention.1 = (bf16[128,1152]{1,0:T(8,128)(2,1)S(1)}, bf16[128,1152]{1,0:T(8,128)(2,1)S(1)}, bf16[128,1152]{1,0:T(8,128)(2,1)S(1)}, bf16[128,384]{1,0:T(8,128)(2,1)S(1)}) custom-call(bf16[512,1152]{1,0:T(8,128)(2,1)S(1)} %get-tuple-element.27.refs_0_, bf16[128,1920]{1,0:T(8,128)(2,1)S(1)} %get-tuple-element.26.refs_0_.refs_9_.refs_1_, ...), custom_call_target="tpu_custom_call" | custom-call | flops 12000000000 | bytes 36000000 | tf_op jit(solution)/shard_map/attention/pallas_call | solution.py:363
  39.0 1.3 %collective-permute-start.8 = (bf16[128,384]{1,0:T(8,128)(2,1)S(1)}, bf16[128,384]{1,0:T(8,128)(2,1)S(1)}, u32[]{:S(2)}, u32[]{:S(2)}) collective-permute-start(bf16[128,384]{1,0:T(8,128)(2,1)S(1)} %get-tuple-element.31), channel_id=1, source_target_pairs={{4,12},{8,0},{5,13},{9,1},{6,14},{10,2},{7,15},{11,3},{20,28},{24,... | collective-permute-start | bytes 294920 | tf_op jit(solution)/shard_map/ppermute | solution.py:597
  40.3 1.3 %collective-permute-start.10 = (bf16[128,1152]{1,0:T(8,128)(2,1)S(1)}, bf16[128,1152]{1,0:T(8,128)(2,1)S(1)}, u32[]{:S(2)}, u32[]{:S(2)}) collective-permute-start(bf16[128,1152]{1,0:T(8,128)(2,1)S(1)} %get-tuple-element.32), channel_id=1, source_target_pairs={{4,0},{8,12},{5,1},{9,13},{6,2},{10,14},{7,3},{11,15},{20,16},{24,... | collective-permute-start | bytes 884744 | tf_op jit(solution)/shard_map/ppermute | solution.py:599
  41.6 0.0 copy-start.4
  41.6 0.8 %collective-permute-start.11 = (bf16[128,1152]{1,0:T(8,128)(2,1)S(1)}, bf16[128,1152]{1,0:T(8,128)(2,1)S(1)}, u32[]{:S(2)}, u32[]{:S(2)}) collective-permute-start(bf16[128,1152]{1,0:T(8,128)(2,1)S(1)} %get-tuple-element.33), channel_id=1, source_target_pairs={{4,8},{8,4},{5,9},{9,5},{6,10},{10,6},{7,11},{11,7},{20,24},{24,20... | collective-permute-start | bytes 884744 | tf_op jit(solution)/shard_map/ppermute | solution.py:598
  42.4 7.3 %collective-permute-done.8.after_ref.refs_9_.skip_second = bf16[128,384]{1,0:T(8,128)(2,1)S(1)} collective-permute-done((bf16[128,384]{1,0:T(8,128)(2,1)S(1)}, bf16[128,384]{1,0:T(8,128)(2,1)S(1)}, u32[]{:S(2)}, u32[]{:S(2)}) %collective-permute-start.8) | collective-permute-done | bytes 98336 | tf_op jit(solution)/shard_map/ppermute | solution.py:597
  49.7 0.1 chip_weight.1
  49.9 0.1 collective-permute-start.9
  50.0 1.1 %grad_norm_part.1 = (f32[128,1536]{1,0:T(8,128)S(1)}, f32[128,1536]{1,0:T(8,128)S(1)}, f32[128,128]{1,0:T(8,128)S(1)}) custom-call(bf16[384,1152]{1,0:T(8,128)(2,1)S(1)} %get-tuple-element.22.refs_2_.refs_0_, bf16[384,1152]{1,0:T(8,128)(2,1)S(1)} %collective-permute-done.refs_3_.refs_1_, ...), custom_call_target="tpu_custom_call" | custom-call | flops 49999998976 | bytes 150000000 | tf_op jit(solution)/shard_map/grad_norm_part/pallas_call | solution.py:417
  51.1 2.5 %collective-permute-done.9.pair.refs_7_ = bf16[768,1152]{1,0:T(8,128)(2,1)S(1)} collective-permute-done((bf16[768,1152]{1,0:T(8,128)(2,1)S(1)}, bf16[768,1152]{1,0:T(8,128)(2,1)S(1)}, u32[]{:S(2)}, u32[]{:S(2)}) %collective-permute-start.9) | collective-permute-done | bytes 1769504 | tf_op jit(solution)/shard_map/ppermute | solution.py:600
  53.6 0.7 %pair_part.1.refs_10_ = f32[128,1536]{1,0:T(8,128)S(1)} custom-call(bf16[768,1152]{1,0:T(8,128)(2,1)S(1)} %collective-permute-done.9.pair.refs_7_, bf16[128,768]{1,0:T(8,128)(2,1)S(1)} %collective-permute-done.12.refs_8_.skip_first, bf16[128,384]{1,0:T(8,128)(2,1)S(1)} %collective-permute-done.8.after_ref.refs_9_.skip_second, ...), custom_call_target="tpu_custom_call" | custom-call | flops 10000000 | bytes 30000 | tf_op jit(solution)/shard_map/pair_part/pallas_call | solution.py:443
  54.3 1.6 %collective-permute-done.10.refs_8_ = bf16[128,1152]{1,0:T(8,128)(2,1)S(1)} collective-permute-done((bf16[128,1152]{1,0:T(8,128)(2,1)S(1)}, bf16[128,1152]{1,0:T(8,128)(2,1)S(1)}, u32[]{:S(2)}, u32[]{:S(2)}) %collective-permute-start.10) | collective-permute-done | bytes 294944 | tf_op jit(solution)/shard_map/ppermute | solution.py:599
  55.9 2.3 %input_grad.1 = f32[1,128,1536]{2,1,0:T(8,128)} custom-call(bf16[384,1152]{1,0:T(8,128)(2,1)S(1)} %get-tuple-element.22.refs_2_.refs_0_, bf16[384,1152]{1,0:T(8,128)(2,1)S(1)} %collective-permute-done.refs_3_.refs_1_, bf16[384,1152]{1,0:T(8,128)(2,1)S(1)} %collective-permute-done.1.value_ref.after_ref.refs_4_.refs_2_, ...), custom_call_target="tpu_custom_call" | custom-call | flops 2000000000 | bytes 6000000 | tf_op jit(solution)/shard_map/input_grad/pallas_call | solution.py:498
  (14 shorter events, 0.0 us)
Async XLA Ops:
  0.0 26.8 %copy-start.3 = (f32[3,18]{1,0:T(4,128)S(1)}, f32[3,18]{1,0:T(4,128)}, u32[]{:S(2)}) copy-start(f32[3,18]{1,0:T(4,128)} %scales_ref.3) | copy-start | bytes 652
  0.0 26.8 %copy-start = (bf16[384,2304]{1,0:T(8,128)(2,1)S(1)}, bf16[384,2304]{1,0:T(8,128)(2,1)}, u32[]{:S(2)}) copy-start(bf16[384,2304]{1,0:T(8,128)(2,1)} %codes_ref.3) | copy-start | bytes 5308420
  3.5 22.7 %collective-permute-start.1 = (bf16[384,1152]{1,0:T(8,128)(2,1)S(1)}, bf16[384,1152]{1,0:T(8,128)(2,1)S(1)}, u32[]{:S(2)}, u32[]{:S(2)}) collective-permute-start(bf16[384,1152]{1,0:T(8,128)(2,1)S(1)} %get-tuple-element.22.refs_2_.refs_0_), channel_id=1, source_target_pairs={{0,2},{1,3},{2,0},{3,1},{4,6},{5,7},{6,4},{7,5},{8,10},{9,11},{10,... | collective-permute-start | bytes 2654216 | tf_op jit(solution)/shard_map/ppermute | solution.py:583
  6.5 19.8 %collective-permute-start.7 = (bf16[128,1920]{1,0:T(8,128)(2,1)S(1)}, bf16[128,1920]{1,0:T(8,128)(2,1)S(1)}, u32[]{:S(2)}, u32[]{:S(2)}) collective-permute-start(bf16[128,1920]{1,0:T(8,128)(2,1)S(1)} %get-tuple-element.26.refs_0_.refs_9_.refs_1_), channel_id=1, source_target_pairs={{0,4},{12,8},{1,5},{13,9},{2,6},{14,10},{3,7},{15,11},{16,20},{28,... | collective-permute-start | bytes 1474568 | tf_op jit(solution)/shard_map/ppermute | solution.py:582
  10.0 17.6 %collective-permute-start = (bf16[384,1152]{1,0:T(8,128)(2,1)S(1)}, bf16[384,1152]{1,0:T(8,128)(2,1)S(1)}, u32[]{:S(2)}, u32[]{:S(2)}) collective-permute-start(bf16[384,1152]{1,0:T(8,128)(2,1)S(1)} %get-tuple-element.22.refs_2_.refs_0_), channel_id=1, source_target_pairs={{0,1},{1,0},{2,3},{3,2},{4,5},{5,4},{6,7},{7,6},{8,9},{9,8},{10,11... | collective-permute-start | bytes 2654216 | tf_op jit(solution)/shard_map/ppermute | solution.py:584
  10.0 20.7 %collective-permute-start.5 = (bf16[128,1920]{1,0:T(8,128)(2,1)}, bf16[128,1920]{1,0:T(8,128)(2,1)S(1)}, u32[]{:S(2)}, u32[]{:S(2)}) collective-permute-start(bf16[128,1920]{1,0:T(8,128)(2,1)} %get-tuple-element.25), channel_id=1, source_target_pairs={{4,8},{8,4},{5,9},{9,5},{6,10},{10,6},{7,11},{11,7},{20,24},{24,20... | collective-permute-start | bytes 1474568 | tf_op jit(solution)/shard_map/ppermute | solution.py:580
  10.7 20.1 %collective-permute-start.6 = (bf16[128,1920]{1,0:T(8,128)(2,1)}, bf16[128,1920]{1,0:T(8,128)(2,1)S(1)}, u32[]{:S(2)}, u32[]{:S(2)}) collective-permute-start(bf16[128,1920]{1,0:T(8,128)(2,1)} %get-tuple-element.25), channel_id=1, source_target_pairs={{0,8},{12,4},{1,9},{13,5},{2,10},{14,6},{3,11},{15,7},{16,24},{28,... | collective-permute-start | bytes 1474568 | tf_op jit(solution)/shard_map/ppermute | solution.py:581
  26.2 3.2 %collective-permute-start.2 = (bf16[192,1152]{1,0:T(8,128)(2,1)S(1)}, bf16[192,1152]{1,0:T(8,128)(2,1)S(1)}, u32[]{:S(2)}, u32[]{:S(2)}) collective-permute-start(bf16[192,1152]{1,0:T(8,128)(2,1)S(1)} %get-tuple-element.23), channel_id=1, source_target_pairs={{0,1},{1,0},{2,3},{3,2},{4,5},{5,4},{6,7},{7,6},{8,9},{9,8},{10,11... | collective-permute-start | bytes 1327112 | tf_op jit(solution)/shard_map/ppermute | solution.py:585
  26.3 3.1 %copy-start.1 = (f32[2304]{0:T(1024)S(1)}, f32[2304]{0:T(1024)}, u32[]{:S(2)}) copy-start(f32[2304]{0:T(1024)} %refs_7_.3) | copy-start | bytes 27652
  26.3 3.1 %collective-permute-start.3 = (bf16[192,1152]{1,0:T(8,128)(2,1)S(1)}, bf16[192,1152]{1,0:T(8,128)(2,1)S(1)}, u32[]{:S(2)}, u32[]{:S(2)}) collective-permute-start(bf16[192,1152]{1,0:T(8,128)(2,1)S(1)} %get-tuple-element.24), channel_id=1, source_target_pairs={{0,1},{1,0},{2,3},{3,2},{4,5},{5,4},{6,7},{7,6},{8,9},{9,8},{10,11... | collective-permute-start | bytes 1327112 | tf_op jit(solution)/shard_map/ppermute | solution.py:585
  27.6 22.2 %collective-permute-start.4 = (bf16[384,1152]{1,0:T(8,128)(2,1)S(1)}, bf16[384,1152]{1,0:T(8,128)(2,1)S(1)}, u32[]{:S(2)}, u32[]{:S(2)}) collective-permute-start(bf16[384,1152]{1,0:T(8,128)(2,1)S(1)} %far_weight.1.refs_13_.first_ref.refs_5_), channel_id=1, source_target_pairs={{0,2},{1,3},{2,0},{3,1},{4,6},{5,7},{6,4},{7,5},{8,10},{9,11},{10,... | collective-permute-start | bytes 2654216 | tf_op jit(solution)/shard_map/ppermute | solution.py:587
  35.6 14.3 %collective-permute-start.12 = (bf16[128,768]{1,0:T(8,128)(2,1)S(1)}, bf16[128,768]{1,0:T(8,128)(2,1)S(1)}, u32[]{:S(2)}, u32[]{:S(2)}) collective-permute-start(bf16[128,768]{1,0:T(8,128)(2,1)S(1)} %get-tuple-element.34), channel_id=1, source_target_pairs={{4,12},{8,0},{5,13},{9,1},{6,14},{10,2},{7,15},{11,3},{20,28},{24,... | collective-permute-start | bytes 589832 | tf_op jit(solution)/shard_map/ppermute | solution.py:595
  39.0 10.8 %collective-permute-start.8 = (bf16[128,384]{1,0:T(8,128)(2,1)S(1)}, bf16[128,384]{1,0:T(8,128)(2,1)S(1)}, u32[]{:S(2)}, u32[]{:S(2)}) collective-permute-start(bf16[128,384]{1,0:T(8,128)(2,1)S(1)} %get-tuple-element.31), channel_id=1, source_target_pairs={{4,12},{8,0},{5,13},{9,1},{6,14},{10,2},{7,15},{11,3},{20,28},{24,... | collective-permute-start | bytes 294920 | tf_op jit(solution)/shard_map/ppermute | solution.py:597
  40.3 15.7 %collective-permute-start.10 = (bf16[128,1152]{1,0:T(8,128)(2,1)S(1)}, bf16[128,1152]{1,0:T(8,128)(2,1)S(1)}, u32[]{:S(2)}, u32[]{:S(2)}) collective-permute-start(bf16[128,1152]{1,0:T(8,128)(2,1)S(1)} %get-tuple-element.32), channel_id=1, source_target_pairs={{4,0},{8,12},{5,1},{9,13},{6,2},{10,14},{7,3},{11,15},{20,16},{24,... | collective-permute-start | bytes 884744 | tf_op jit(solution)/shard_map/ppermute | solution.py:599
  41.6 8.4 %copy-start.4 = (bf16[1,128,1536]{2,1,0:T(8,128)(2,1)S(1)}, bf16[1,128,1536]{2,1,0:T(8,128)(2,1)}, u32[]{:S(2)}) copy-start(bf16[1,128,1536]{2,1,0:T(8,128)(2,1)} %refs_10_.1) | copy-start | bytes 1179652
  41.6 14.4 %collective-permute-start.11 = (bf16[128,1152]{1,0:T(8,128)(2,1)S(1)}, bf16[128,1152]{1,0:T(8,128)(2,1)S(1)}, u32[]{:S(2)}, u32[]{:S(2)}) collective-permute-start(bf16[128,1152]{1,0:T(8,128)(2,1)S(1)} %get-tuple-element.33), channel_id=1, source_target_pairs={{4,8},{8,4},{5,9},{9,5},{6,10},{10,6},{7,11},{11,7},{20,24},{24,20... | collective-permute-start | bytes 884744 | tf_op jit(solution)/shard_map/ppermute | solution.py:598
  49.9 3.8 %collective-permute-start.9 = (bf16[768,1152]{1,0:T(8,128)(2,1)S(1)}, bf16[768,1152]{1,0:T(8,128)(2,1)S(1)}, u32[]{:S(2)}, u32[]{:S(2)}) collective-permute-start(bf16[768,1152]{1,0:T(8,128)(2,1)S(1)} %chip_weight.1), channel_id=1, source_target_pairs={{0,1},{1,0},{2,3},{3,2},{4,5},{5,4},{6,7},{7,6},{8,9},{9,8},{10,11... | collective-permute-start | bytes 5308424 | tf_op jit(solution)/shard_map/ppermute | solution.py:600
  53.6 2.3 %copy-start.2 = (f32[1536]{0:T(1024)S(1)}, f32[1536]{0:T(1024)}, u32[]{:S(2)}) copy-start(f32[1536]{0:T(1024)} %refs_13_.1) | copy-start | bytes 18436

commit v7 on v6

--- a/solution.py
+++ b/solution.py
@@ -334,7 +334,7 @@
             finish(*behind)
         behind = (*head, *soft_part(*now))
     finish(*behind)
-    for old, out in zip(before[:3] if held else (), outs):
+    for old, out in zip(before, outs[0:3:2]):
         for part in range(3):
             out[:, part * HALF : part * HALF + held] = old[:, part * held : (part + 1) * held]
 
@@ -358,7 +358,7 @@
     tokens = grads[0].shape[0]
     widths = [3 * len(pairs) * PAIR] * 4
     for i in range(len(before)):
-        widths[i] = 3 * HALF
+        widths[2 * i] = 3 * HALF
     held = before[0].shape[1] // 3 if before else 0
     return pl.pallas_call(
         functools.partial(attention_kernel, pairs, held),
@@ -371,8 +371,14 @@
     )(proj, *grads, *before)
 
 
-def near_shard(refs, j):
-    return refs[j][...] if j < 3 else jnp.concatenate([ref[...] for ref in refs[3:5]], axis=0)
+def near_shard(refs, j, pairs=None):
+    def columns(ref):
+        if pairs is None:
+            return ref[...]
+        first, last = pairs[0] * PAIR, (pairs[-1] + 1) * PAIR
+        return jnp.concatenate([ref[:, part * HALF + first : part * HALF + last] for part in range(3)], axis=1)
+
+    return columns(refs[j]) if j < 3 else jnp.concatenate([columns(ref) for ref in refs[3:5]], axis=0)
 
 
 def join_skip(first, second):
@@ -425,35 +431,39 @@
     )(*near_w, *far_w, own, *skips, tokens)
 
 
-def pair_part_kernel(pair, skip_first, skip_second, sums, out_ref):
+def pair_part_kernel(*refs):
+    near_w = refs[0:5]
+    pair, skip_first, skip_second, back_first, sums, out_ref = refs[5:]
     mine = lax.axis_index("weight")
     depth = pair.shape[0] // 2
     out_ref[...] = sums[...]
 
     @pl.when(jnp.logical_not(on_middle()))
     def _():
-        for i, j in enumerate((1, 3)):
+        skip = join_skip(skip_first, skip_second)
+        for j in range(4):
             at = pl.ds(pl.multiple_of((mine ^ j) * depth, QBLOCK), depth)
-            out_ref[:, at] = sums[:, at] + dot_last(
-                join_skip(skip_first, skip_second), pair[i * depth : (i + 1) * depth]
-            )
-
-
-def pair_part_step(pair, skips, sums):
+            total = sums[:, at] + dot_last(back_first[...], near_shard(near_w, j, EARLY))
+            if j % 2 == 1:
+                total += dot_last(skip, pair[j // 2 * depth : (j // 2 + 1) * depth])
+            out_ref[:, at] = total
+
+
+def pair_part_step(near_w, pair, skips, back_first, sums):
     return pl.pallas_call(
         pair_part_kernel,
         out_shape=jax.ShapeDtypeStruct(sums.shape, sums.dtype),
-        in_specs=[spec()] * 4,
+        in_specs=[spec()] * 10,
         out_specs=spec(),
         compiler_params=pltpu.CompilerParams(vmem_limit_bytes=24 * 2**20),
         cost_estimate=cost(0.01),
         name="pair_part",
-    )(pair, *skips, sums)
+    )(*near_w, pair, *skips, back_first, sums)
 
 
 def last_kernel(*refs):
     near_w, pair = refs[0:5], refs[7]
-    back_ref, cross_ref, sums, normed_ref, inverse_ref, gain_ref, out_ref = refs[8:15]
+    sums, back_ref, cross_ref, normed_ref, inverse_ref, gain_ref, out_ref = refs[8:15]
     gain, grad_hat, first_sum, second_sum, result, sems = refs[15:]
     middle = on_middle()
     mine = lax.axis_index("weight")
@@ -476,7 +486,7 @@
         second_sum[...] = second
 
     pl.when(middle)(lambda: fill(cross_ref, lambda j: far_w[j][...]))
-    pl.when(jnp.logical_not(middle))(lambda: fill(back_ref, lambda j: near_shard(near_w, j)))
+    pl.when(jnp.logical_not(middle))(lambda: fill(back_ref, lambda j: near_shard(near_w, j, LATE)))
     rows, width = normed_ref.shape
     copies = []
     for i, first in enumerate(range(0, rows, ROWS_OUT)):
@@ -511,7 +521,7 @@
         compiler_params=pltpu.CompilerParams(vmem_limit_bytes=24 * 2**20),
         cost_estimate=cost(2),
         name="input_grad",
-    )(*near_w, *far_w, back, cross, sums, normed, inverse, gain)
+    )(*near_w, *far_w, sums, back, cross, normed, inverse, gain)
 
 
 def split_kernel(value_ref, upper_ref, lower_ref):
@@ -551,6 +561,8 @@
     )(first, second, after)
 
 
+EARLY = (0, 1)
+LATE = (2,)
 END_TO_MIDDLE = [(0, 1), (3, 2)]
 MIDDLE = [(1, 2), (2, 1)]
 END_TO_FAR = [(0, 2), (3, 1)]
@@ -589,11 +601,12 @@
     near_w = (near, near_beside, near_across, *near_diagonal)
     proj = project_step(rows[:2], near_w, input_bias)
     grads = (both_near, both_end, both_mid, both_far)
-    proj, *kept, skip_first = project_attention_step(
-        rows[2:], near_w, input_bias, proj, grads, (0, 1), far
-    )
+    proj, own, end, mid, skip_first = project_attention_step(
+        rows[2:], near_w, input_bias, proj, grads, EARLY, far
+    )
+    back_first = lax.ppermute(end, "seq", MIDDLE_TO_END)
     skip_first = lax.ppermute(skip_first, "seq", FAR_TO_END)
-    own, end, mid, skip_second = attention_step(proj, grads, (2,), kept)
+    own, end, mid, skip_second = attention_step(proj, grads, LATE, (own, mid))
     skip_second = lax.ppermute(skip_second, "seq", FAR_TO_END)
     cross = lax.ppermute(mid, "seq", MIDDLE)
     back = lax.ppermute(end, "seq", MIDDLE_TO_END)
@@ -601,7 +614,7 @@
     far_w = (far, far_across)
     skips = (skip_first, skip_second)
     sums, normed, inverse = early_step(near_w, far_w, own, skips, tokens)
-    sums = pair_part_step(far_pair, skips, sums)
+    sums = pair_part_step(near_w, far_pair, skips, back_first, sums)
     return last_step(near_w, (*far_w, far_pair), back, cross, sums, normed, inverse, norm_gain)
 
 

time: 58.6 us -> 58.1 us (level)
  waiting for transfers between devices: 22.8 us -> 20.8 us
  starting transfers between devices: 18.4 us -> 19.6 us
    ppermute x1, waiting for transfers between devices: 2.5 us -> 0.52 us  [local_middle(): lax.ppermute(pair_step(far, far_across, skip_second), 'weight', flip(1))]
    ppermute x0 -> x1, waiting for transfers between devices: none -> 1.98 us  [local_middle(): back_first = lax.ppermute(end, 'seq', MIDDLE_TO_END)]
    ppermute x1, waiting for transfers between devices: 1.61 us -> 0.08 us  [local_middle(): back = lax.ppermute(end, 'seq', MIDDLE_TO_END)]
    ppermute x0 -> x1, starting transfers between devices: none -> 1.29 us  [local_middle(): back_first = lax.ppermute(end, 'seq', MIDDLE_TO_END)]
    pallas_call x1, Pallas kernels: 0.71 us -> 1.42 us  [pair_part_step(): pl.pallas_call(pair_part_kernel, out_shape=jax.ShapeDtypeStruct(sums.shap...]
    pallas_call x1, Pallas kernels: 2.28 us -> 1.63 us  [last_step(): pl.pallas_call(last_kernel, out_shape=jax.ShapeDtypeStruct((1, *normed.sh...]
  transfers between devices with their start and end apart: 13 -> 14, of which waited for: 4 -> 5; matrix products, arithmetic and copies ran while one was open for 0% -> 0% of each run, Pallas kernels for 19% -> 20%
where the time goes in v7:
time: 58.1 us; the launch traced here: 57.7 us
  waiting for transfers between devices  20.8 us (36%)
  starting transfers between devices  19.6 us (34%)
  Pallas kernels  16.9 us (29%)
    ppermute x1, waiting for transfers between devices, local_middle(): near_across = lax.ppermute(near, 'weight', flip(2))  11.4 us
    ppermute x1, waiting for transfers between devices, local_middle(): skip_second = lax.ppermute(skip_second, 'seq', FAR_TO_END)  6.85 us
    pallas_call x1, Pallas kernels, project_attention_step(): pl.pallas_call(functools.partial(project_attention_kernel, pairs), out_sh...  4.79 us
    ppermute x1, starting transfers between devices, local_middle(): both_far = lax.ppermute(both_other, 'seq', END_TO_FAR)  3.97 us
    ppermute x1, starting transfers between devices, local_middle(): both_end = lax.ppermute(both_near, 'seq', END_TO_MIDDLE)  3.5 us
    pallas_call x1, Pallas kernels, first_step(): pl.pallas_call(first_kernel, out_shape=(VMEM((depth, 3 * HALF), jnp.bfloa...  3.44 us
    ppermute x1, starting transfers between devices, local_middle(): near_across = lax.ppermute(near, 'weight', flip(2))  3 us
    pallas_call x1, Pallas kernels, attention_step(): pl.pallas_call(functools.partial(attention_kernel, pairs, held), out_shap...  2.06 us
  transfers between devices with their start and end apart: 14, of which 5 were waited for; matrix products, arithmetic and copies ran while one was open for 0% of the time, Pallas kernels for 20%

profile of v7, /device:TPU:0, one launch (start us, length us, event | category | flops | bytes accessed | tf_op | source)
XLA Modules:
  0.0 57.7 jit_solution(7024937980348721085)
XLA Ops:
  0.0 3.4 %first_weights_and_rows.1 = (bf16[384,1152]{1,0:T(8,128)(2,1)S(1)}, bf16[128,1920]{1,0:T(8,128)(2,1)S(1)}, bf16[128,1920]{1,0:T(8,128)(2,1)}) custom-call(bf16[1,128,1536]{2,1,0:T(8,128)(2,1)} %refs_10_.1, f32[1536]{0:T(1024)} %refs_13_.1, f32[1536]{0:T(1024)} %shift_ref.1, f32[3,18]{1,0:T(4,128)} %scales_ref.3, bf16[384,2304]{1,0:T(8,128)(2,1)} %codes_ref.3, ...), custom_call_target="tpu_custom_call" | custom-call | flops 3000000000 | bytes 9000000 | tf_op jit(solution)/shard_map/first_weights_and_rows/pallas_call | solution.py:121
  3.5 3.0 %collective-permute-start.1 = (bf16[384,1152]{1,0:T(8,128)(2,1)S(1)}, bf16[384,1152]{1,0:T(8,128)(2,1)S(1)}, u32[]{:S(2)}, u32[]{:S(2)}) collective-permute-start(bf16[384,1152]{1,0:T(8,128)(2,1)S(1)} %get-tuple-element.22.refs_2_.refs_0_), channel_id=1, source_target_pairs={{0,2},{1,3},{2,0},{3,1},{4,6},{5,7},{6,4},{7,5},{8,10},{9,11},{10,... | collective-permute-start | bytes 2654216 | tf_op jit(solution)/shard_map/ppermute | solution.py:595
  6.5 3.5 %collective-permute-start.7 = (bf16[128,1920]{1,0:T(8,128)(2,1)S(1)}, bf16[128,1920]{1,0:T(8,128)(2,1)S(1)}, u32[]{:S(2)}, u32[]{:S(2)}) collective-permute-start(bf16[128,1920]{1,0:T(8,128)(2,1)S(1)} %get-tuple-element.26.refs_0_.refs_9_.refs_1_), channel_id=1, source_target_pairs={{0,4},{12,8},{1,5},{13,9},{2,6},{14,10},{3,7},{15,11},{16,20},{28,... | collective-permute-start | bytes 1474568 | tf_op jit(solution)/shard_map/ppermute | solution.py:594
  10.0 0.1 collective-permute-start
  10.0 0.7 %collective-permute-start.5 = (bf16[128,1920]{1,0:T(8,128)(2,1)}, bf16[128,1920]{1,0:T(8,128)(2,1)S(1)}, u32[]{:S(2)}, u32[]{:S(2)}) collective-permute-start(bf16[128,1920]{1,0:T(8,128)(2,1)} %get-tuple-element.25), channel_id=1, source_target_pairs={{4,8},{8,4},{5,9},{9,5},{6,10},{10,6},{7,11},{11,7},{20,24},{24,20... | collective-permute-start | bytes 1474568 | tf_op jit(solution)/shard_map/ppermute | solution.py:592
  10.7 4.0 %collective-permute-start.6 = (bf16[128,1920]{1,0:T(8,128)(2,1)}, bf16[128,1920]{1,0:T(8,128)(2,1)S(1)}, u32[]{:S(2)}, u32[]{:S(2)}) collective-permute-start(bf16[128,1920]{1,0:T(8,128)(2,1)} %get-tuple-element.25), channel_id=1, source_target_pairs={{0,8},{12,4},{1,9},{13,5},{2,10},{14,6},{3,11},{15,7},{16,24},{28,... | collective-permute-start | bytes 1474568 | tf_op jit(solution)/shard_map/ppermute | solution.py:593
  14.7 11.4 %collective-permute-done.1.value_ref.after_ref.refs_4_.refs_2_ = bf16[384,1152]{1,0:T(8,128)(2,1)S(1)} collective-permute-done((bf16[384,1152]{1,0:T(8,128)(2,1)S(1)}, bf16[384,1152]{1,0:T(8,128)(2,1)S(1)}, u32[]{:S(2)}, u32[]{:S(2)}) %collective-permute-start.1) | collective-permute-done | bytes 884768 | tf_op jit(solution)/shard_map/ppermute | solution.py:595
  26.1 0.1 split_rows.1
  26.2 0.1 collective-permute-start.2
  26.2 0.0 collective-permute-done.7.refs_1_.refs_10_.refs_2_
  26.3 0.0 copy-start.1
  26.3 0.5 collective-permute-start.3
  26.8 0.8 %far_weight.1.refs_13_.first_ref.refs_5_ = bf16[384,1152]{1,0:T(8,128)(2,1)S(1)} custom-call(f32[3,18]{1,0:T(4,128)S(1)} %copy-done.3, bf16[384,2304]{1,0:T(8,128)(2,1)S(1)} %copy-done, bf16[384,1152]{1,0:T(8,128)(2,1)S(1)} %collective-permute-done.1.value_ref.after_ref.refs_4_.refs_2_), custom_call_target="tpu_custom_call" | custom-call | flops 10000000 | bytes 30000 | tf_op jit(solution)/shard_map/far_weight/pallas_call | solution.py:174
  27.6 1.8 %collective-permute-start.4 = (bf16[384,1152]{1,0:T(8,128)(2,1)S(1)}, bf16[384,1152]{1,0:T(8,128)(2,1)S(1)}, u32[]{:S(2)}, u32[]{:S(2)}) collective-permute-start(bf16[384,1152]{1,0:T(8,128)(2,1)S(1)} %far_weight.1.refs_13_.first_ref.refs_5_), channel_id=1, source_target_pairs={{0,2},{1,3},{2,0},{3,1},{4,6},{5,7},{6,4},{7,5},{8,10},{9,11},{10,... | collective-permute-start | bytes 2654216 | tf_op jit(solution)/shard_map/ppermute | solution.py:599
  29.4 1.4 %projection.1.refs_8_ = bf16[512,1152]{1,0:T(8,128)(2,1)S(1)} custom-call(bf16[128,1920]{1,0:T(8,128)(2,1)S(1)} %get-tuple-element.26.refs_0_.refs_9_.refs_1_, bf16[128,1920]{1,0:T(8,128)(2,1)S(1)} %collective-permute-done.7.refs_1_.refs_10_.refs_2_, bf16[384,1152]{1,0:T(8,128)(2,1)S(1)} %get-tuple-element.22.refs_2_.refs_0_, ...), custom_call_target="tpu_custom_call" | custom-call | flops 10000000 | bytes 30000 | tf_op jit(solution)/shard_map/projection/pallas_call | solution.py:236
  30.8 0.0 collective-permute-done.6.refs_1_.refs_12_.refs_4_
  30.8 4.8 %projection_attention.1 = (bf16[512,1152]{1,0:T(8,128)(2,1)S(1)}, bf16[128,768]{1,0:T(8,128)(2,1)S(1)}, bf16[128,768]{1,0:T(8,128)(2,1)S(1)}, bf16[128,768]{1,0:T(8,128)(2,1)S(1)}, bf16[128,768]{1,0:T(8,128)(2,1)S(1)}) custom-call(bf16[128,1920]{1,0:T(8,128)(2,1)S(1)} %collective-permute-done.5.refs_0_.refs_11_.refs_3_, ...), custom_call_target="tpu_custom_call", output_to_operand_aliasing={{0}: (8, {})} | custom-call | flops 12000000000 | bytes 36000000 | tf_op jit(solution)/shard_map/projection_attention/pallas_call | solution.py:345
  35.6 1.3 %collective-permute-start.10 = (bf16[128,768]{1,0:T(8,128)(2,1)S(1)}, bf16[128,768]{1,0:T(8,128)(2,1)S(1)}, u32[]{:S(2)}, u32[]{:S(2)}) collective-permute-start(bf16[128,768]{1,0:T(8,128)(2,1)S(1)} %get-tuple-element.31), channel_id=1, source_target_pairs={{4,12},{8,0},{5,13},{9,1},{6,14},{10,2},{7,15},{11,3},{20,28},{24,... | collective-permute-start | bytes 589832 | tf_op jit(solution)/shard_map/ppermute | solution.py:608
  36.9 2.1 %attention.1 = (bf16[128,1152]{1,0:T(8,128)(2,1)S(1)}, bf16[128,384]{1,0:T(8,128)(2,1)S(1)}, bf16[128,1152]{1,0:T(8,128)(2,1)S(1)}, bf16[128,384]{1,0:T(8,128)(2,1)S(1)}) custom-call(bf16[512,1152]{1,0:T(8,128)(2,1)S(1)} %get-tuple-element.27.refs_0_, bf16[128,1920]{1,0:T(8,128)(2,1)S(1)} %get-tuple-element.26.refs_0_.refs_9_.refs_1_, ...), custom_call_target="tpu_custom_call" | custom-call | flops 12000000000 | bytes 36000000 | tf_op jit(solution)/shard_map/attention/pallas_call | solution.py:363
  39.0 1.3 %collective-permute-start.8 = (bf16[128,384]{1,0:T(8,128)(2,1)S(1)}, bf16[128,384]{1,0:T(8,128)(2,1)S(1)}, u32[]{:S(2)}, u32[]{:S(2)}) collective-permute-start(bf16[128,384]{1,0:T(8,128)(2,1)S(1)} %get-tuple-element.30), channel_id=1, source_target_pairs={{4,12},{8,0},{5,13},{9,1},{6,14},{10,2},{7,15},{11,3},{20,28},{24,... | collective-permute-start | bytes 294920 | tf_op jit(solution)/shard_map/ppermute | solution.py:610
  40.3 1.3 %collective-permute-start.11 = (bf16[128,768]{1,0:T(8,128)(2,1)S(1)}, bf16[128,768]{1,0:T(8,128)(2,1)S(1)}, u32[]{:S(2)}, u32[]{:S(2)}) collective-permute-start(bf16[128,768]{1,0:T(8,128)(2,1)S(1)} %get-tuple-element.32), channel_id=1, source_target_pairs={{4,0},{8,12},{5,1},{9,13},{6,2},{10,14},{7,3},{11,15},{20,16},{24,... | collective-permute-start | bytes 589832 | tf_op jit(solution)/shard_map/ppermute | solution.py:607
  41.6 1.3 %collective-permute-start.12 = (bf16[128,384]{1,0:T(8,128)(2,1)S(1)}, bf16[128,384]{1,0:T(8,128)(2,1)S(1)}, u32[]{:S(2)}, u32[]{:S(2)}) collective-permute-start(bf16[128,384]{1,0:T(8,128)(2,1)S(1)} %get-tuple-element.35), channel_id=1, source_target_pairs={{4,0},{8,12},{5,1},{9,13},{6,2},{10,14},{7,3},{11,15},{20,16},{24,... | collective-permute-start | bytes 294920 | tf_op jit(solution)/shard_map/ppermute | solution.py:612
  42.9 6.8 %collective-permute-done.8.after_ref.refs_9_.refs_7_ = bf16[128,384]{1,0:T(8,128)(2,1)S(1)} collective-permute-done((bf16[128,384]{1,0:T(8,128)(2,1)S(1)}, bf16[128,384]{1,0:T(8,128)(2,1)S(1)}, u32[]{:S(2)}, u32[]{:S(2)}) %collective-permute-start.8) | collective-permute-done | bytes 98336 | tf_op jit(solution)/shard_map/ppermute | solution.py:610
  49.7 0.8 %collective-permute-start.13 = (bf16[128,1152]{1,0:T(8,128)(2,1)S(1)}, bf16[128,1152]{1,0:T(8,128)(2,1)S(1)}, u32[]{:S(2)}, u32[]{:S(2)}) collective-permute-start(bf16[128,1152]{1,0:T(8,128)(2,1)S(1)} %get-tuple-element.36), channel_id=1, source_target_pairs={{4,8},{8,4},{5,9},{9,5},{6,10},{10,6},{7,11},{11,7},{20,24},{24,20... | collective-permute-start | bytes 884744 | tf_op jit(solution)/shard_map/ppermute | solution.py:611
  50.5 0.1 chip_weight.1
  50.7 0.1 collective-permute-start.9
  50.8 1.2 %grad_norm_part.1 = (f32[128,1536]{1,0:T(8,128)S(1)}, f32[128,1536]{1,0:T(8,128)S(1)}, f32[128,128]{1,0:T(8,128)S(1)}) custom-call(bf16[384,1152]{1,0:T(8,128)(2,1)S(1)} %get-tuple-element.22.refs_2_.refs_0_, bf16[384,1152]{1,0:T(8,128)(2,1)S(1)} %collective-permute-done.refs_3_.refs_1_, ...), custom_call_target="tpu_custom_call" | custom-call | flops 49999998976 | bytes 150000000 | tf_op jit(solution)/shard_map/grad_norm_part/pallas_call | solution.py:423
  51.9 2.0 %collective-permute-done.11.refs_8_ = bf16[128,768]{1,0:T(8,128)(2,1)S(1)} collective-permute-done((bf16[128,768]{1,0:T(8,128)(2,1)S(1)}, bf16[128,768]{1,0:T(8,128)(2,1)S(1)}, u32[]{:S(2)}, u32[]{:S(2)}) %collective-permute-start.11) | collective-permute-done | bytes 196640 | tf_op jit(solution)/shard_map/ppermute | solution.py:607
  53.9 0.5 collective-permute-done.9.refs_5_.refs_7_
  54.4 1.4 %pair_part.1.refs_8_ = f32[128,1536]{1,0:T(8,128)S(1)} custom-call(bf16[384,1152]{1,0:T(8,128)(2,1)S(1)} %get-tuple-element.22.refs_2_.refs_0_, bf16[384,1152]{1,0:T(8,128)(2,1)S(1)} %collective-permute-done.refs_3_.refs_1_, bf16[384,1152]{1,0:T(8,128)(2,1)S(1)} %collective-permute-done.1.value_ref.after_ref.refs_4_.refs_2_, ...), custom_call_target="tpu_custom_call" | custom-call | flops 10000000 | bytes 30000 | tf_op jit(solution)/shard_map/pair_part/pallas_call | solution.py:453
  55.8 0.1 collective-permute-done.12.refs_9_
  55.9 1.6 %input_grad.1 = f32[1,128,1536]{2,1,0:T(8,128)} custom-call(bf16[384,1152]{1,0:T(8,128)(2,1)S(1)} %get-tuple-element.22.refs_2_.refs_0_, bf16[384,1152]{1,0:T(8,128)(2,1)S(1)} %collective-permute-done.refs_3_.refs_1_, bf16[384,1152]{1,0:T(8,128)(2,1)S(1)} %collective-permute-done.1.value_ref.after_ref.refs_4_.refs_2_, ...), custom_call_target="tpu_custom_call" | custom-call | flops 2000000000 | bytes 6000000 | tf_op jit(solution)/shard_map/input_grad/pallas_call | solution.py:508
  (16 shorter events, 0.0 us)
Async XLA Ops:
  0.0 26.8 %copy-start.3 = (f32[3,18]{1,0:T(4,128)S(1)}, f32[3,18]{1,0:T(4,128)}, u32[]{:S(2)}) copy-start(f32[3,18]{1,0:T(4,128)} %scales_ref.3) | copy-start | bytes 652
  0.0 26.8 %copy-start = (bf16[384,2304]{1,0:T(8,128)(2,1)S(1)}, bf16[384,2304]{1,0:T(8,128)(2,1)}, u32[]{:S(2)}) copy-start(bf16[384,2304]{1,0:T(8,128)(2,1)} %codes_ref.3) | copy-start | bytes 5308420
  3.5 22.7 %collective-permute-start.1 = (bf16[384,1152]{1,0:T(8,128)(2,1)S(1)}, bf16[384,1152]{1,0:T(8,128)(2,1)S(1)}, u32[]{:S(2)}, u32[]{:S(2)}) collective-permute-start(bf16[384,1152]{1,0:T(8,128)(2,1)S(1)} %get-tuple-element.22.refs_2_.refs_0_), channel_id=1, source_target_pairs={{0,2},{1,3},{2,0},{3,1},{4,6},{5,7},{6,4},{7,5},{8,10},{9,11},{10,... | collective-permute-start | bytes 2654216 | tf_op jit(solution)/shard_map/ppermute | solution.py:595
  6.5 19.8 %collective-permute-start.7 = (bf16[128,1920]{1,0:T(8,128)(2,1)S(1)}, bf16[128,1920]{1,0:T(8,128)(2,1)S(1)}, u32[]{:S(2)}, u32[]{:S(2)}) collective-permute-start(bf16[128,1920]{1,0:T(8,128)(2,1)S(1)} %get-tuple-element.26.refs_0_.refs_9_.refs_1_), channel_id=1, source_target_pairs={{0,4},{12,8},{1,5},{13,9},{2,6},{14,10},{3,7},{15,11},{16,20},{28,... | collective-permute-start | bytes 1474568 | tf_op jit(solution)/shard_map/ppermute | solution.py:594
  10.0 17.6 %collective-permute-start = (bf16[384,1152]{1,0:T(8,128)(2,1)S(1)}, bf16[384,1152]{1,0:T(8,128)(2,1)S(1)}, u32[]{:S(2)}, u32[]{:S(2)}) collective-permute-start(bf16[384,1152]{1,0:T(8,128)(2,1)S(1)} %get-tuple-element.22.refs_2_.refs_0_), channel_id=1, source_target_pairs={{0,1},{1,0},{2,3},{3,2},{4,5},{5,4},{6,7},{7,6},{8,9},{9,8},{10,11... | collective-permute-start | bytes 2654216 | tf_op jit(solution)/shard_map/ppermute | solution.py:596
  10.0 20.7 %collective-permute-start.5 = (bf16[128,1920]{1,0:T(8,128)(2,1)}, bf16[128,1920]{1,0:T(8,128)(2,1)S(1)}, u32[]{:S(2)}, u32[]{:S(2)}) collective-permute-start(bf16[128,1920]{1,0:T(8,128)(2,1)} %get-tuple-element.25), channel_id=1, source_target_pairs={{4,8},{8,4},{5,9},{9,5},{6,10},{10,6},{7,11},{11,7},{20,24},{24,20... | collective-permute-start | bytes 1474568 | tf_op jit(solution)/shard_map/ppermute | solution.py:592
  10.7 20.1 %collective-permute-start.6 = (bf16[128,1920]{1,0:T(8,128)(2,1)}, bf16[128,1920]{1,0:T(8,128)(2,1)S(1)}, u32[]{:S(2)}, u32[]{:S(2)}) collective-permute-start(bf16[128,1920]{1,0:T(8,128)(2,1)} %get-tuple-element.25), channel_id=1, source_target_pairs={{0,8},{12,4},{1,9},{13,5},{2,10},{14,6},{3,11},{15,7},{16,24},{28,... | collective-permute-start | bytes 1474568 | tf_op jit(solution)/shard_map/ppermute | solution.py:593
  26.2 3.2 %collective-permute-start.2 = (bf16[192,1152]{1,0:T(8,128)(2,1)S(1)}, bf16[192,1152]{1,0:T(8,128)(2,1)S(1)}, u32[]{:S(2)}, u32[]{:S(2)}) collective-permute-start(bf16[192,1152]{1,0:T(8,128)(2,1)S(1)} %get-tuple-element.23), channel_id=1, source_target_pairs={{0,1},{1,0},{2,3},{3,2},{4,5},{5,4},{6,7},{7,6},{8,9},{9,8},{10,11... | collective-permute-start | bytes 1327112 | tf_op jit(solution)/shard_map/ppermute | solution.py:597
  26.3 3.1 %copy-start.1 = (f32[2304]{0:T(1024)S(1)}, f32[2304]{0:T(1024)}, u32[]{:S(2)}) copy-start(f32[2304]{0:T(1024)} %refs_7_.3) | copy-start | bytes 27652
  26.3 3.1 %collective-permute-start.3 = (bf16[192,1152]{1,0:T(8,128)(2,1)S(1)}, bf16[192,1152]{1,0:T(8,128)(2,1)S(1)}, u32[]{:S(2)}, u32[]{:S(2)}) collective-permute-start(bf16[192,1152]{1,0:T(8,128)(2,1)S(1)} %get-tuple-element.24), channel_id=1, source_target_pairs={{0,1},{1,0},{2,3},{3,2},{4,5},{5,4},{6,7},{7,6},{8,9},{9,8},{10,11... | collective-permute-start | bytes 1327112 | tf_op jit(solution)/shard_map/ppermute | solution.py:597
  27.6 23.0 %collective-permute-start.4 = (bf16[384,1152]{1,0:T(8,128)(2,1)S(1)}, bf16[384,1152]{1,0:T(8,128)(2,1)S(1)}, u32[]{:S(2)}, u32[]{:S(2)}) collective-permute-start(bf16[384,1152]{1,0:T(8,128)(2,1)S(1)} %far_weight.1.refs_13_.first_ref.refs_5_), channel_id=1, source_target_pairs={{0,2},{1,3},{2,0},{3,1},{4,6},{5,7},{6,4},{7,5},{8,10},{9,11},{10,... | collective-permute-start | bytes 2654216 | tf_op jit(solution)/shard_map/ppermute | solution.py:599
  35.6 15.2 %collective-permute-start.10 = (bf16[128,768]{1,0:T(8,128)(2,1)S(1)}, bf16[128,768]{1,0:T(8,128)(2,1)S(1)}, u32[]{:S(2)}, u32[]{:S(2)}) collective-permute-start(bf16[128,768]{1,0:T(8,128)(2,1)S(1)} %get-tuple-element.31), channel_id=1, source_target_pairs={{4,12},{8,0},{5,13},{9,1},{6,14},{10,2},{7,15},{11,3},{20,28},{24,... | collective-permute-start | bytes 589832 | tf_op jit(solution)/shard_map/ppermute | solution.py:608
  39.0 10.7 %collective-permute-start.8 = (bf16[128,384]{1,0:T(8,128)(2,1)S(1)}, bf16[128,384]{1,0:T(8,128)(2,1)S(1)}, u32[]{:S(2)}, u32[]{:S(2)}) collective-permute-start(bf16[128,384]{1,0:T(8,128)(2,1)S(1)} %get-tuple-element.30), channel_id=1, source_target_pairs={{4,12},{8,0},{5,13},{9,1},{6,14},{10,2},{7,15},{11,3},{20,28},{24,... | collective-permute-start | bytes 294920 | tf_op jit(solution)/shard_map/ppermute | solution.py:610
  40.3 13.6 %collective-permute-start.11 = (bf16[128,768]{1,0:T(8,128)(2,1)S(1)}, bf16[128,768]{1,0:T(8,128)(2,1)S(1)}, u32[]{:S(2)}, u32[]{:S(2)}) collective-permute-start(bf16[128,768]{1,0:T(8,128)(2,1)S(1)} %get-tuple-element.32), channel_id=1, source_target_pairs={{4,0},{8,12},{5,1},{9,13},{6,2},{10,14},{7,3},{11,15},{20,16},{24,... | collective-permute-start | bytes 589832 | tf_op jit(solution)/shard_map/ppermute | solution.py:607
  41.6 14.4 %collective-permute-start.12 = (bf16[128,384]{1,0:T(8,128)(2,1)S(1)}, bf16[128,384]{1,0:T(8,128)(2,1)S(1)}, u32[]{:S(2)}, u32[]{:S(2)}) collective-permute-start(bf16[128,384]{1,0:T(8,128)(2,1)S(1)} %get-tuple-element.35), channel_id=1, source_target_pairs={{4,0},{8,12},{5,1},{9,13},{6,2},{10,14},{7,3},{11,15},{20,16},{24,... | collective-permute-start | bytes 294920 | tf_op jit(solution)/shard_map/ppermute | solution.py:612
  49.7 1.0 %copy-start.4 = (bf16[1,128,1536]{2,1,0:T(8,128)(2,1)S(1)}, bf16[1,128,1536]{2,1,0:T(8,128)(2,1)}, u32[]{:S(2)}) copy-start(bf16[1,128,1536]{2,1,0:T(8,128)(2,1)} %refs_10_.1) | copy-start | bytes 1179652
  49.7 6.2 %collective-permute-start.13 = (bf16[128,1152]{1,0:T(8,128)(2,1)S(1)}, bf16[128,1152]{1,0:T(8,128)(2,1)S(1)}, u32[]{:S(2)}, u32[]{:S(2)}) collective-permute-start(bf16[128,1152]{1,0:T(8,128)(2,1)S(1)} %get-tuple-element.36), channel_id=1, source_target_pairs={{4,8},{8,4},{5,9},{9,5},{6,10},{10,6},{7,11},{11,7},{20,24},{24,20... | collective-permute-start | bytes 884744 | tf_op jit(solution)/shard_map/ppermute | solution.py:611
  50.7 3.8 %collective-permute-start.9 = (bf16[768,1152]{1,0:T(8,128)(2,1)S(1)}, bf16[768,1152]{1,0:T(8,128)(2,1)S(1)}, u32[]{:S(2)}, u32[]{:S(2)}) collective-permute-start(bf16[768,1152]{1,0:T(8,128)(2,1)S(1)} %chip_weight.1), channel_id=1, source_target_pairs={{0,1},{1,0},{2,3},{3,2},{4,5},{5,4},{6,7},{7,6},{8,9},{9,8},{10,11... | collective-permute-start | bytes 5308424 | tf_op jit(solution)/shard_map/ppermute | solution.py:613
  54.4 1.5 %copy-start.2 = (f32[1536]{0:T(1024)S(1)}, f32[1536]{0:T(1024)}, u32[]{:S(2)}) copy-start(f32[1536]{0:T(1024)} %refs_13_.1) | copy-start | bytes 18436

commit v8 on v7

--- a/solution.py
+++ b/solution.py
@@ -426,14 +426,38 @@
         in_specs=[spec()] * 11,
         out_specs=(spec(),) * 3,
         compiler_params=pltpu.CompilerParams(vmem_limit_bytes=24 * 2**20),
-        cost_estimate=cost(50),
+        cost_estimate=cost(0.01),
         name="grad_norm_part",
     )(*near_w, *far_w, own, *skips, tokens)
 
 
-def pair_part_kernel(*refs):
-    near_w = refs[0:5]
-    pair, skip_first, skip_second, back_first, sums, out_ref = refs[5:]
+def back_part_kernel(*refs):
+    near_w, back_first, sums, out_ref = refs[0:5], refs[5], refs[6], refs[7]
+    depth = near_w[0].shape[0]
+    mine = lax.axis_index("weight")
+    out_ref[...] = sums[...]
+
+    @pl.when(jnp.logical_not(on_middle()))
+    def _():
+        back = back_first[...]
+        for j in range(4):
+            at = pl.ds(pl.multiple_of((mine ^ j) * depth, QBLOCK), depth)
+            out_ref[:, at] = sums[:, at] + dot_last(back, near_shard(near_w, j, EARLY))
+
+
+def back_part_step(near_w, back_first, sums):
+    return pl.pallas_call(
+        back_part_kernel,
+        out_shape=jax.ShapeDtypeStruct(sums.shape, sums.dtype),
+        in_specs=[spec()] * 7,
+        out_specs=spec(),
+        compiler_params=pltpu.CompilerParams(vmem_limit_bytes=24 * 2**20),
+        cost_estimate=cost(50),
+        name="back_part",
+    )(*near_w, back_first, sums)
+
+
+def pair_part_kernel(pair, skip_first, skip_second, sums, out_ref):
     mine = lax.axis_index("weight")
     depth = pair.shape[0] // 2
     out_ref[...] = sums[...]
@@ -441,29 +465,26 @@
     @pl.when(jnp.logical_not(on_middle()))
     def _():
         skip = join_skip(skip_first, skip_second)
-        for j in range(4):
+        for i, j in enumerate((1, 3)):
             at = pl.ds(pl.multiple_of((mine ^ j) * depth, QBLOCK), depth)
-            total = sums[:, at] + dot_last(back_first[...], near_shard(near_w, j, EARLY))
-            if j % 2 == 1:
-                total += dot_last(skip, pair[j // 2 * depth : (j // 2 + 1) * depth])
-            out_ref[:, at] = total
-
-
-def pair_part_step(near_w, pair, skips, back_first, sums):
+            out_ref[:, at] = sums[:, at] + dot_last(skip, pair[i * depth : (i + 1) * depth])
+
+
+def pair_part_step(pair, skips, sums):
     return pl.pallas_call(
         pair_part_kernel,
         out_shape=jax.ShapeDtypeStruct(sums.shape, sums.dtype),
-        in_specs=[spec()] * 10,
+        in_specs=[spec()] * 4,
         out_specs=spec(),
         compiler_params=pltpu.CompilerParams(vmem_limit_bytes=24 * 2**20),
         cost_estimate=cost(0.01),
         name="pair_part",
-    )(*near_w, pair, *skips, back_first, sums)
+    )(pair, *skips, sums)
 
 
 def last_kernel(*refs):
     near_w, pair = refs[0:5], refs[7]
-    sums, back_ref, cross_ref, normed_ref, inverse_ref, gain_ref, out_ref = refs[8:15]
+    sums, cross_ref, back_ref, normed_ref, inverse_ref, gain_ref, out_ref = refs[8:15]
     gain, grad_hat, first_sum, second_sum, result, sems = refs[15:]
     middle = on_middle()
     mine = lax.axis_index("weight")
@@ -521,7 +542,7 @@
         compiler_params=pltpu.CompilerParams(vmem_limit_bytes=24 * 2**20),
         cost_estimate=cost(2),
         name="input_grad",
-    )(*near_w, *far_w, sums, back, cross, normed, inverse, gain)
+    )(*near_w, *far_w, sums, cross, back, normed, inverse, gain)
 
 
 def split_kernel(value_ref, upper_ref, lower_ref):
@@ -543,22 +564,23 @@
     )(value)
 
 
-def pair_kernel(first_ref, second_ref, after_ref, out_ref):
+def pair_kernel(first_ref, second_ref, *refs):
+    out_ref = refs[-1]
     middle = first_ref.shape[0]
     out_ref[:middle] = first_ref[...]
     out_ref[middle:] = second_ref[...]
 
 
-def pair_step(first, second, after):
+def pair_step(first, second, *after):
     return pl.pallas_call(
         pair_kernel,
         out_shape=jax.ShapeDtypeStruct((2 * first.shape[0], first.shape[1]), first.dtype),
-        in_specs=[spec()] * 3,
+        in_specs=[spec()] * (2 + len(after)),
         out_specs=spec(),
         compiler_params=pltpu.CompilerParams(vmem_limit_bytes=16 * 2**20),
         cost_estimate=cost(0.01),
         name="chip_weight",
-    )(first, second, after)
+    )(first, second, *after)
 
 
 EARLY = (0, 1)
@@ -610,11 +632,12 @@
     skip_second = lax.ppermute(skip_second, "seq", FAR_TO_END)
     cross = lax.ppermute(mid, "seq", MIDDLE)
     back = lax.ppermute(end, "seq", MIDDLE_TO_END)
-    far_pair = lax.ppermute(pair_step(far, far_across, skip_second), "weight", flip(1))
+    far_pair = lax.ppermute(pair_step(far, far_across, skip_first, own), "weight", flip(1))
     far_w = (far, far_across)
     skips = (skip_first, skip_second)
     sums, normed, inverse = early_step(near_w, far_w, own, skips, tokens)
-    sums = pair_part_step(near_w, far_pair, skips, back_first, sums)
+    sums = back_part_step(near_w, back_first, sums)
+    sums = pair_part_step(far_pair, skips, sums)
     return last_step(near_w, (*far_w, far_pair), back, cross, sums, normed, inverse, norm_gain)
 
 

time: 58.1 us -> 58 us (level)
    ppermute x1, waiting for transfers between devices: 6.85 us -> 0.66 us  [local_middle(): skip_second = lax.ppermute(skip_second, 'seq', FAR_TO_END)]
    ppermute x1, waiting for transfers between devices: 0.01 us -> 5.36 us  [local_middle(): skip_first = lax.ppermute(skip_first, 'seq', FAR_TO_END)]
    pallas_call x0 -> x1, Pallas kernels: none -> 0.84 us  [back_part_step(): pl.pallas_call(back_part_kernel, out_shape=jax.ShapeDtypeStruct(sums.shap...]
    pallas_call x1, Pallas kernels: 1.42 us -> 0.7 us  [pair_part_step(): pl.pallas_call(pair_part_kernel, out_shape=jax.ShapeDtypeStruct(sums.shap...]
  transfers between devices with their start and end apart: 14 -> 14, of which waited for: 5 -> 6; matrix products, arithmetic and copies ran while one was open for 0% -> 0% of each run, Pallas kernels for 20% -> 21%
where the time goes in v8:
time: 58 us; the launch traced here: 57.7 us
  waiting for transfers between devices  20.8 us (36%)
  starting transfers between devices  19.5 us (34%)
  Pallas kernels  17 us (29%)
    ppermute x1, waiting for transfers between devices, local_middle(): near_across = lax.ppermute(near, 'weight', flip(2))  11.4 us
    ppermute x1, waiting for transfers between devices, local_middle(): skip_first = lax.ppermute(skip_first, 'seq', FAR_TO_END)  5.36 us
    pallas_call x1, Pallas kernels, project_attention_step(): pl.pallas_call(functools.partial(project_attention_kernel, pairs), out_sh...  4.81 us
    ppermute x1, starting transfers between devices, local_middle(): both_far = lax.ppermute(both_other, 'seq', END_TO_FAR)  3.97 us
    ppermute x1, starting transfers between devices, local_middle(): both_end = lax.ppermute(both_near, 'seq', END_TO_MIDDLE)  3.5 us
    pallas_call x1, Pallas kernels, first_step(): pl.pallas_call(first_kernel, out_shape=(VMEM((depth, 3 * HALF), jnp.bfloa...  3.44 us
    ppermute x1, starting transfers between devices, local_middle(): near_across = lax.ppermute(near, 'weight', flip(2))  3 us
    ppermute x1, waiting for transfers between devices, local_middle(): back_first = lax.ppermute(end, 'seq', MIDDLE_TO_END)  2.53 us
  transfers between devices with their start and end apart: 14, of which 6 were waited for; matrix products, arithmetic and copies ran while one was open for 0% of the time, Pallas kernels for 21%

profile of v8, /device:TPU:0, one launch (start us, length us, event | category | flops | bytes accessed | tf_op | source)
XLA Modules:
  0.0 57.7 jit_solution(9645098986661912169)
XLA Ops:
  0.0 3.4 %first_weights_and_rows.1 = (bf16[384,1152]{1,0:T(8,128)(2,1)S(1)}, bf16[128,1920]{1,0:T(8,128)(2,1)S(1)}, bf16[128,1920]{1,0:T(8,128)(2,1)}) custom-call(bf16[1,128,1536]{2,1,0:T(8,128)(2,1)} %refs_10_.1, f32[1536]{0:T(1024)} %refs_13_.1, f32[1536]{0:T(1024)} %shift_ref.1, f32[3,18]{1,0:T(4,128)} %scales_ref.3, bf16[384,2304]{1,0:T(8,128)(2,1)} %codes_ref.3, ...), custom_call_target="tpu_custom_call" | custom-call | flops 3000000000 | bytes 9000000 | tf_op jit(solution)/shard_map/first_weights_and_rows/pallas_call | solution.py:121
  3.5 3.0 %collective-permute-start.1 = (bf16[384,1152]{1,0:T(8,128)(2,1)S(1)}, bf16[384,1152]{1,0:T(8,128)(2,1)S(1)}, u32[]{:S(2)}, u32[]{:S(2)}) collective-permute-start(bf16[384,1152]{1,0:T(8,128)(2,1)S(1)} %get-tuple-element.22.refs_2_.refs_0_), channel_id=1, source_target_pairs={{0,2},{1,3},{2,0},{3,1},{4,6},{5,7},{6,4},{7,5},{8,10},{9,11},{10,... | collective-permute-start | bytes 2654216 | tf_op jit(solution)/shard_map/ppermute | solution.py:617
  6.5 3.5 %collective-permute-start.7 = (bf16[128,1920]{1,0:T(8,128)(2,1)S(1)}, bf16[128,1920]{1,0:T(8,128)(2,1)S(1)}, u32[]{:S(2)}, u32[]{:S(2)}) collective-permute-start(bf16[128,1920]{1,0:T(8,128)(2,1)S(1)} %get-tuple-element.26.refs_0_.refs_9_.refs_1_), channel_id=1, source_target_pairs={{0,4},{12,8},{1,5},{13,9},{2,6},{14,10},{3,7},{15,11},{16,20},{28,... | collective-permute-start | bytes 1474568 | tf_op jit(solution)/shard_map/ppermute | solution.py:616
  10.0 0.1 collective-permute-start
  10.0 0.7 %collective-permute-start.5 = (bf16[128,1920]{1,0:T(8,128)(2,1)}, bf16[128,1920]{1,0:T(8,128)(2,1)S(1)}, u32[]{:S(2)}, u32[]{:S(2)}) collective-permute-start(bf16[128,1920]{1,0:T(8,128)(2,1)} %get-tuple-element.25), channel_id=1, source_target_pairs={{4,8},{8,4},{5,9},{9,5},{6,10},{10,6},{7,11},{11,7},{20,24},{24,20... | collective-permute-start | bytes 1474568 | tf_op jit(solution)/shard_map/ppermute | solution.py:614
  10.7 4.0 %collective-permute-start.6 = (bf16[128,1920]{1,0:T(8,128)(2,1)}, bf16[128,1920]{1,0:T(8,128)(2,1)S(1)}, u32[]{:S(2)}, u32[]{:S(2)}) collective-permute-start(bf16[128,1920]{1,0:T(8,128)(2,1)} %get-tuple-element.25), channel_id=1, source_target_pairs={{0,8},{12,4},{1,9},{13,5},{2,10},{14,6},{3,11},{15,7},{16,24},{28,... | collective-permute-start | bytes 1474568 | tf_op jit(solution)/shard_map/ppermute | solution.py:615
  14.7 11.4 %collective-permute-done.1.value_ref.after_ref.refs_4_.refs_2_ = bf16[384,1152]{1,0:T(8,128)(2,1)S(1)} collective-permute-done((bf16[384,1152]{1,0:T(8,128)(2,1)S(1)}, bf16[384,1152]{1,0:T(8,128)(2,1)S(1)}, u32[]{:S(2)}, u32[]{:S(2)}) %collective-permute-start.1) | collective-permute-done | bytes 884768 | tf_op jit(solution)/shard_map/ppermute | solution.py:617
  26.1 0.1 split_rows.1
  26.2 0.1 collective-permute-start.2
  26.3 0.5 collective-permute-start.3
  26.8 0.8 %far_weight.1.refs_13_.first_ref.refs_5_ = bf16[384,1152]{1,0:T(8,128)(2,1)S(1)} custom-call(f32[3,18]{1,0:T(4,128)S(1)} %copy-done.4, bf16[384,2304]{1,0:T(8,128)(2,1)S(1)} %copy-done, bf16[384,1152]{1,0:T(8,128)(2,1)S(1)} %collective-permute-done.1.value_ref.after_ref.refs_4_.refs_2_), custom_call_target="tpu_custom_call" | custom-call | flops 10000000 | bytes 30000 | tf_op jit(solution)/shard_map/far_weight/pallas_call | solution.py:174
  27.6 1.8 %collective-permute-start.4 = (bf16[384,1152]{1,0:T(8,128)(2,1)S(1)}, bf16[384,1152]{1,0:T(8,128)(2,1)S(1)}, u32[]{:S(2)}, u32[]{:S(2)}) collective-permute-start(bf16[384,1152]{1,0:T(8,128)(2,1)S(1)} %far_weight.1.refs_13_.first_ref.refs_5_), channel_id=1, source_target_pairs={{0,2},{1,3},{2,0},{3,1},{4,6},{5,7},{6,4},{7,5},{8,10},{9,11},{10,... | collective-permute-start | bytes 2654216 | tf_op jit(solution)/shard_map/ppermute | solution.py:621
  29.4 1.4 %projection.1.refs_8_ = bf16[512,1152]{1,0:T(8,128)(2,1)S(1)} custom-call(bf16[128,1920]{1,0:T(8,128)(2,1)S(1)} %get-tuple-element.26.refs_0_.refs_9_.refs_1_, bf16[128,1920]{1,0:T(8,128)(2,1)S(1)} %collective-permute-done.7.refs_1_.refs_10_.refs_2_, bf16[384,1152]{1,0:T(8,128)(2,1)S(1)} %get-tuple-element.22.refs_2_.refs_0_, ...), custom_call_target="tpu_custom_call" | custom-call | flops 10000000 | bytes 30000 | tf_op jit(solution)/shard_map/projection/pallas_call | solution.py:236
  30.8 4.8 %projection_attention.1 = (bf16[512,1152]{1,0:T(8,128)(2,1)S(1)}, bf16[128,768]{1,0:T(8,128)(2,1)S(1)}, bf16[128,768]{1,0:T(8,128)(2,1)S(1)}, bf16[128,768]{1,0:T(8,128)(2,1)S(1)}, bf16[128,768]{1,0:T(8,128)(2,1)S(1)}) custom-call(bf16[128,1920]{1,0:T(8,128)(2,1)S(1)} %collective-permute-done.5.refs_0_.refs_11_.refs_3_, ...), custom_call_target="tpu_custom_call", output_to_operand_aliasing={{0}: (8, {})} | custom-call | flops 12000000000 | bytes 36000000 | tf_op jit(solution)/shard_map/projection_attention/pallas_call | solution.py:345
  35.6 1.3 %collective-permute-start.8 = (bf16[128,768]{1,0:T(8,128)(2,1)S(1)}, bf16[128,768]{1,0:T(8,128)(2,1)S(1)}, u32[]{:S(2)}, u32[]{:S(2)}) collective-permute-start(bf16[128,768]{1,0:T(8,128)(2,1)S(1)} %get-tuple-element.27), channel_id=1, source_target_pairs={{4,12},{8,0},{5,13},{9,1},{6,14},{10,2},{7,15},{11,3},{20,28},{24,... | collective-permute-start | bytes 589832 | tf_op jit(solution)/shard_map/ppermute | solution.py:630
  36.9 1.3 %collective-permute-start.11 = (bf16[128,768]{1,0:T(8,128)(2,1)S(1)}, bf16[128,768]{1,0:T(8,128)(2,1)S(1)}, u32[]{:S(2)}, u32[]{:S(2)}) collective-permute-start(bf16[128,768]{1,0:T(8,128)(2,1)S(1)} %get-tuple-element.33), channel_id=1, source_target_pairs={{4,0},{8,12},{5,1},{9,13},{6,2},{10,14},{7,3},{11,15},{20,16},{24,... | collective-permute-start | bytes 589832 | tf_op jit(solution)/shard_map/ppermute | solution.py:629
  38.2 2.1 %attention.1 = (bf16[128,1152]{1,0:T(8,128)(2,1)S(1)}, bf16[128,384]{1,0:T(8,128)(2,1)S(1)}, bf16[128,1152]{1,0:T(8,128)(2,1)S(1)}, bf16[128,384]{1,0:T(8,128)(2,1)S(1)}) custom-call(bf16[512,1152]{1,0:T(8,128)(2,1)S(1)} %get-tuple-element.28.refs_0_, bf16[128,1920]{1,0:T(8,128)(2,1)S(1)} %get-tuple-element.26.refs_0_.refs_9_.refs_1_, ...), custom_call_target="tpu_custom_call" | custom-call | flops 12000000000 | bytes 36000000 | tf_op jit(solution)/shard_map/attention/pallas_call | solution.py:363
  40.3 1.3 %collective-permute-start.10 = (bf16[128,384]{1,0:T(8,128)(2,1)S(1)}, bf16[128,384]{1,0:T(8,128)(2,1)S(1)}, u32[]{:S(2)}, u32[]{:S(2)}) collective-permute-start(bf16[128,384]{1,0:T(8,128)(2,1)S(1)} %get-tuple-element.32), channel_id=1, source_target_pairs={{4,12},{8,0},{5,13},{9,1},{6,14},{10,2},{7,15},{11,3},{20,28},{24,... | collective-permute-start | bytes 294920 | tf_op jit(solution)/shard_map/ppermute | solution.py:632
  41.6 0.7 %collective-permute-start.12 = (bf16[128,1152]{1,0:T(8,128)(2,1)S(1)}, bf16[128,1152]{1,0:T(8,128)(2,1)S(1)}, u32[]{:S(2)}, u32[]{:S(2)}) collective-permute-start(bf16[128,1152]{1,0:T(8,128)(2,1)S(1)} %get-tuple-element.35), channel_id=1, source_target_pairs={{4,8},{8,4},{5,9},{9,5},{6,10},{10,6},{7,11},{11,7},{20,24},{24,20... | collective-permute-start | bytes 884744 | tf_op jit(solution)/shard_map/ppermute | solution.py:633
  42.3 5.4 %collective-permute-done.8.refs_0_.refs_8_.skip_first = bf16[128,768]{1,0:T(8,128)(2,1)S(1)} collective-permute-done((bf16[128,768]{1,0:T(8,128)(2,1)S(1)}, bf16[128,768]{1,0:T(8,128)(2,1)S(1)}, u32[]{:S(2)}, u32[]{:S(2)}) %collective-permute-start.8) | collective-permute-done | bytes 196640 | tf_op jit(solution)/shard_map/ppermute | solution.py:630
  47.6 1.3 %collective-permute-start.13 = (bf16[128,384]{1,0:T(8,128)(2,1)S(1)}, bf16[128,384]{1,0:T(8,128)(2,1)S(1)}, u32[]{:S(2)}, u32[]{:S(2)}) collective-permute-start(bf16[128,384]{1,0:T(8,128)(2,1)S(1)} %get-tuple-element.36), channel_id=1, source_target_pairs={{4,0},{8,12},{5,1},{9,13},{6,2},{10,14},{7,3},{11,15},{20,16},{24,... | collective-permute-start | bytes 294920 | tf_op jit(solution)/shard_map/ppermute | solution.py:634
  48.9 0.4 collective-permute-done.4.second_ref.refs_6_
  49.3 0.1 chip_weight.1
  49.4 0.1 collective-permute-start.9
  49.5 0.7 %collective-permute-done.10.refs_9_.skip_second = bf16[128,384]{1,0:T(8,128)(2,1)S(1)} collective-permute-done((bf16[128,384]{1,0:T(8,128)(2,1)S(1)}, bf16[128,384]{1,0:T(8,128)(2,1)S(1)}, u32[]{:S(2)}, u32[]{:S(2)}) %collective-permute-start.10) | collective-permute-done | bytes 98336 | tf_op jit(solution)/shard_map/ppermute | solution.py:632
  50.1 0.1 copy-done.1
  50.3 1.1 %grad_norm_part.1 = (f32[128,1536]{1,0:T(8,128)S(1)}, f32[128,1536]{1,0:T(8,128)S(1)}, f32[128,128]{1,0:T(8,128)S(1)}) custom-call(bf16[384,1152]{1,0:T(8,128)(2,1)S(1)} %get-tuple-element.22.refs_2_.refs_0_, bf16[384,1152]{1,0:T(8,128)(2,1)S(1)} %collective-permute-done.refs_3_.refs_1_, ...), custom_call_target="tpu_custom_call" | custom-call | flops 10000000 | bytes 30000 | tf_op jit(solution)/shard_map/grad_norm_part/pallas_call | solution.py:423
  51.4 2.5 %collective-permute-done.11.refs_5_ = bf16[128,768]{1,0:T(8,128)(2,1)S(1)} collective-permute-done((bf16[128,768]{1,0:T(8,128)(2,1)S(1)}, bf16[128,768]{1,0:T(8,128)(2,1)S(1)}, u32[]{:S(2)}, u32[]{:S(2)}) %collective-permute-start.11) | collective-permute-done | bytes 196640 | tf_op jit(solution)/shard_map/ppermute | solution.py:629
  53.9 0.8 %back_part.1.sums = f32[128,1536]{1,0:T(8,128)S(1)} custom-call(bf16[384,1152]{1,0:T(8,128)(2,1)S(1)} %get-tuple-element.22.refs_2_.refs_0_, bf16[384,1152]{1,0:T(8,128)(2,1)S(1)} %collective-permute-done.refs_3_.refs_1_, bf16[384,1152]{1,0:T(8,128)(2,1)S(1)} %collective-permute-done.1.value_ref.after_ref.refs_4_.refs_2_, ...), custom_call_target="tpu_custom_call" | custom-call | flops 49999998976 | bytes 150000000 | tf_op jit(solution)/shard_map/back_part/pallas_call | solution.py:449
  54.8 0.7 %pair_part.1.refs_8_ = f32[128,1536]{1,0:T(8,128)S(1)} custom-call(bf16[768,1152]{1,0:T(8,128)(2,1)S(1)} %collective-permute-done.9.pair.refs_7_, bf16[128,768]{1,0:T(8,128)(2,1)S(1)} %collective-permute-done.8.refs_0_.refs_8_.skip_first, bf16[128,384]{1,0:T(8,128)(2,1)S(1)} %collective-permute-done.10.refs_9_.skip_second, f32[128,1536]{1,0:T(8,128)S(1)} %back_part.1.sums), custom_call_target="tpu_custom_call" | custom-call | flops 10000000 | bytes 30000 | tf_op jit(solution)/shard_map/pair_part/pallas_call | solution.py:474
  55.5 0.4 collective-permute-done.13.refs_10_
  55.9 1.6 %input_grad.1 = f32[1,128,1536]{2,1,0:T(8,128)} custom-call(bf16[384,1152]{1,0:T(8,128)(2,1)S(1)} %get-tuple-element.22.refs_2_.refs_0_, bf16[384,1152]{1,0:T(8,128)(2,1)S(1)} %collective-permute-done.refs_3_.refs_1_, bf16[384,1152]{1,0:T(8,128)(2,1)S(1)} %collective-permute-done.1.value_ref.after_ref.refs_4_.refs_2_, ...), custom_call_target="tpu_custom_call" | custom-call | flops 2000000000 | bytes 6000000 | tf_op jit(solution)/shard_map/input_grad/pallas_call | solution.py:529
  (17 shorter events, 0.1 us)
Async XLA Ops:
  0.0 26.8 %copy-start.4 = (f32[3,18]{1,0:T(4,128)S(1)}, f32[3,18]{1,0:T(4,128)}, u32[]{:S(2)}) copy-start(f32[3,18]{1,0:T(4,128)} %scales_ref.3) | copy-start | bytes 652
  0.0 26.8 %copy-start = (bf16[384,2304]{1,0:T(8,128)(2,1)S(1)}, bf16[384,2304]{1,0:T(8,128)(2,1)}, u32[]{:S(2)}) copy-start(bf16[384,2304]{1,0:T(8,128)(2,1)} %codes_ref.3) | copy-start | bytes 5308420
  3.5 22.7 %collective-permute-start.1 = (bf16[384,1152]{1,0:T(8,128)(2,1)S(1)}, bf16[384,1152]{1,0:T(8,128)(2,1)S(1)}, u32[]{:S(2)}, u32[]{:S(2)}) collective-permute-start(bf16[384,1152]{1,0:T(8,128)(2,1)S(1)} %get-tuple-element.22.refs_2_.refs_0_), channel_id=1, source_target_pairs={{0,2},{1,3},{2,0},{3,1},{4,6},{5,7},{6,4},{7,5},{8,10},{9,11},{10,... | collective-permute-start | bytes 2654216 | tf_op jit(solution)/shard_map/ppermute | solution.py:617
  6.5 19.8 %collective-permute-start.7 = (bf16[128,1920]{1,0:T(8,128)(2,1)S(1)}, bf16[128,1920]{1,0:T(8,128)(2,1)S(1)}, u32[]{:S(2)}, u32[]{:S(2)}) collective-permute-start(bf16[128,1920]{1,0:T(8,128)(2,1)S(1)} %get-tuple-element.26.refs_0_.refs_9_.refs_1_), channel_id=1, source_target_pairs={{0,4},{12,8},{1,5},{13,9},{2,6},{14,10},{3,7},{15,11},{16,20},{28,... | collective-permute-start | bytes 1474568 | tf_op jit(solution)/shard_map/ppermute | solution.py:616
  10.0 17.6 %collective-permute-start = (bf16[384,1152]{1,0:T(8,128)(2,1)S(1)}, bf16[384,1152]{1,0:T(8,128)(2,1)S(1)}, u32[]{:S(2)}, u32[]{:S(2)}) collective-permute-start(bf16[384,1152]{1,0:T(8,128)(2,1)S(1)} %get-tuple-element.22.refs_2_.refs_0_), channel_id=1, source_target_pairs={{0,1},{1,0},{2,3},{3,2},{4,5},{5,4},{6,7},{7,6},{8,9},{9,8},{10,11... | collective-permute-start | bytes 2654216 | tf_op jit(solution)/shard_map/ppermute | solution.py:618
  10.0 20.7 %collective-permute-start.5 = (bf16[128,1920]{1,0:T(8,128)(2,1)}, bf16[128,1920]{1,0:T(8,128)(2,1)S(1)}, u32[]{:S(2)}, u32[]{:S(2)}) collective-permute-start(bf16[128,1920]{1,0:T(8,128)(2,1)} %get-tuple-element.25), channel_id=1, source_target_pairs={{4,8},{8,4},{5,9},{9,5},{6,10},{10,6},{7,11},{11,7},{20,24},{24,20... | collective-permute-start | bytes 1474568 | tf_op jit(solution)/shard_map/ppermute | solution.py:614
  10.7 20.1 %collective-permute-start.6 = (bf16[128,1920]{1,0:T(8,128)(2,1)}, bf16[128,1920]{1,0:T(8,128)(2,1)S(1)}, u32[]{:S(2)}, u32[]{:S(2)}) collective-permute-start(bf16[128,1920]{1,0:T(8,128)(2,1)} %get-tuple-element.25), channel_id=1, source_target_pairs={{0,8},{12,4},{1,9},{13,5},{2,10},{14,6},{3,11},{15,7},{16,24},{28,... | collective-permute-start | bytes 1474568 | tf_op jit(solution)/shard_map/ppermute | solution.py:615
  26.2 3.2 %collective-permute-start.2 = (bf16[192,1152]{1,0:T(8,128)(2,1)S(1)}, bf16[192,1152]{1,0:T(8,128)(2,1)S(1)}, u32[]{:S(2)}, u32[]{:S(2)}) collective-permute-start(bf16[192,1152]{1,0:T(8,128)(2,1)S(1)} %get-tuple-element.23), channel_id=1, source_target_pairs={{0,1},{1,0},{2,3},{3,2},{4,5},{5,4},{6,7},{7,6},{8,9},{9,8},{10,11... | collective-permute-start | bytes 1327112 | tf_op jit(solution)/shard_map/ppermute | solution.py:619
  26.3 3.1 %copy-start.2 = (f32[2304]{0:T(1024)S(1)}, f32[2304]{0:T(1024)}, u32[]{:S(2)}) copy-start(f32[2304]{0:T(1024)} %refs_7_.3) | copy-start | bytes 27652
  26.3 3.1 %collective-permute-start.3 = (bf16[192,1152]{1,0:T(8,128)(2,1)S(1)}, bf16[192,1152]{1,0:T(8,128)(2,1)S(1)}, u32[]{:S(2)}, u32[]{:S(2)}) collective-permute-start(bf16[192,1152]{1,0:T(8,128)(2,1)S(1)} %get-tuple-element.24), channel_id=1, source_target_pairs={{0,1},{1,0},{2,3},{3,2},{4,5},{5,4},{6,7},{7,6},{8,9},{9,8},{10,11... | collective-permute-start | bytes 1327112 | tf_op jit(solution)/shard_map/ppermute | solution.py:619
  27.6 21.7 %collective-permute-start.4 = (bf16[384,1152]{1,0:T(8,128)(2,1)S(1)}, bf16[384,1152]{1,0:T(8,128)(2,1)S(1)}, u32[]{:S(2)}, u32[]{:S(2)}) collective-permute-start(bf16[384,1152]{1,0:T(8,128)(2,1)S(1)} %far_weight.1.refs_13_.first_ref.refs_5_), channel_id=1, source_target_pairs={{0,2},{1,3},{2,0},{3,1},{4,6},{5,7},{6,4},{7,5},{8,10},{9,11},{10,... | collective-permute-start | bytes 2654216 | tf_op jit(solution)/shard_map/ppermute | solution.py:621
  35.6 12.0 %collective-permute-start.8 = (bf16[128,768]{1,0:T(8,128)(2,1)S(1)}, bf16[128,768]{1,0:T(8,128)(2,1)S(1)}, u32[]{:S(2)}, u32[]{:S(2)}) collective-permute-start(bf16[128,768]{1,0:T(8,128)(2,1)S(1)} %get-tuple-element.27), channel_id=1, source_target_pairs={{4,12},{8,0},{5,13},{9,1},{6,14},{10,2},{7,15},{11,3},{20,28},{24,... | collective-permute-start | bytes 589832 | tf_op jit(solution)/shard_map/ppermute | solution.py:630
  36.9 17.0 %collective-permute-start.11 = (bf16[128,768]{1,0:T(8,128)(2,1)S(1)}, bf16[128,768]{1,0:T(8,128)(2,1)S(1)}, u32[]{:S(2)}, u32[]{:S(2)}) collective-permute-start(bf16[128,768]{1,0:T(8,128)(2,1)S(1)} %get-tuple-element.33), channel_id=1, source_target_pairs={{4,0},{8,12},{5,1},{9,13},{6,2},{10,14},{7,3},{11,15},{20,16},{24,... | collective-permute-start | bytes 589832 | tf_op jit(solution)/shard_map/ppermute | solution.py:629
  40.3 9.9 %collective-permute-start.10 = (bf16[128,384]{1,0:T(8,128)(2,1)S(1)}, bf16[128,384]{1,0:T(8,128)(2,1)S(1)}, u32[]{:S(2)}, u32[]{:S(2)}) collective-permute-start(bf16[128,384]{1,0:T(8,128)(2,1)S(1)} %get-tuple-element.32), channel_id=1, source_target_pairs={{4,12},{8,0},{5,13},{9,1},{6,14},{10,2},{7,15},{11,3},{20,28},{24,... | collective-permute-start | bytes 294920 | tf_op jit(solution)/shard_map/ppermute | solution.py:632
  41.6 14.4 %collective-permute-start.12 = (bf16[128,1152]{1,0:T(8,128)(2,1)S(1)}, bf16[128,1152]{1,0:T(8,128)(2,1)S(1)}, u32[]{:S(2)}, u32[]{:S(2)}) collective-permute-start(bf16[128,1152]{1,0:T(8,128)(2,1)S(1)} %get-tuple-element.35), channel_id=1, source_target_pairs={{4,8},{8,4},{5,9},{9,5},{6,10},{10,6},{7,11},{11,7},{20,24},{24,20... | collective-permute-start | bytes 884744 | tf_op jit(solution)/shard_map/ppermute | solution.py:633
  47.6 8.3 %collective-permute-start.13 = (bf16[128,384]{1,0:T(8,128)(2,1)S(1)}, bf16[128,384]{1,0:T(8,128)(2,1)S(1)}, u32[]{:S(2)}, u32[]{:S(2)}) collective-permute-start(bf16[128,384]{1,0:T(8,128)(2,1)S(1)} %get-tuple-element.36), channel_id=1, source_target_pairs={{4,0},{8,12},{5,1},{9,13},{6,2},{10,14},{7,3},{11,15},{20,16},{24,... | collective-permute-start | bytes 294920 | tf_op jit(solution)/shard_map/ppermute | solution.py:634
  49.3 1.0 %copy-start.1 = (bf16[1,128,1536]{2,1,0:T(8,128)(2,1)S(1)}, bf16[1,128,1536]{2,1,0:T(8,128)(2,1)}, u32[]{:S(2)}) copy-start(bf16[1,128,1536]{2,1,0:T(8,128)(2,1)} %refs_10_.1) | copy-start | bytes 1179652
  49.4 5.4 %collective-permute-start.9 = (bf16[768,1152]{1,0:T(8,128)(2,1)S(1)}, bf16[768,1152]{1,0:T(8,128)(2,1)S(1)}, u32[]{:S(2)}, u32[]{:S(2)}) collective-permute-start(bf16[768,1152]{1,0:T(8,128)(2,1)S(1)} %chip_weight.1), channel_id=1, source_target_pairs={{0,1},{1,0},{2,3},{3,2},{4,5},{5,4},{6,7},{7,6},{8,9},{9,8},{10,11... | collective-permute-start | bytes 5308424 | tf_op jit(solution)/shard_map/ppermute | solution.py:635
  54.8 1.2 %copy-start.3 = (f32[1536]{0:T(1024)S(1)}, f32[1536]{0:T(1024)}, u32[]{:S(2)}) copy-start(f32[1536]{0:T(1024)} %refs_13_.1) | copy-start | bytes 18436

commit v9 on v8

--- a/solution.py
+++ b/solution.py
@@ -67,15 +67,26 @@
     def rows(which):
         return out_codes_ref.at[pl.ds(pl.multiple_of(which * HALF, QBLOCK), HALF), :]
 
-    scales_copy = copy(scales_ref, scales, 0)
-    codes_copies = [copy(columns(part), codes.at[part], 1 + part) for part in range(3)]
     tokens_copies = [
         copy(tokens_ref, tokens, 4), copy(gain_ref, gain, 5), copy(shift_ref, shift, 6)
     ]
+    scales_copy = copy(scales_ref, scales, 0)
+    codes_copies = [copy(columns(part), codes.at[part], 1 + part) for part in range(3)]
     grad_copies = [
         copy(grad_ref, grad, 7), copy(layer_ref, layer, 8), copy(out_scales_ref, out_scales, 9)
     ]
     out_copies = [copy(rows(other), out_codes.at[0], 10), copy(rows(half), out_codes.at[1], 11)]
+
+    for started in tokens_copies:
+        started.wait()
+    width = tokens.shape[2]
+    gain_row = row_vector(gain)
+    shift_row = row_vector(shift)
+    for r in range(0, tokens.shape[1], 16):
+        normed, _ = norm_rows(tokens[0, r : r + 16, :].astype(jnp.float32))
+        norm_out = (normed * gain_row + shift_row).astype(jnp.bfloat16)
+        near_out[r : r + 16, :width] = norm_out
+        far[r : r + 16, :width] = norm_out
 
     scales_copy.wait()
     for part in range(3):
@@ -87,17 +98,6 @@
                 weight_out[lines, part * HALF + c * QBLOCK : part * HALF + (c + 1) * QBLOCK] = scale_block(
                     codes[part, lines, c * QBLOCK : (c + 1) * QBLOCK], scale
                 )
-
-    for started in tokens_copies:
-        started.wait()
-    width = tokens.shape[2]
-    gain_row = row_vector(gain)
-    shift_row = row_vector(shift)
-    for r in range(0, tokens.shape[1], 16):
-        normed, _ = norm_rows(tokens[0, r : r + 16, :].astype(jnp.float32))
-        norm_out = (normed * gain_row + shift_row).astype(jnp.bfloat16)
-        near_out[r : r + 16, :width] = norm_out
-        far[r : r + 16, :width] = norm_out
 
     for started in grad_copies:
         started.wait()
@@ -235,7 +235,7 @@
     tokens = norms[0].shape[0]
     return pl.pallas_call(
         project_kernel,
-        out_shape=jax.ShapeDtypeStruct((4 * tokens, 3 * HALF), jnp.bfloat16),
+        out_shape=jax.ShapeDtypeStruct((2 * tokens, 3 * HALF), jnp.bfloat16),
         in_specs=[spec()] * 8,
         out_specs=spec(),
         compiler_params=pltpu.CompilerParams(vmem_limit_bytes=24 * 2**20),
@@ -256,32 +256,33 @@
 
 
 def attention_kernel(pairs, held, *refs):
-    proj, grads, before, outs = refs[0], refs[1:5], refs[5:-4], refs[-4:]
+    proj, grads, before, outs = refs[0:2], refs[2:6], refs[6:-4], refs[-4:]
     attention(pairs, held, proj, grads, before, outs)
 
 
 def project_attention_kernel(pairs, *refs):
     norms, weights, bias_ref, proj_in, grads = refs[0:2], refs[2:7], refs[7], refs[8], refs[9:13]
     proj, outs = refs[-5], refs[-4:]
-    tokens = norms[0].shape[0]
-    proj[: 2 * tokens] = proj_in[: 2 * tokens]
 
     def project(part):
-        project_part(norms, weights, bias_ref, proj, 2 * tokens, part)
+        project_part(norms, weights, bias_ref, proj, 0, part)
 
     project(0)
     project(1)
-    attention(pairs, 0, proj, grads, (), outs, lambda: project(2))
+    attention(pairs, 0, (proj_in, proj), grads, (), outs, lambda: project(2))
 
 
 def attention(pairs, held, proj, grads, before, outs, between=None):
-    total = proj.shape[0]
+    total = sum(ref.shape[0] for ref in proj)
     tokens = grads[0].shape[0]
     low = lax.broadcasted_iota(jnp.int32, (total, PAIR), 1) < HEAD_DIM
     zero = jnp.zeros((total, PAIR), jnp.bfloat16)
 
     def load(t):
-        query, key, value = (proj[:, part * HALF + t * PAIR : part * HALF + (t + 1) * PAIR] for part in range(3))
+        query, key, value = (
+            jnp.concatenate([p[:, part * HALF + t * PAIR : part * HALF + (t + 1) * PAIR] for p in proj], axis=0)
+            for part in range(3)
+        )
         grad = jnp.concatenate(
             [g[:, g.shape[1] - HALF + t * PAIR : g.shape[1] - HALF + (t + 1) * PAIR] for g in grads], axis=0
         )
@@ -347,7 +348,6 @@
         out_shape=(jax.ShapeDtypeStruct(proj.shape, proj.dtype),) + (out,) * 4,
         in_specs=[spec()] * 14,
         out_specs=(spec(),) * 5,
-        input_output_aliases={8: 0},
         compiler_params=pltpu.CompilerParams(vmem_limit_bytes=24 * 2**20),
         cost_estimate=cost(12),
         name="projection_attention",
@@ -363,12 +363,12 @@
     return pl.pallas_call(
         functools.partial(attention_kernel, pairs, held),
         out_shape=tuple(jax.ShapeDtypeStruct((tokens, width), jnp.bfloat16) for width in widths),
-        in_specs=[spec()] * (5 + len(before)),
+        in_specs=[spec()] * (6 + len(before)),
         out_specs=(spec(),) * 4,
         compiler_params=pltpu.CompilerParams(vmem_limit_bytes=24 * 2**20),
         cost_estimate=cost(12),
         name="attention",
-    )(proj, *grads, *before)
+    )(*proj, *grads, *before)
 
 
 def near_shard(refs, j, pairs=None):
@@ -623,12 +623,12 @@
     near_w = (near, near_beside, near_across, *near_diagonal)
     proj = project_step(rows[:2], near_w, input_bias)
     grads = (both_near, both_end, both_mid, both_far)
-    proj, own, end, mid, skip_first = project_attention_step(
+    proj_last, own, end, mid, skip_first = project_attention_step(
         rows[2:], near_w, input_bias, proj, grads, EARLY, far
     )
     back_first = lax.ppermute(end, "seq", MIDDLE_TO_END)
     skip_first = lax.ppermute(skip_first, "seq", FAR_TO_END)
-    own, end, mid, skip_second = attention_step(proj, grads, LATE, (own, mid))
+    own, end, mid, skip_second = attention_step((proj, proj_last), grads, LATE, (own, mid))
     skip_second = lax.ppermute(skip_second, "seq", FAR_TO_END)
     cross = lax.ppermute(mid, "seq", MIDDLE)
     back = lax.ppermute(end, "seq", MIDDLE_TO_END)

time: 58 us -> 57.9 us (level)
  transfers between devices with their start and end apart: 14 -> 14, of which waited for: 6 -> 6; matrix products, arithmetic and copies ran while one was open for 0% -> 0% of each run, Pallas kernels for 21% -> 20%
where the time goes in v9:
time: 57.9 us; the launch traced here: 57.6 us
  waiting for transfers between devices  20.7 us (36%)
  starting transfers between devices  19.5 us (34%)
  Pallas kernels  16.8 us (29%)
    ppermute x1, waiting for transfers between devices, local_middle(): near_across = lax.ppermute(near, 'weight', flip(2))  11.4 us
    ppermute x1, waiting for transfers between devices, local_middle(): skip_first = lax.ppermute(skip_first, 'seq', FAR_TO_END)  5.41 us
    pallas_call x1, Pallas kernels, project_attention_step(): pl.pallas_call(functools.partial(project_attention_kernel, pairs), out_sh...  4.7 us
    ppermute x1, starting transfers between devices, local_middle(): both_far = lax.ppermute(both_other, 'seq', END_TO_FAR)  3.97 us
    ppermute x1, starting transfers between devices, local_middle(): both_end = lax.ppermute(both_near, 'seq', END_TO_MIDDLE)  3.5 us
    pallas_call x1, Pallas kernels, first_step(): pl.pallas_call(first_kernel, out_shape=(VMEM((depth, 3 * HALF), jnp.bfloa...  3.44 us
    ppermute x1, starting transfers between devices, local_middle(): near_across = lax.ppermute(near, 'weight', flip(2))  3.01 us
    ppermute x1, waiting for transfers between devices, local_middle(): back_first = lax.ppermute(end, 'seq', MIDDLE_TO_END)  2.43 us
  transfers between devices with their start and end apart: 14, of which 6 were waited for; matrix products, arithmetic and copies ran while one was open for 0% of the time, Pallas kernels for 20%

profile of v9, /device:TPU:0, one launch (start us, length us, event | category | flops | bytes accessed | tf_op | source)
XLA Modules:
  0.0 57.6 jit_solution(2887079794823515279)
XLA Ops:
  0.0 3.4 %first_weights_and_rows.1 = (bf16[384,1152]{1,0:T(8,128)(2,1)S(1)}, bf16[128,1920]{1,0:T(8,128)(2,1)S(1)}, bf16[128,1920]{1,0:T(8,128)(2,1)}) custom-call(bf16[1,128,1536]{2,1,0:T(8,128)(2,1)} %refs_10_.1, f32[1536]{0:T(1024)} %refs_13_.1, f32[1536]{0:T(1024)} %shift_ref.1, f32[3,18]{1,0:T(4,128)} %scales_ref.3, bf16[384,2304]{1,0:T(8,128)(2,1)} %codes_ref.3, ...), custom_call_target="tpu_custom_call" | custom-call | flops 3000000000 | bytes 9000000 | tf_op jit(solution)/shard_map/first_weights_and_rows/pallas_call | solution.py:121
  3.5 3.0 %collective-permute-start.1 = (bf16[384,1152]{1,0:T(8,128)(2,1)S(1)}, bf16[384,1152]{1,0:T(8,128)(2,1)S(1)}, u32[]{:S(2)}, u32[]{:S(2)}) collective-permute-start(bf16[384,1152]{1,0:T(8,128)(2,1)S(1)} %get-tuple-element.22.refs_2_.refs_0_), channel_id=1, source_target_pairs={{0,2},{1,3},{2,0},{3,1},{4,6},{5,7},{6,4},{7,5},{8,10},{9,11},{10,... | collective-permute-start | bytes 2654216 | tf_op jit(solution)/shard_map/ppermute | solution.py:617
  6.5 3.5 %collective-permute-start.7 = (bf16[128,1920]{1,0:T(8,128)(2,1)S(1)}, bf16[128,1920]{1,0:T(8,128)(2,1)S(1)}, u32[]{:S(2)}, u32[]{:S(2)}) collective-permute-start(bf16[128,1920]{1,0:T(8,128)(2,1)S(1)} %get-tuple-element.26.refs_0_.refs_9_.refs_2_), channel_id=1, source_target_pairs={{0,4},{12,8},{1,5},{13,9},{2,6},{14,10},{3,7},{15,11},{16,20},{28,... | collective-permute-start | bytes 1474568 | tf_op jit(solution)/shard_map/ppermute | solution.py:616
  10.0 0.1 collective-permute-start
  10.0 0.7 %collective-permute-start.5 = (bf16[128,1920]{1,0:T(8,128)(2,1)}, bf16[128,1920]{1,0:T(8,128)(2,1)S(1)}, u32[]{:S(2)}, u32[]{:S(2)}) collective-permute-start(bf16[128,1920]{1,0:T(8,128)(2,1)} %get-tuple-element.25), channel_id=1, source_target_pairs={{4,8},{8,4},{5,9},{9,5},{6,10},{10,6},{7,11},{11,7},{20,24},{24,20... | collective-permute-start | bytes 1474568 | tf_op jit(solution)/shard_map/ppermute | solution.py:614
  10.7 4.0 %collective-permute-start.6 = (bf16[128,1920]{1,0:T(8,128)(2,1)}, bf16[128,1920]{1,0:T(8,128)(2,1)S(1)}, u32[]{:S(2)}, u32[]{:S(2)}) collective-permute-start(bf16[128,1920]{1,0:T(8,128)(2,1)} %get-tuple-element.25), channel_id=1, source_target_pairs={{0,8},{12,4},{1,9},{13,5},{2,10},{14,6},{3,11},{15,7},{16,24},{28,... | collective-permute-start | bytes 1474568 | tf_op jit(solution)/shard_map/ppermute | solution.py:615
  14.7 11.4 %collective-permute-done.1.value_ref.after_ref.refs_4_.refs_2_ = bf16[384,1152]{1,0:T(8,128)(2,1)S(1)} collective-permute-done((bf16[384,1152]{1,0:T(8,128)(2,1)S(1)}, bf16[384,1152]{1,0:T(8,128)(2,1)S(1)}, u32[]{:S(2)}, u32[]{:S(2)}) %collective-permute-start.1) | collective-permute-done | bytes 884768 | tf_op jit(solution)/shard_map/ppermute | solution.py:617
  26.1 0.1 split_rows.1
  26.2 0.1 collective-permute-start.2
  26.3 0.5 collective-permute-start.3
  26.8 0.8 %far_weight.1.refs_13_.first_ref.refs_5_ = bf16[384,1152]{1,0:T(8,128)(2,1)S(1)} custom-call(f32[3,18]{1,0:T(4,128)S(1)} %copy-done.4, bf16[384,2304]{1,0:T(8,128)(2,1)S(1)} %copy-done, bf16[384,1152]{1,0:T(8,128)(2,1)S(1)} %collective-permute-done.1.value_ref.after_ref.refs_4_.refs_2_), custom_call_target="tpu_custom_call" | custom-call | flops 10000000 | bytes 30000 | tf_op jit(solution)/shard_map/far_weight/pallas_call | solution.py:174
  27.6 1.8 %collective-permute-start.4 = (bf16[384,1152]{1,0:T(8,128)(2,1)S(1)}, bf16[384,1152]{1,0:T(8,128)(2,1)S(1)}, u32[]{:S(2)}, u32[]{:S(2)}) collective-permute-start(bf16[384,1152]{1,0:T(8,128)(2,1)S(1)} %far_weight.1.refs_13_.first_ref.refs_5_), channel_id=1, source_target_pairs={{0,2},{1,3},{2,0},{3,1},{4,6},{5,7},{6,4},{7,5},{8,10},{9,11},{10,... | collective-permute-start | bytes 2654216 | tf_op jit(solution)/shard_map/ppermute | solution.py:621
  29.4 1.4 %projection.1.refs_8_.refs_0_ = bf16[256,1152]{1,0:T(8,128)(2,1)S(1)} custom-call(bf16[128,1920]{1,0:T(8,128)(2,1)S(1)} %get-tuple-element.26.refs_0_.refs_9_.refs_2_, bf16[128,1920]{1,0:T(8,128)(2,1)S(1)} %collective-permute-done.7.refs_1_.refs_10_.refs_3_, bf16[384,1152]{1,0:T(8,128)(2,1)S(1)} %get-tuple-element.22.refs_2_.refs_0_, ...), custom_call_target="tpu_custom_call" | custom-call | flops 10000000 | bytes 30000 | tf_op jit(solution)/shard_map/projection/pallas_call | solution.py:236
  30.8 4.7 %projection_attention.1 = (bf16[256,1152]{1,0:T(8,128)(2,1)S(1)}, bf16[128,768]{1,0:T(8,128)(2,1)S(1)}, bf16[128,768]{1,0:T(8,128)(2,1)S(1)}, bf16[128,768]{1,0:T(8,128)(2,1)S(1)}, bf16[128,768]{1,0:T(8,128)(2,1)S(1)}) custom-call(bf16[128,1920]{1,0:T(8,128)(2,1)S(1)} %collective-permute-done.5.refs_0_.refs_11_.refs_4_, ...), custom_call_target="tpu_custom_call" | custom-call | flops 12000000000 | bytes 36000000 | tf_op jit(solution)/shard_map/projection_attention/pallas_call | solution.py:346
  35.5 1.3 %collective-permute-start.8 = (bf16[128,768]{1,0:T(8,128)(2,1)S(1)}, bf16[128,768]{1,0:T(8,128)(2,1)S(1)}, u32[]{:S(2)}, u32[]{:S(2)}) collective-permute-start(bf16[128,768]{1,0:T(8,128)(2,1)S(1)} %get-tuple-element.27), channel_id=1, source_target_pairs={{4,12},{8,0},{5,13},{9,1},{6,14},{10,2},{7,15},{11,3},{20,28},{24,... | collective-permute-start | bytes 589832 | tf_op jit(solution)/shard_map/ppermute | solution.py:630
  36.8 1.3 %collective-permute-start.11 = (bf16[128,768]{1,0:T(8,128)(2,1)S(1)}, bf16[128,768]{1,0:T(8,128)(2,1)S(1)}, u32[]{:S(2)}, u32[]{:S(2)}) collective-permute-start(bf16[128,768]{1,0:T(8,128)(2,1)S(1)} %get-tuple-element.33), channel_id=1, source_target_pairs={{4,0},{8,12},{5,1},{9,13},{6,2},{10,14},{7,3},{11,15},{20,16},{24,... | collective-permute-start | bytes 589832 | tf_op jit(solution)/shard_map/ppermute | solution.py:629
  38.1 2.0 %attention.1 = (bf16[128,1152]{1,0:T(8,128)(2,1)S(1)}, bf16[128,384]{1,0:T(8,128)(2,1)S(1)}, bf16[128,1152]{1,0:T(8,128)(2,1)S(1)}, bf16[128,384]{1,0:T(8,128)(2,1)S(1)}) custom-call(bf16[256,1152]{1,0:T(8,128)(2,1)S(1)} %projection.1.refs_8_.refs_0_, bf16[256,1152]{1,0:T(8,128)(2,1)S(1)} %get-tuple-element.28.refs_1_, ...), custom_call_target="tpu_custom_call" | custom-call | flops 12000000000 | bytes 36000000 | tf_op jit(solution)/shard_map/attention/pallas_call | solution.py:363
  40.1 1.3 %collective-permute-start.10 = (bf16[128,384]{1,0:T(8,128)(2,1)S(1)}, bf16[128,384]{1,0:T(8,128)(2,1)S(1)}, u32[]{:S(2)}, u32[]{:S(2)}) collective-permute-start(bf16[128,384]{1,0:T(8,128)(2,1)S(1)} %get-tuple-element.32), channel_id=1, source_target_pairs={{4,12},{8,0},{5,13},{9,1},{6,14},{10,2},{7,15},{11,3},{20,28},{24,... | collective-permute-start | bytes 294920 | tf_op jit(solution)/shard_map/ppermute | solution.py:632
  41.4 0.7 %collective-permute-start.12 = (bf16[128,1152]{1,0:T(8,128)(2,1)S(1)}, bf16[128,1152]{1,0:T(8,128)(2,1)S(1)}, u32[]{:S(2)}, u32[]{:S(2)}) collective-permute-start(bf16[128,1152]{1,0:T(8,128)(2,1)S(1)} %get-tuple-element.35), channel_id=1, source_target_pairs={{4,8},{8,4},{5,9},{9,5},{6,10},{10,6},{7,11},{11,7},{20,24},{24,20... | collective-permute-start | bytes 884744 | tf_op jit(solution)/shard_map/ppermute | solution.py:633
  42.1 5.4 %collective-permute-done.8.refs_0_.refs_8_.skip_first = bf16[128,768]{1,0:T(8,128)(2,1)S(1)} collective-permute-done((bf16[128,768]{1,0:T(8,128)(2,1)S(1)}, bf16[128,768]{1,0:T(8,128)(2,1)S(1)}, u32[]{:S(2)}, u32[]{:S(2)}) %collective-permute-start.8) | collective-permute-done | bytes 196640 | tf_op jit(solution)/shard_map/ppermute | solution.py:630
  47.5 1.3 %collective-permute-start.13 = (bf16[128,384]{1,0:T(8,128)(2,1)S(1)}, bf16[128,384]{1,0:T(8,128)(2,1)S(1)}, u32[]{:S(2)}, u32[]{:S(2)}) collective-permute-start(bf16[128,384]{1,0:T(8,128)(2,1)S(1)} %get-tuple-element.36), channel_id=1, source_target_pairs={{4,0},{8,12},{5,1},{9,13},{6,2},{10,14},{7,3},{11,15},{20,16},{24,... | collective-permute-start | bytes 294920 | tf_op jit(solution)/shard_map/ppermute | solution.py:634
  48.8 0.5 collective-permute-done.4.second_ref.refs_6_
  49.3 0.1 chip_weight.1
  49.4 0.1 collective-permute-start.9
  49.5 0.5 collective-permute-done.10.refs_9_.skip_second
  50.0 0.2 copy-done.1
  50.3 1.1 %grad_norm_part.1 = (f32[128,1536]{1,0:T(8,128)S(1)}, f32[128,1536]{1,0:T(8,128)S(1)}, f32[128,128]{1,0:T(8,128)S(1)}) custom-call(bf16[384,1152]{1,0:T(8,128)(2,1)S(1)} %get-tuple-element.22.refs_2_.refs_0_, bf16[384,1152]{1,0:T(8,128)(2,1)S(1)} %collective-permute-done.refs_3_.refs_1_, ...), custom_call_target="tpu_custom_call" | custom-call | flops 10000000 | bytes 30000 | tf_op jit(solution)/shard_map/grad_norm_part/pallas_call | solution.py:423
  51.4 2.4 %collective-permute-done.11.refs_5_ = bf16[128,768]{1,0:T(8,128)(2,1)S(1)} collective-permute-done((bf16[128,768]{1,0:T(8,128)(2,1)S(1)}, bf16[128,768]{1,0:T(8,128)(2,1)S(1)}, u32[]{:S(2)}, u32[]{:S(2)}) %collective-permute-start.11) | collective-permute-done | bytes 196640 | tf_op jit(solution)/shard_map/ppermute | solution.py:629
  53.8 0.8 %back_part.1.sums = f32[128,1536]{1,0:T(8,128)S(1)} custom-call(bf16[384,1152]{1,0:T(8,128)(2,1)S(1)} %get-tuple-element.22.refs_2_.refs_0_, bf16[384,1152]{1,0:T(8,128)(2,1)S(1)} %collective-permute-done.refs_3_.refs_1_, bf16[384,1152]{1,0:T(8,128)(2,1)S(1)} %collective-permute-done.1.value_ref.after_ref.refs_4_.refs_2_, ...), custom_call_target="tpu_custom_call" | custom-call | flops 49999998976 | bytes 150000000 | tf_op jit(solution)/shard_map/back_part/pallas_call | solution.py:449
  54.7 0.7 %pair_part.1.refs_8_ = f32[128,1536]{1,0:T(8,128)S(1)} custom-call(bf16[768,1152]{1,0:T(8,128)(2,1)S(1)} %collective-permute-done.9.pair.refs_7_, bf16[128,768]{1,0:T(8,128)(2,1)S(1)} %collective-permute-done.8.refs_0_.refs_8_.skip_first, bf16[128,384]{1,0:T(8,128)(2,1)S(1)} %collective-permute-done.10.refs_9_.skip_second, f32[128,1536]{1,0:T(8,128)S(1)} %back_part.1.sums), custom_call_target="tpu_custom_call" | custom-call | flops 10000000 | bytes 30000 | tf_op jit(solution)/shard_map/pair_part/pallas_call | solution.py:474
  55.4 0.4 collective-permute-done.13.refs_10_
  55.9 1.6 %input_grad.1 = f32[1,128,1536]{2,1,0:T(8,128)} custom-call(bf16[384,1152]{1,0:T(8,128)(2,1)S(1)} %get-tuple-element.22.refs_2_.refs_0_, bf16[384,1152]{1,0:T(8,128)(2,1)S(1)} %collective-permute-done.refs_3_.refs_1_, bf16[384,1152]{1,0:T(8,128)(2,1)S(1)} %collective-permute-done.1.value_ref.after_ref.refs_4_.refs_2_, ...), custom_call_target="tpu_custom_call" | custom-call | flops 2000000000 | bytes 6000000 | tf_op jit(solution)/shard_map/input_grad/pallas_call | solution.py:529
  (17 shorter events, 0.1 us)
Async XLA Ops:
  0.0 26.8 %copy-start.4 = (f32[3,18]{1,0:T(4,128)S(1)}, f32[3,18]{1,0:T(4,128)}, u32[]{:S(2)}) copy-start(f32[3,18]{1,0:T(4,128)} %scales_ref.3) | copy-start | bytes 652
  0.0 26.8 %copy-start = (bf16[384,2304]{1,0:T(8,128)(2,1)S(1)}, bf16[384,2304]{1,0:T(8,128)(2,1)}, u32[]{:S(2)}) copy-start(bf16[384,2304]{1,0:T(8,128)(2,1)} %codes_ref.3) | copy-start | bytes 5308420
  3.5 22.7 %collective-permute-start.1 = (bf16[384,1152]{1,0:T(8,128)(2,1)S(1)}, bf16[384,1152]{1,0:T(8,128)(2,1)S(1)}, u32[]{:S(2)}, u32[]{:S(2)}) collective-permute-start(bf16[384,1152]{1,0:T(8,128)(2,1)S(1)} %get-tuple-element.22.refs_2_.refs_0_), channel_id=1, source_target_pairs={{0,2},{1,3},{2,0},{3,1},{4,6},{5,7},{6,4},{7,5},{8,10},{9,11},{10,... | collective-permute-start | bytes 2654216 | tf_op jit(solution)/shard_map/ppermute | solution.py:617
  6.5 19.8 %collective-permute-start.7 = (bf16[128,1920]{1,0:T(8,128)(2,1)S(1)}, bf16[128,1920]{1,0:T(8,128)(2,1)S(1)}, u32[]{:S(2)}, u32[]{:S(2)}) collective-permute-start(bf16[128,1920]{1,0:T(8,128)(2,1)S(1)} %get-tuple-element.26.refs_0_.refs_9_.refs_2_), channel_id=1, source_target_pairs={{0,4},{12,8},{1,5},{13,9},{2,6},{14,10},{3,7},{15,11},{16,20},{28,... | collective-permute-start | bytes 1474568 | tf_op jit(solution)/shard_map/ppermute | solution.py:616
  10.0 17.6 %collective-permute-start = (bf16[384,1152]{1,0:T(8,128)(2,1)S(1)}, bf16[384,1152]{1,0:T(8,128)(2,1)S(1)}, u32[]{:S(2)}, u32[]{:S(2)}) collective-permute-start(bf16[384,1152]{1,0:T(8,128)(2,1)S(1)} %get-tuple-element.22.refs_2_.refs_0_), channel_id=1, source_target_pairs={{0,1},{1,0},{2,3},{3,2},{4,5},{5,4},{6,7},{7,6},{8,9},{9,8},{10,11... | collective-permute-start | bytes 2654216 | tf_op jit(solution)/shard_map/ppermute | solution.py:618
  10.0 20.7 %collective-permute-start.5 = (bf16[128,1920]{1,0:T(8,128)(2,1)}, bf16[128,1920]{1,0:T(8,128)(2,1)S(1)}, u32[]{:S(2)}, u32[]{:S(2)}) collective-permute-start(bf16[128,1920]{1,0:T(8,128)(2,1)} %get-tuple-element.25), channel_id=1, source_target_pairs={{4,8},{8,4},{5,9},{9,5},{6,10},{10,6},{7,11},{11,7},{20,24},{24,20... | collective-permute-start | bytes 1474568 | tf_op jit(solution)/shard_map/ppermute | solution.py:614
  10.7 20.1 %collective-permute-start.6 = (bf16[128,1920]{1,0:T(8,128)(2,1)}, bf16[128,1920]{1,0:T(8,128)(2,1)S(1)}, u32[]{:S(2)}, u32[]{:S(2)}) collective-permute-start(bf16[128,1920]{1,0:T(8,128)(2,1)} %get-tuple-element.25), channel_id=1, source_target_pairs={{0,8},{12,4},{1,9},{13,5},{2,10},{14,6},{3,11},{15,7},{16,24},{28,... | collective-permute-start | bytes 1474568 | tf_op jit(solution)/shard_map/ppermute | solution.py:615
  26.2 3.2 %collective-permute-start.2 = (bf16[192,1152]{1,0:T(8,128)(2,1)S(1)}, bf16[192,1152]{1,0:T(8,128)(2,1)S(1)}, u32[]{:S(2)}, u32[]{:S(2)}) collective-permute-start(bf16[192,1152]{1,0:T(8,128)(2,1)S(1)} %get-tuple-element.23), channel_id=1, source_target_pairs={{0,1},{1,0},{2,3},{3,2},{4,5},{5,4},{6,7},{7,6},{8,9},{9,8},{10,11... | collective-permute-start | bytes 1327112 | tf_op jit(solution)/shard_map/ppermute | solution.py:619
  26.3 3.1 %copy-start.2 = (f32[2304]{0:T(1024)S(1)}, f32[2304]{0:T(1024)}, u32[]{:S(2)}) copy-start(f32[2304]{0:T(1024)} %refs_7_.3) | copy-start | bytes 27652
  26.3 3.1 %collective-permute-start.3 = (bf16[192,1152]{1,0:T(8,128)(2,1)S(1)}, bf16[192,1152]{1,0:T(8,128)(2,1)S(1)}, u32[]{:S(2)}, u32[]{:S(2)}) collective-permute-start(bf16[192,1152]{1,0:T(8,128)(2,1)S(1)} %get-tuple-element.24), channel_id=1, source_target_pairs={{0,1},{1,0},{2,3},{3,2},{4,5},{5,4},{6,7},{7,6},{8,9},{9,8},{10,11... | collective-permute-start | bytes 1327112 | tf_op jit(solution)/shard_map/ppermute | solution.py:619
  27.6 21.7 %collective-permute-start.4 = (bf16[384,1152]{1,0:T(8,128)(2,1)S(1)}, bf16[384,1152]{1,0:T(8,128)(2,1)S(1)}, u32[]{:S(2)}, u32[]{:S(2)}) collective-permute-start(bf16[384,1152]{1,0:T(8,128)(2,1)S(1)} %far_weight.1.refs_13_.first_ref.refs_5_), channel_id=1, source_target_pairs={{0,2},{1,3},{2,0},{3,1},{4,6},{5,7},{6,4},{7,5},{8,10},{9,11},{10,... | collective-permute-start | bytes 2654216 | tf_op jit(solution)/shard_map/ppermute | solution.py:621
  35.5 12.0 %collective-permute-start.8 = (bf16[128,768]{1,0:T(8,128)(2,1)S(1)}, bf16[128,768]{1,0:T(8,128)(2,1)S(1)}, u32[]{:S(2)}, u32[]{:S(2)}) collective-permute-start(bf16[128,768]{1,0:T(8,128)(2,1)S(1)} %get-tuple-element.27), channel_id=1, source_target_pairs={{4,12},{8,0},{5,13},{9,1},{6,14},{10,2},{7,15},{11,3},{20,28},{24,... | collective-permute-start | bytes 589832 | tf_op jit(solution)/shard_map/ppermute | solution.py:630
  36.8 17.0 %collective-permute-start.11 = (bf16[128,768]{1,0:T(8,128)(2,1)S(1)}, bf16[128,768]{1,0:T(8,128)(2,1)S(1)}, u32[]{:S(2)}, u32[]{:S(2)}) collective-permute-start(bf16[128,768]{1,0:T(8,128)(2,1)S(1)} %get-tuple-element.33), channel_id=1, source_target_pairs={{4,0},{8,12},{5,1},{9,13},{6,2},{10,14},{7,3},{11,15},{20,16},{24,... | collective-permute-start | bytes 589832 | tf_op jit(solution)/shard_map/ppermute | solution.py:629
  40.1 9.9 %collective-permute-start.10 = (bf16[128,384]{1,0:T(8,128)(2,1)S(1)}, bf16[128,384]{1,0:T(8,128)(2,1)S(1)}, u32[]{:S(2)}, u32[]{:S(2)}) collective-permute-start(bf16[128,384]{1,0:T(8,128)(2,1)S(1)} %get-tuple-element.32), channel_id=1, source_target_pairs={{4,12},{8,0},{5,13},{9,1},{6,14},{10,2},{7,15},{11,3},{20,28},{24,... | collective-permute-start | bytes 294920 | tf_op jit(solution)/shard_map/ppermute | solution.py:632
  41.4 14.4 %collective-permute-start.12 = (bf16[128,1152]{1,0:T(8,128)(2,1)S(1)}, bf16[128,1152]{1,0:T(8,128)(2,1)S(1)}, u32[]{:S(2)}, u32[]{:S(2)}) collective-permute-start(bf16[128,1152]{1,0:T(8,128)(2,1)S(1)} %get-tuple-element.35), channel_id=1, source_target_pairs={{4,8},{8,4},{5,9},{9,5},{6,10},{10,6},{7,11},{11,7},{20,24},{24,20... | collective-permute-start | bytes 884744 | tf_op jit(solution)/shard_map/ppermute | solution.py:633
  47.5 8.3 %collective-permute-start.13 = (bf16[128,384]{1,0:T(8,128)(2,1)S(1)}, bf16[128,384]{1,0:T(8,128)(2,1)S(1)}, u32[]{:S(2)}, u32[]{:S(2)}) collective-permute-start(bf16[128,384]{1,0:T(8,128)(2,1)S(1)} %get-tuple-element.36), channel_id=1, source_target_pairs={{4,0},{8,12},{5,1},{9,13},{6,2},{10,14},{7,3},{11,15},{20,16},{24,... | collective-permute-start | bytes 294920 | tf_op jit(solution)/shard_map/ppermute | solution.py:634
  49.3 1.0 %copy-start.1 = (bf16[1,128,1536]{2,1,0:T(8,128)(2,1)S(1)}, bf16[1,128,1536]{2,1,0:T(8,128)(2,1)}, u32[]{:S(2)}) copy-start(bf16[1,128,1536]{2,1,0:T(8,128)(2,1)} %refs_10_.1) | copy-start | bytes 1179652
  49.4 5.3 %collective-permute-start.9 = (bf16[768,1152]{1,0:T(8,128)(2,1)S(1)}, bf16[768,1152]{1,0:T(8,128)(2,1)S(1)}, u32[]{:S(2)}, u32[]{:S(2)}) collective-permute-start(bf16[768,1152]{1,0:T(8,128)(2,1)S(1)} %chip_weight.1), channel_id=1, source_target_pairs={{0,1},{1,0},{2,3},{3,2},{4,5},{5,4},{6,7},{7,6},{8,9},{9,8},{10,11... | collective-permute-start | bytes 5308424 | tf_op jit(solution)/shard_map/ppermute | solution.py:635
  54.7 1.2 %copy-start.3 = (f32[1536]{0:T(1024)S(1)}, f32[1536]{0:T(1024)}, u32[]{:S(2)}) copy-start(f32[1536]{0:T(1024)} %refs_13_.1) | copy-start | bytes 18436

commit v10 on v9

--- a/solution.py
+++ b/solution.py
@@ -13,7 +13,7 @@
 QBLOCK = 128
 HD = 768
 HALF = HD // 2
-ROWS_OUT = 32
+ROWS_OUT = 64
 EPSILON = 1e-06
 VMEM = pltpu.VMEM
 SMEM = pltpu.SMEM

time: 57.9 us -> 57.9 us (level)
  no operation moved by 1% of the time
where the time goes in v10:
time: 57.9 us; the launch traced here: 57.7 us
  waiting for transfers between devices  20.7 us (36%)
  starting transfers between devices  19.5 us (34%)
  Pallas kernels  16.8 us (29%)
    ppermute x1, waiting for transfers between devices, local_middle(): near_across = lax.ppermute(near, 'weight', flip(2))  11.4 us
    ppermute x1, waiting for transfers between devices, local_middle(): skip_first = lax.ppermute(skip_first, 'seq', FAR_TO_END)  5.41 us
    pallas_call x1, Pallas kernels, project_attention_step(): pl.pallas_call(functools.partial(project_attention_kernel, pairs), out_sh...  4.7 us
    ppermute x1, starting transfers between devices, local_middle(): both_far = lax.ppermute(both_other, 'seq', END_TO_FAR)  3.97 us
    ppermute x1, starting transfers between devices, local_middle(): both_end = lax.ppermute(both_near, 'seq', END_TO_MIDDLE)  3.5 us
    pallas_call x1, Pallas kernels, first_step(): pl.pallas_call(first_kernel, out_shape=(VMEM((depth, 3 * HALF), jnp.bfloa...  3.44 us
    ppermute x1, starting transfers between devices, local_middle(): near_across = lax.ppermute(near, 'weight', flip(2))  3.01 us
    ppermute x1, waiting for transfers between devices, local_middle(): back_first = lax.ppermute(end, 'seq', MIDDLE_TO_END)  2.43 us
  transfers between devices with their start and end apart: 14, of which 6 were waited for; matrix products, arithmetic and copies ran while one was open for 0% of the time, Pallas kernels for 20%

profile of v10, /device:TPU:0, one launch (start us, length us, event | category | flops | bytes accessed | tf_op | source)
XLA Modules:
  0.0 57.7 jit_solution(31810514365364936)
XLA Ops:
  0.0 3.4 %first_weights_and_rows.1 = (bf16[384,1152]{1,0:T(8,128)(2,1)S(1)}, bf16[128,1920]{1,0:T(8,128)(2,1)S(1)}, bf16[128,1920]{1,0:T(8,128)(2,1)}) custom-call(bf16[1,128,1536]{2,1,0:T(8,128)(2,1)} %refs_10_.1, f32[1536]{0:T(1024)} %refs_13_.1, f32[1536]{0:T(1024)} %shift_ref.1, f32[3,18]{1,0:T(4,128)} %scales_ref.3, bf16[384,2304]{1,0:T(8,128)(2,1)} %codes_ref.3, ...), custom_call_target="tpu_custom_call" | custom-call | flops 3000000000 | bytes 9000000 | tf_op jit(solution)/shard_map/first_weights_and_rows/pallas_call | solution.py:121
  3.5 3.0 %collective-permute-start.1 = (bf16[384,1152]{1,0:T(8,128)(2,1)S(1)}, bf16[384,1152]{1,0:T(8,128)(2,1)S(1)}, u32[]{:S(2)}, u32[]{:S(2)}) collective-permute-start(bf16[384,1152]{1,0:T(8,128)(2,1)S(1)} %get-tuple-element.22.refs_2_.refs_0_), channel_id=1, source_target_pairs={{0,2},{1,3},{2,0},{3,1},{4,6},{5,7},{6,4},{7,5},{8,10},{9,11},{10,... | collective-permute-start | bytes 2654216 | tf_op jit(solution)/shard_map/ppermute | solution.py:617
  6.5 3.5 %collective-permute-start.7 = (bf16[128,1920]{1,0:T(8,128)(2,1)S(1)}, bf16[128,1920]{1,0:T(8,128)(2,1)S(1)}, u32[]{:S(2)}, u32[]{:S(2)}) collective-permute-start(bf16[128,1920]{1,0:T(8,128)(2,1)S(1)} %get-tuple-element.26.refs_0_.refs_9_.refs_2_), channel_id=1, source_target_pairs={{0,4},{12,8},{1,5},{13,9},{2,6},{14,10},{3,7},{15,11},{16,20},{28,... | collective-permute-start | bytes 1474568 | tf_op jit(solution)/shard_map/ppermute | solution.py:616
  10.0 0.1 collective-permute-start
  10.0 0.7 %collective-permute-start.5 = (bf16[128,1920]{1,0:T(8,128)(2,1)}, bf16[128,1920]{1,0:T(8,128)(2,1)S(1)}, u32[]{:S(2)}, u32[]{:S(2)}) collective-permute-start(bf16[128,1920]{1,0:T(8,128)(2,1)} %get-tuple-element.25), channel_id=1, source_target_pairs={{4,8},{8,4},{5,9},{9,5},{6,10},{10,6},{7,11},{11,7},{20,24},{24,20... | collective-permute-start | bytes 1474568 | tf_op jit(solution)/shard_map/ppermute | solution.py:614
  10.7 4.0 %collective-permute-start.6 = (bf16[128,1920]{1,0:T(8,128)(2,1)}, bf16[128,1920]{1,0:T(8,128)(2,1)S(1)}, u32[]{:S(2)}, u32[]{:S(2)}) collective-permute-start(bf16[128,1920]{1,0:T(8,128)(2,1)} %get-tuple-element.25), channel_id=1, source_target_pairs={{0,8},{12,4},{1,9},{13,5},{2,10},{14,6},{3,11},{15,7},{16,24},{28,... | collective-permute-start | bytes 1474568 | tf_op jit(solution)/shard_map/ppermute | solution.py:615
  14.7 11.4 %collective-permute-done.1.value_ref.after_ref.refs_4_.refs_2_ = bf16[384,1152]{1,0:T(8,128)(2,1)S(1)} collective-permute-done((bf16[384,1152]{1,0:T(8,128)(2,1)S(1)}, bf16[384,1152]{1,0:T(8,128)(2,1)S(1)}, u32[]{:S(2)}, u32[]{:S(2)}) %collective-permute-start.1) | collective-permute-done | bytes 884768 | tf_op jit(solution)/shard_map/ppermute | solution.py:617
  26.1 0.1 split_rows.1
  26.2 0.1 collective-permute-start.2
  26.3 0.5 collective-permute-start.3
  26.8 0.8 %far_weight.1.refs_13_.first_ref.refs_5_ = bf16[384,1152]{1,0:T(8,128)(2,1)S(1)} custom-call(f32[3,18]{1,0:T(4,128)S(1)} %copy-done.4, bf16[384,2304]{1,0:T(8,128)(2,1)S(1)} %copy-done, bf16[384,1152]{1,0:T(8,128)(2,1)S(1)} %collective-permute-done.1.value_ref.after_ref.refs_4_.refs_2_), custom_call_target="tpu_custom_call" | custom-call | flops 10000000 | bytes 30000 | tf_op jit(solution)/shard_map/far_weight/pallas_call | solution.py:174
  27.6 1.8 %collective-permute-start.4 = (bf16[384,1152]{1,0:T(8,128)(2,1)S(1)}, bf16[384,1152]{1,0:T(8,128)(2,1)S(1)}, u32[]{:S(2)}, u32[]{:S(2)}) collective-permute-start(bf16[384,1152]{1,0:T(8,128)(2,1)S(1)} %far_weight.1.refs_13_.first_ref.refs_5_), channel_id=1, source_target_pairs={{0,2},{1,3},{2,0},{3,1},{4,6},{5,7},{6,4},{7,5},{8,10},{9,11},{10,... | collective-permute-start | bytes 2654216 | tf_op jit(solution)/shard_map/ppermute | solution.py:621
  29.4 1.4 %projection.1.refs_8_.refs_0_ = bf16[256,1152]{1,0:T(8,128)(2,1)S(1)} custom-call(bf16[128,1920]{1,0:T(8,128)(2,1)S(1)} %get-tuple-element.26.refs_0_.refs_9_.refs_2_, bf16[128,1920]{1,0:T(8,128)(2,1)S(1)} %collective-permute-done.7.refs_1_.refs_10_.refs_3_, bf16[384,1152]{1,0:T(8,128)(2,1)S(1)} %get-tuple-element.22.refs_2_.refs_0_, ...), custom_call_target="tpu_custom_call" | custom-call | flops 10000000 | bytes 30000 | tf_op jit(solution)/shard_map/projection/pallas_call | solution.py:236
  30.8 4.7 %projection_attention.1 = (bf16[256,1152]{1,0:T(8,128)(2,1)S(1)}, bf16[128,768]{1,0:T(8,128)(2,1)S(1)}, bf16[128,768]{1,0:T(8,128)(2,1)S(1)}, bf16[128,768]{1,0:T(8,128)(2,1)S(1)}, bf16[128,768]{1,0:T(8,128)(2,1)S(1)}) custom-call(bf16[128,1920]{1,0:T(8,128)(2,1)S(1)} %collective-permute-done.5.refs_0_.refs_11_.refs_4_, ...), custom_call_target="tpu_custom_call" | custom-call | flops 12000000000 | bytes 36000000 | tf_op jit(solution)/shard_map/projection_attention/pallas_call | solution.py:346
  35.5 1.3 %collective-permute-start.8 = (bf16[128,768]{1,0:T(8,128)(2,1)S(1)}, bf16[128,768]{1,0:T(8,128)(2,1)S(1)}, u32[]{:S(2)}, u32[]{:S(2)}) collective-permute-start(bf16[128,768]{1,0:T(8,128)(2,1)S(1)} %get-tuple-element.27), channel_id=1, source_target_pairs={{4,12},{8,0},{5,13},{9,1},{6,14},{10,2},{7,15},{11,3},{20,28},{24,... | collective-permute-start | bytes 589832 | tf_op jit(solution)/shard_map/ppermute | solution.py:630
  36.8 1.3 %collective-permute-start.11 = (bf16[128,768]{1,0:T(8,128)(2,1)S(1)}, bf16[128,768]{1,0:T(8,128)(2,1)S(1)}, u32[]{:S(2)}, u32[]{:S(2)}) collective-permute-start(bf16[128,768]{1,0:T(8,128)(2,1)S(1)} %get-tuple-element.33), channel_id=1, source_target_pairs={{4,0},{8,12},{5,1},{9,13},{6,2},{10,14},{7,3},{11,15},{20,16},{24,... | collective-permute-start | bytes 589832 | tf_op jit(solution)/shard_map/ppermute | solution.py:629
  38.1 2.0 %attention.1 = (bf16[128,1152]{1,0:T(8,128)(2,1)S(1)}, bf16[128,384]{1,0:T(8,128)(2,1)S(1)}, bf16[128,1152]{1,0:T(8,128)(2,1)S(1)}, bf16[128,384]{1,0:T(8,128)(2,1)S(1)}) custom-call(bf16[256,1152]{1,0:T(8,128)(2,1)S(1)} %projection.1.refs_8_.refs_0_, bf16[256,1152]{1,0:T(8,128)(2,1)S(1)} %get-tuple-element.28.refs_1_, ...), custom_call_target="tpu_custom_call" | custom-call | flops 12000000000 | bytes 36000000 | tf_op jit(solution)/shard_map/attention/pallas_call | solution.py:363
  40.1 1.3 %collective-permute-start.10 = (bf16[128,384]{1,0:T(8,128)(2,1)S(1)}, bf16[128,384]{1,0:T(8,128)(2,1)S(1)}, u32[]{:S(2)}, u32[]{:S(2)}) collective-permute-start(bf16[128,384]{1,0:T(8,128)(2,1)S(1)} %get-tuple-element.32), channel_id=1, source_target_pairs={{4,12},{8,0},{5,13},{9,1},{6,14},{10,2},{7,15},{11,3},{20,28},{24,... | collective-permute-start | bytes 294920 | tf_op jit(solution)/shard_map/ppermute | solution.py:632
  41.4 0.7 %collective-permute-start.12 = (bf16[128,1152]{1,0:T(8,128)(2,1)S(1)}, bf16[128,1152]{1,0:T(8,128)(2,1)S(1)}, u32[]{:S(2)}, u32[]{:S(2)}) collective-permute-start(bf16[128,1152]{1,0:T(8,128)(2,1)S(1)} %get-tuple-element.35), channel_id=1, source_target_pairs={{4,8},{8,4},{5,9},{9,5},{6,10},{10,6},{7,11},{11,7},{20,24},{24,20... | collective-permute-start | bytes 884744 | tf_op jit(solution)/shard_map/ppermute | solution.py:633
  42.1 5.4 %collective-permute-done.8.refs_0_.refs_8_.skip_first = bf16[128,768]{1,0:T(8,128)(2,1)S(1)} collective-permute-done((bf16[128,768]{1,0:T(8,128)(2,1)S(1)}, bf16[128,768]{1,0:T(8,128)(2,1)S(1)}, u32[]{:S(2)}, u32[]{:S(2)}) %collective-permute-start.8) | collective-permute-done | bytes 196640 | tf_op jit(solution)/shard_map/ppermute | solution.py:630
  47.5 1.3 %collective-permute-start.13 = (bf16[128,384]{1,0:T(8,128)(2,1)S(1)}, bf16[128,384]{1,0:T(8,128)(2,1)S(1)}, u32[]{:S(2)}, u32[]{:S(2)}) collective-permute-start(bf16[128,384]{1,0:T(8,128)(2,1)S(1)} %get-tuple-element.36), channel_id=1, source_target_pairs={{4,0},{8,12},{5,1},{9,13},{6,2},{10,14},{7,3},{11,15},{20,16},{24,... | collective-permute-start | bytes 294920 | tf_op jit(solution)/shard_map/ppermute | solution.py:634
  48.8 0.5 collective-permute-done.4.second_ref.refs_6_
  49.3 0.1 chip_weight.1
  49.4 0.1 collective-permute-start.9
  49.5 0.5 collective-permute-done.10.refs_9_.skip_second
  50.0 0.2 copy-done.1
  50.3 1.1 %grad_norm_part.1 = (f32[128,1536]{1,0:T(8,128)S(1)}, f32[128,1536]{1,0:T(8,128)S(1)}, f32[128,128]{1,0:T(8,128)S(1)}) custom-call(bf16[384,1152]{1,0:T(8,128)(2,1)S(1)} %get-tuple-element.22.refs_2_.refs_0_, bf16[384,1152]{1,0:T(8,128)(2,1)S(1)} %collective-permute-done.refs_3_.refs_1_, ...), custom_call_target="tpu_custom_call" | custom-call | flops 10000000 | bytes 30000 | tf_op jit(solution)/shard_map/grad_norm_part/pallas_call | solution.py:423
  51.4 2.4 %collective-permute-done.11.refs_5_ = bf16[128,768]{1,0:T(8,128)(2,1)S(1)} collective-permute-done((bf16[128,768]{1,0:T(8,128)(2,1)S(1)}, bf16[128,768]{1,0:T(8,128)(2,1)S(1)}, u32[]{:S(2)}, u32[]{:S(2)}) %collective-permute-start.11) | collective-permute-done | bytes 196640 | tf_op jit(solution)/shard_map/ppermute | solution.py:629
  53.8 0.8 %back_part.1.sums = f32[128,1536]{1,0:T(8,128)S(1)} custom-call(bf16[384,1152]{1,0:T(8,128)(2,1)S(1)} %get-tuple-element.22.refs_2_.refs_0_, bf16[384,1152]{1,0:T(8,128)(2,1)S(1)} %collective-permute-done.refs_3_.refs_1_, bf16[384,1152]{1,0:T(8,128)(2,1)S(1)} %collective-permute-done.1.value_ref.after_ref.refs_4_.refs_2_, ...), custom_call_target="tpu_custom_call" | custom-call | flops 49999998976 | bytes 150000000 | tf_op jit(solution)/shard_map/back_part/pallas_call | solution.py:449
  54.7 0.7 %pair_part.1.refs_8_ = f32[128,1536]{1,0:T(8,128)S(1)} custom-call(bf16[768,1152]{1,0:T(8,128)(2,1)S(1)} %collective-permute-done.9.pair.refs_7_, bf16[128,768]{1,0:T(8,128)(2,1)S(1)} %collective-permute-done.8.refs_0_.refs_8_.skip_first, bf16[128,384]{1,0:T(8,128)(2,1)S(1)} %collective-permute-done.10.refs_9_.skip_second, f32[128,1536]{1,0:T(8,128)S(1)} %back_part.1.sums), custom_call_target="tpu_custom_call" | custom-call | flops 10000000 | bytes 30000 | tf_op jit(solution)/shard_map/pair_part/pallas_call | solution.py:474
  55.4 0.4 collective-permute-done.13.refs_10_
  55.9 1.6 %input_grad.1 = f32[1,128,1536]{2,1,0:T(8,128)} custom-call(bf16[384,1152]{1,0:T(8,128)(2,1)S(1)} %get-tuple-element.22.refs_2_.refs_0_, bf16[384,1152]{1,0:T(8,128)(2,1)S(1)} %collective-permute-done.refs_3_.refs_1_, bf16[384,1152]{1,0:T(8,128)(2,1)S(1)} %collective-permute-done.1.value_ref.after_ref.refs_4_.refs_2_, ...), custom_call_target="tpu_custom_call" | custom-call | flops 2000000000 | bytes 6000000 | tf_op jit(solution)/shard_map/input_grad/pallas_call | solution.py:529
  (17 shorter events, 0.1 us)
Async XLA Ops:
  0.0 26.8 %copy-start.4 = (f32[3,18]{1,0:T(4,128)S(1)}, f32[3,18]{1,0:T(4,128)}, u32[]{:S(2)}) copy-start(f32[3,18]{1,0:T(4,128)} %scales_ref.3) | copy-start | bytes 652
  0.0 26.8 %copy-start = (bf16[384,2304]{1,0:T(8,128)(2,1)S(1)}, bf16[384,2304]{1,0:T(8,128)(2,1)}, u32[]{:S(2)}) copy-start(bf16[384,2304]{1,0:T(8,128)(2,1)} %codes_ref.3) | copy-start | bytes 5308420
  3.5 22.7 %collective-permute-start.1 = (bf16[384,1152]{1,0:T(8,128)(2,1)S(1)}, bf16[384,1152]{1,0:T(8,128)(2,1)S(1)}, u32[]{:S(2)}, u32[]{:S(2)}) collective-permute-start(bf16[384,1152]{1,0:T(8,128)(2,1)S(1)} %get-tuple-element.22.refs_2_.refs_0_), channel_id=1, source_target_pairs={{0,2},{1,3},{2,0},{3,1},{4,6},{5,7},{6,4},{7,5},{8,10},{9,11},{10,... | collective-permute-start | bytes 2654216 | tf_op jit(solution)/shard_map/ppermute | solution.py:617
  6.5 19.8 %collective-permute-start.7 = (bf16[128,1920]{1,0:T(8,128)(2,1)S(1)}, bf16[128,1920]{1,0:T(8,128)(2,1)S(1)}, u32[]{:S(2)}, u32[]{:S(2)}) collective-permute-start(bf16[128,1920]{1,0:T(8,128)(2,1)S(1)} %get-tuple-element.26.refs_0_.refs_9_.refs_2_), channel_id=1, source_target_pairs={{0,4},{12,8},{1,5},{13,9},{2,6},{14,10},{3,7},{15,11},{16,20},{28,... | collective-permute-start | bytes 1474568 | tf_op jit(solution)/shard_map/ppermute | solution.py:616
  10.0 17.6 %collective-permute-start = (bf16[384,1152]{1,0:T(8,128)(2,1)S(1)}, bf16[384,1152]{1,0:T(8,128)(2,1)S(1)}, u32[]{:S(2)}, u32[]{:S(2)}) collective-permute-start(bf16[384,1152]{1,0:T(8,128)(2,1)S(1)} %get-tuple-element.22.refs_2_.refs_0_), channel_id=1, source_target_pairs={{0,1},{1,0},{2,3},{3,2},{4,5},{5,4},{6,7},{7,6},{8,9},{9,8},{10,11... | collective-permute-start | bytes 2654216 | tf_op jit(solution)/shard_map/ppermute | solution.py:618
  10.0 20.7 %collective-permute-start.5 = (bf16[128,1920]{1,0:T(8,128)(2,1)}, bf16[128,1920]{1,0:T(8,128)(2,1)S(1)}, u32[]{:S(2)}, u32[]{:S(2)}) collective-permute-start(bf16[128,1920]{1,0:T(8,128)(2,1)} %get-tuple-element.25), channel_id=1, source_target_pairs={{4,8},{8,4},{5,9},{9,5},{6,10},{10,6},{7,11},{11,7},{20,24},{24,20... | collective-permute-start | bytes 1474568 | tf_op jit(solution)/shard_map/ppermute | solution.py:614
  10.7 20.1 %collective-permute-start.6 = (bf16[128,1920]{1,0:T(8,128)(2,1)}, bf16[128,1920]{1,0:T(8,128)(2,1)S(1)}, u32[]{:S(2)}, u32[]{:S(2)}) collective-permute-start(bf16[128,1920]{1,0:T(8,128)(2,1)} %get-tuple-element.25), channel_id=1, source_target_pairs={{0,8},{12,4},{1,9},{13,5},{2,10},{14,6},{3,11},{15,7},{16,24},{28,... | collective-permute-start | bytes 1474568 | tf_op jit(solution)/shard_map/ppermute | solution.py:615
  26.2 3.2 %collective-permute-start.2 = (bf16[192,1152]{1,0:T(8,128)(2,1)S(1)}, bf16[192,1152]{1,0:T(8,128)(2,1)S(1)}, u32[]{:S(2)}, u32[]{:S(2)}) collective-permute-start(bf16[192,1152]{1,0:T(8,128)(2,1)S(1)} %get-tuple-element.23), channel_id=1, source_target_pairs={{0,1},{1,0},{2,3},{3,2},{4,5},{5,4},{6,7},{7,6},{8,9},{9,8},{10,11... | collective-permute-start | bytes 1327112 | tf_op jit(solution)/shard_map/ppermute | solution.py:619
  26.3 3.1 %copy-start.2 = (f32[2304]{0:T(1024)S(1)}, f32[2304]{0:T(1024)}, u32[]{:S(2)}) copy-start(f32[2304]{0:T(1024)} %refs_7_.3) | copy-start | bytes 27652
  26.3 3.1 %collective-permute-start.3 = (bf16[192,1152]{1,0:T(8,128)(2,1)S(1)}, bf16[192,1152]{1,0:T(8,128)(2,1)S(1)}, u32[]{:S(2)}, u32[]{:S(2)}) collective-permute-start(bf16[192,1152]{1,0:T(8,128)(2,1)S(1)} %get-tuple-element.24), channel_id=1, source_target_pairs={{0,1},{1,0},{2,3},{3,2},{4,5},{5,4},{6,7},{7,6},{8,9},{9,8},{10,11... | collective-permute-start | bytes 1327112 | tf_op jit(solution)/shard_map/ppermute | solution.py:619
  27.6 21.7 %collective-permute-start.4 = (bf16[384,1152]{1,0:T(8,128)(2,1)S(1)}, bf16[384,1152]{1,0:T(8,128)(2,1)S(1)}, u32[]{:S(2)}, u32[]{:S(2)}) collective-permute-start(bf16[384,1152]{1,0:T(8,128)(2,1)S(1)} %far_weight.1.refs_13_.first_ref.refs_5_), channel_id=1, source_target_pairs={{0,2},{1,3},{2,0},{3,1},{4,6},{5,7},{6,4},{7,5},{8,10},{9,11},{10,... | collective-permute-start | bytes 2654216 | tf_op jit(solution)/shard_map/ppermute | solution.py:621
  35.5 12.0 %collective-permute-start.8 = (bf16[128,768]{1,0:T(8,128)(2,1)S(1)}, bf16[128,768]{1,0:T(8,128)(2,1)S(1)}, u32[]{:S(2)}, u32[]{:S(2)}) collective-permute-start(bf16[128,768]{1,0:T(8,128)(2,1)S(1)} %get-tuple-element.27), channel_id=1, source_target_pairs={{4,12},{8,0},{5,13},{9,1},{6,14},{10,2},{7,15},{11,3},{20,28},{24,... | collective-permute-start | bytes 589832 | tf_op jit(solution)/shard_map/ppermute | solution.py:630
  36.8 17.0 %collective-permute-start.11 = (bf16[128,768]{1,0:T(8,128)(2,1)S(1)}, bf16[128,768]{1,0:T(8,128)(2,1)S(1)}, u32[]{:S(2)}, u32[]{:S(2)}) collective-permute-start(bf16[128,768]{1,0:T(8,128)(2,1)S(1)} %get-tuple-element.33), channel_id=1, source_target_pairs={{4,0},{8,12},{5,1},{9,13},{6,2},{10,14},{7,3},{11,15},{20,16},{24,... | collective-permute-start | bytes 589832 | tf_op jit(solution)/shard_map/ppermute | solution.py:629
  40.1 9.9 %collective-permute-start.10 = (bf16[128,384]{1,0:T(8,128)(2,1)S(1)}, bf16[128,384]{1,0:T(8,128)(2,1)S(1)}, u32[]{:S(2)}, u32[]{:S(2)}) collective-permute-start(bf16[128,384]{1,0:T(8,128)(2,1)S(1)} %get-tuple-element.32), channel_id=1, source_target_pairs={{4,12},{8,0},{5,13},{9,1},{6,14},{10,2},{7,15},{11,3},{20,28},{24,... | collective-permute-start | bytes 294920 | tf_op jit(solution)/shard_map/ppermute | solution.py:632
  41.4 14.4 %collective-permute-start.12 = (bf16[128,1152]{1,0:T(8,128)(2,1)S(1)}, bf16[128,1152]{1,0:T(8,128)(2,1)S(1)}, u32[]{:S(2)}, u32[]{:S(2)}) collective-permute-start(bf16[128,1152]{1,0:T(8,128)(2,1)S(1)} %get-tuple-element.35), channel_id=1, source_target_pairs={{4,8},{8,4},{5,9},{9,5},{6,10},{10,6},{7,11},{11,7},{20,24},{24,20... | collective-permute-start | bytes 884744 | tf_op jit(solution)/shard_map/ppermute | solution.py:633
  47.5 8.3 %collective-permute-start.13 = (bf16[128,384]{1,0:T(8,128)(2,1)S(1)}, bf16[128,384]{1,0:T(8,128)(2,1)S(1)}, u32[]{:S(2)}, u32[]{:S(2)}) collective-permute-start(bf16[128,384]{1,0:T(8,128)(2,1)S(1)} %get-tuple-element.36), channel_id=1, source_target_pairs={{4,0},{8,12},{5,1},{9,13},{6,2},{10,14},{7,3},{11,15},{20,16},{24,... | collective-permute-start | bytes 294920 | tf_op jit(solution)/shard_map/ppermute | solution.py:634
  49.3 1.0 %copy-start.1 = (bf16[1,128,1536]{2,1,0:T(8,128)(2,1)S(1)}, bf16[1,128,1536]{2,1,0:T(8,128)(2,1)}, u32[]{:S(2)}) copy-start(bf16[1,128,1536]{2,1,0:T(8,128)(2,1)} %refs_10_.1) | copy-start | bytes 1179652
  49.4 5.3 %collective-permute-start.9 = (bf16[768,1152]{1,0:T(8,128)(2,1)S(1)}, bf16[768,1152]{1,0:T(8,128)(2,1)S(1)}, u32[]{:S(2)}, u32[]{:S(2)}) collective-permute-start(bf16[768,1152]{1,0:T(8,128)(2,1)S(1)} %chip_weight.1), channel_id=1, source_target_pairs={{0,1},{1,0},{2,3},{3,2},{4,5},{5,4},{6,7},{7,6},{8,9},{9,8},{10,11... | collective-permute-start | bytes 5308424 | tf_op jit(solution)/shard_map/ppermute | solution.py:635
  54.7 1.2 %copy-start.3 = (f32[1536]{0:T(1024)S(1)}, f32[1536]{0:T(1024)}, u32[]{:S(2)}) copy-start(f32[1536]{0:T(1024)} %refs_13_.1) | copy-start | bytes 18436
